TPU v7x, 128 devices: a whole 4x4x4 slice. The times are simulated.
128 devices in a mesh: chan: 16 (over z, x_hi, core), rows: 8 (over x_lo, y).
Axes of the slice: x: 4 (x_hi: 2, x_lo: 2; x = x_hi * 2 + x_lo), y: 4, z: 4, core: 2. Of those that a mesh axis runs over, the one named last changes fastest.
Arguments:
- latents: bfloat16 [480, 6, 32, 512], P(None, None, 'rows', 'chan'), may hold values from -60 to 60
- conv_in_weight: bfloat16 [3, 3, 3, 512, 512], P(None, None, None, None, 'chan'), may hold values from -0.0546875 to 0.0546875
- conv_in_bias: float32 [512], replicated, may hold values from -4 to 4
- norm_gain: float32 [512], replicated, may hold values from 0.5 to 1.5
- norm_shift: float32 [512], replicated, may hold values from -3 to 3
- hidden_rim: bfloat16 [960, 2, 64, 512], P('chan', None, 'rows'), may hold values from -0.29882812 to 2
- conv_out_weight: bfloat16 [3, 3, 3, 512, 256], replicated, may hold values from -0.0546875 to 0.0546875
- conv_out_bias: float32 [256], replicated, may hold values from -3 to 3
Outputs:
- decoded: bfloat16 [960, 4, 64, 256], P('chan', None, 'rows')
All inputs are finite; a program needn't handle non-finite values.
Results may differ from a plain program's by a relative error of at most 0.0042.
Values may be sent and summed in bfloat16 or wider, within the bound.
No kernel may reach another device: no remote copies, remote signals or barrier semaphores. Data moves between devices by JAX's collectives and lax.ppermute only.
A program may use at most 768 MiB of HBM per device.

v0:
```python
import jax
import jax.numpy as jnp
from jax import lax
from jax.experimental import pallas as pl
from jax.experimental.pallas import tpu as pltpu
from jax.sharding import PartitionSpec as P

GROUPS = 32
BOTH = ("chan", "rows")
BF16 = jnp.bfloat16
F32 = jnp.float32
VMEM = 58 * 1024 * 1024


def device_perm(move):
    pairs = []
    for d in range(128):
        chan, row = divmod(d, 8)
        to = move(chan // 4, chan // 2 % 2, chan % 2, row)
        if to is not None:
            z, half, core, row = to
            pairs.append((d, ((z % 4) * 4 + half * 2 + core) * 8 + row))
    return pairs


def send(array, move):
    return lax.ppermute(array, BOTH, device_perm(move))


def to_row(step):
    return lambda z, half, core, row: (z, half, core, row + step) if 0 <= row + step < 8 else None


def to_chan(step):
    def move(z, half, core, row):
        chan = z * 4 + half * 2 + core + step
        return (chan // 4, chan // 2 % 2, chan % 2, row) if 0 <= chan < 16 else None

    return move


def conv_in_kernel(place, main, other, up, up_other, down, down_other, w0, w1, w2, w3, bias,
                   strips, stats, x, w, turned, moments, sems):
    z, half, core = place[0], place[1], place[2]
    copies = []
    count = 0
    for array, slab, owner in (
        (main, slice(1, 5), core), (other, slice(1, 5), 1 - core),
        (up, 0, core), (up_other, 0, 1 - core), (down, 5, core), (down_other, 5, 1 - core),
    ):
        for k in range(8):
            dz, dh = k // 2, k % 2
            start = (((z + 4 - dz) % 4) * 4 + (half + dh) % 2 * 2 + owner) * 32
            copies.append(pltpu.make_async_copy(
                array.at[k], x.at[:, slab, pl.ds(pl.multiple_of(start, 32), 32), :], sems.at[count]))
            count += 1
    for dz, array in enumerate((w0, w1, w2, w3)):
        copies.append(pltpu.make_async_copy(array, w.at[:, :, (z + 4 - dz) % 4], sems.at[count]))
        count += 1
    for copy in copies:
        copy.start()
    moments[...] = jnp.zeros_like(moments)
    lane = lax.broadcasted_iota(jnp.int32, (128, 128), 1)
    inside = (lane >= 4) & (lane < 124)
    for copy in copies:
        copy.wait()

    def frame(t, _):
        for g in range(2):
            summed = None
            for a in range(3):
                for b in range(3):
                    rhs = jnp.concatenate([x[t + a, b + g * 2 + h] for h in range(2)], axis=1)
                    lhs = w[a * 3 + b].reshape(384, 512)
                    term = jnp.dot(lhs, rhs, preferred_element_type=F32)
                    summed = term if summed is None else summed + term
            for h in range(2):
                part = summed[:, h * 128 : (h + 1) * 128]
                value = pltpu.roll(part[0:128], 1, 1) + part[128:256] + pltpu.roll(part[256:384], 127, 1)
                value = (value + bias[...]).astype(BF16).astype(F32)
                kept = jnp.where(inside, value, 0.0)
                moments[0] += kept
                moments[1] += kept * kept
                turned[...] = value.T
                for s in range(4):
                    strips[s, t, g * 2 + h] = turned[3 + 30 * s : 35 + 30 * s, :].astype(BF16)
        return 0

    lax.fori_loop(0, 4, frame, 0)
    for i in range(2):
        grouped = jnp.sum(moments[i].reshape(8, 16, 128), axis=1)
        stats[i] = jnp.broadcast_to(jnp.sum(grouped, axis=1, keepdims=True), (8, 128))


def conv_in(place, main, other, up, up_other, down, down_other, weights, bias):
    return pl.pallas_call(
        conv_in_kernel,
        out_shape=(jax.ShapeDtypeStruct((4, 4, 4, 32, 128), BF16), jax.ShapeDtypeStruct((2, 8, 128), F32)),
        in_specs=[pl.BlockSpec(memory_space=pltpu.SMEM)] + [pl.BlockSpec(memory_space=pl.ANY)] * 10
        + [pl.BlockSpec(memory_space=pltpu.VMEM)],
        out_specs=(pl.BlockSpec(memory_space=pltpu.VMEM), pl.BlockSpec(memory_space=pltpu.VMEM)),
        scratch_shapes=[
            pltpu.VMEM((6, 6, 512, 128), BF16),
            pltpu.VMEM((9, 3, 4, 32, 512), BF16),
            pltpu.VMEM((128, 128), F32),
            pltpu.VMEM((2, 128, 128), F32),
            pltpu.SemaphoreType.DMA((52,)),
        ],
        compiler_params=pltpu.CompilerParams(vmem_limit_bytes=VMEM),
        cost_estimate=pl.CostEstimate(flops=7_200_000_000, bytes_accessed=9_000_000, transcendentals=0),
        name="conv_in",
    )(place, main, other, up, up_other, down, down_other, *weights, bias)


def collapse_kernel(taps, out):
    def pairs(t0, t1, t2):
        return ((t0, t1 + t2), (t0 + t1, t2))

    for z in range(4):
        wide = [[taps[0, b, c, z, 0].astype(F32) for c in range(3)] for b in range(3)]
        by_col = [pairs(*row) for row in wide]
        for pw in range(2):
            for i in range(2):
                by_row = pairs(by_col[0][pw][i], by_col[1][pw][i], by_col[2][pw][i])
                for ph in range(2):
                    for j in range(2):
                        out[0, ph, j, pw, i, 0, z] = by_row[ph][j].astype(BF16)


def collapse(weight):
    out = pl.pallas_call(
        collapse_kernel,
        grid=(3, 4),
        out_shape=jax.ShapeDtypeStruct((3, 2, 2, 2, 2, 4, 4, 32, 256), BF16),
        in_specs=[pl.BlockSpec((1, 3, 3, 4, 1, 32, 256), lambda a, p: (a, 0, 0, 0, p, 0, 0))],
        out_specs=pl.BlockSpec((1, 2, 2, 2, 2, 1, 4, 32, 256), lambda a, p: (a, 0, 0, 0, 0, p, 0, 0, 0)),
        compiler_params=pltpu.CompilerParams(vmem_limit_bytes=24 * 1024 * 1024),
        cost_estimate=pl.CostEstimate(flops=30_000_000, bytes_accessed=20_000_000, transcendentals=0),
        name="collapse",
    )(weight.reshape(3, 3, 3, 4, 4, 32, 256))
    return out.reshape(12, 2, 1024, 256)


def rim_kernel(rim, w, out):
    for pw in range(2):
        for t in range(2):
            summed = None
            for a in range(2 - t):
                for b in range(3):
                    lhs = rim[t + a, b : b + 8, :, pw * 512 : pw * 512 + 1536].reshape(256, 1536)
                    term = jnp.dot(lhs, w[a, b], preferred_element_type=F32)
                    summed = term if summed is None else summed + term
            summed = summed.reshape(8, 32, 256)
            for r in range(8):
                out[pw, r % 2, t, r // 2] = summed[r]


def conv_rim(windows, weight):
    return pl.pallas_call(
        rim_kernel,
        grid=(1,),
        out_shape=jax.ShapeDtypeStruct((2, 2, 2, 4, 32, 256), F32),
        in_specs=[
            pl.BlockSpec((2, 10, 32, 2048), lambda i: (0, 0, 0, 0)),
            pl.BlockSpec((2, 3, 1536, 256), lambda i: (0, 0, 0, 0)),
        ],
        out_specs=pl.BlockSpec((2, 2, 2, 4, 32, 256), lambda i: (0,) * 6),
        compiler_params=pltpu.CompilerParams(vmem_limit_bytes=40 * 1024 * 1024),
        cost_estimate=pl.CostEstimate(flops=3_600_000_000, bytes_accessed=9_500_000, transcendentals=0),
        name="conv_rim",
    )(windows, weight.reshape(3, 3, 1536, 256))


def conv_out_kernel(place, main, up, down, vectors, rim, bias, w, out, n, acc):
    step = pl.program_id(0)

    @pl.when(step == 0)
    def _():
        own, left, right, top, bottom = (place[i] for i in range(5))
        row = lax.broadcasted_iota(jnp.int32, (32, 128), 0)
        keep_col = jnp.where(
            ((row == 0) & (left == 1)) | ((row == 31) & (right == 1)), 0.0, 1.0)
        keep = [keep_col] * 6
        keep[0] = keep_col * jnp.where(top == 1, 0.0, 1.0)
        keep[5] = keep_col * jnp.where(bottom == 1, 0.0, 1.0)

        def frame(t, _):
            for r in range(4):
                p = own ^ r
                vec = vectors[p]
                for h in range(6):
                    raw = up[r, t] if h == 0 else down[r, t] if h == 5 else main[r, t, h - 1]
                    v = (raw.astype(F32) - vec[0:1]) * vec[1:2] + vec[2:3]
                    v = v / (1.0 + jnp.exp(-v)) * keep[h]
                    for s in range(3):
                        moved = v if s == 0 else pltpu.roll(v, 32 - s, 0)
                        start = pl.multiple_of(s * 512 + p * 128, 128)
                        n[t, h, :, pl.ds(start, 128)] = moved.astype(BF16)
            return 0

        lax.fori_loop(0, 4, frame, 0)
        whole = jnp.broadcast_to(bias[...], (32, 256))
        for pw in range(2):
            for ph in range(2):
                for t in range(4):
                    for h in range(4):
                        acc[pw, ph, t, h] = rim[pw, ph, t, h] + whole if t < 2 else whole

    a, ph, j = step // 4, step // 2 % 2, step % 2
    for tap in range(3):
        @pl.when(a == tap)
        def _():
            frames = 2 + tap
            for pw in range(2):
                lhs = n[0:frames, pl.ds(ph + j, 4), :, pw * 512 : pw * 512 + 1024].reshape(frames * 128, 1024)
                term = jnp.dot(lhs, w[0, pw], preferred_element_type=F32).reshape(frames, 4, 32, 256)
                acc[pw, ph, 4 - frames : 4] += term

    @pl.when(step == 11)
    def _():
        out[...] = acc[...].astype(BF16)


def conv_out(place, main, up, down, vectors, rim, bias, weight):
    whole = pl.BlockSpec(memory_space=pltpu.VMEM)
    return pl.pallas_call(
        conv_out_kernel,
        grid=(12,),
        out_shape=jax.ShapeDtypeStruct((2, 2, 4, 4, 32, 256), BF16),
        in_specs=[pl.BlockSpec(memory_space=pltpu.SMEM)] + [whole] * 6
        + [pl.BlockSpec((1, 2, 1024, 256), lambda i: (i, 0, 0, 0))],
        out_specs=pl.BlockSpec((2, 2, 4, 4, 32, 256), lambda i: (0,) * 6),
        scratch_shapes=[pltpu.VMEM((4, 6, 32, 1536), BF16), pltpu.VMEM((2, 2, 4, 4, 32, 256), F32)],
        compiler_params=pltpu.CompilerParams(vmem_limit_bytes=VMEM),
        cost_estimate=pl.CostEstimate(flops=4_900_000_000, bytes_accessed=18_000_000, transcendentals=400_000),
        name="conv_out",
    )(place, main, up, down, vectors, rim, bias, weight)


def rim_windows(rim):
    before, after = send(rim[59:60], to_chan(1)), send(rim[0:1], to_chan(-1))
    wide = jnp.concatenate([before, rim, after], axis=0)
    above, below = send(wide[:, :, 7:8], to_row(1)), send(wide[:, :, 0:1], to_row(-1))
    tall = jnp.concatenate([above, wide, below], axis=2)
    pairs = tall.transpose(1, 2, 0, 3).reshape(2, 10, 31, 1024)
    windows = jnp.concatenate([pairs[:, :, 0:30], pairs[:, :, 1:31]], axis=3)
    return jnp.pad(windows, ((0, 0), (0, 0), (0, 2), (0, 0)))


def body(
    latents,
    conv_in_weight,
    conv_in_bias,
    norm_gain,
    norm_shift,
    hidden_rim,
    conv_out_weight,
    conv_out_bias,
):
    chan, row = lax.axis_index("chan"), lax.axis_index("rows")
    z, half, core = chan // 4, chan // 2 % 2, chan % 2
    own = chan % 4
    flip_core = lambda z, half, core, row: (z, half, 1 - core, row)

    weights = conv_in_weight.swapaxes(3, 4)
    weight_of = [weights]
    for dz in range(1, 4):
        weight_of.append(send(weights, lambda z, half, core, row: (z + dz, half, core, row)))
    weight_of = [array.reshape(9, 3, 32, 512) for array in weight_of]

    padded = jnp.pad(latents.transpose(1, 2, 3, 0), ((0, 0), (0, 0), (0, 0), (4, 4)))
    pieces = jnp.stack([padded[..., 120 * i : 120 * i + 128] for i in range(4)])
    got = []
    for k in range(8):
        dz, dh = k // 2, k % 2
        piece = lax.dynamic_index_in_dim(pieces, (z + dz) % 4, 0, keepdims=False)
        if k:
            piece = send(piece, lambda z, half, core, row: (z + dz, half ^ dh, core, row))
        got.append(piece)
    main = jnp.stack(got)
    up, down = send(main[:, :, 3], to_row(1)), send(main[:, :, 0], to_row(-1))
    other, up_other, down_other = (send(array, flip_core) for array in (main, up, down))

    by_owner = conv_in_bias.reshape(4, 4, 32)
    bias = lax.dynamic_index_in_dim(by_owner, own, 1, keepdims=False).reshape(128, 1)
    place = jnp.stack([z, half, core]).astype(jnp.int32)
    strips, stats = conv_in(place, main, other, up, up_other, down, down_other, weight_of,
                            jnp.broadcast_to(bias, (128, 128)))

    parts = []
    for r in range(4):
        part = lax.dynamic_index_in_dim(strips, own ^ r, 0, keepdims=False)
        if r:
            part = send(part, lambda z, half, core, row: (z, half ^ (r // 2), core ^ (r % 2), row))
        parts.append(part)
    first = jnp.stack(parts)
    above, below = send(first[:, :, 3], to_row(1)), send(first[:, :, 0], to_row(-1))

    sent = jnp.broadcast_to(jnp.pad(stats[:, :, 0].reshape(1, 16), ((0, 0), (0, 112))), (128, 128))
    gathered = lax.all_to_all(sent, BOTH, split_axis=0, concat_axis=0, tiled=True)
    sums, squares = gathered.reshape(4, 4, 8, 128)[..., :16].sum(axis=(0, 2)).reshape(4, 2, 8).swapaxes(0, 1)
    counted = float(480 * 4 * 32 * 16)
    mean = sums / counted
    var = squares / counted - mean * mean
    inv = 1.0 / jnp.sqrt(var + 1e-06)
    by_place = lambda vector: vector.reshape(4, 4, 32).swapaxes(0, 1).reshape(4, 128)
    vectors = jnp.stack(
        [jnp.repeat(mean, 16, axis=1), jnp.repeat(inv, 16, axis=1) * by_place(norm_gain), by_place(norm_shift)]
        + [jnp.zeros((4, 128), F32)] * 5, axis=1)

    rim = conv_rim(rim_windows(hidden_rim), conv_out_weight)
    edges = jnp.stack([own, chan == 0, chan == 15, row == 0, row == 7]).astype(jnp.int32)
    decoded = conv_out(edges, first, above, below, vectors, rim, conv_out_bias.reshape(1, 256),
                       collapse(conv_out_weight))
    return decoded.transpose(4, 0, 2, 3, 1, 5)[:30].reshape(60, 4, 8, 256)


def solution(mesh):
    return jax.shard_map(
        body,
        mesh=mesh,
        in_specs=(
            P(None, None, "rows", "chan"),
            P(None, None, None, None, "chan"),
            P(),
            P(),
            P(),
            P("chan", None, "rows", None),
            P(),
            P(),
        ),
        out_specs=P("chan", None, "rows", None),
        check_vma=False,
    )
```

profile of v0, /device:TPU:2, one launch (start us, length us, event | category | flops | bytes accessed | tf_op | source)
XLA Modules:
  0.0 177.5 jit_solution(9546885833137928071)
XLA Ops:
  0.0 1.2 copy.112
  1.6 0.9 dynamic-slice_bitcast_fusion
  2.6 2.1 %collective-permute-start = (bf16[6,4,32,128]{3,2,0,1:T(8,128)(2,1)S(1)}, bf16[6,4,32,128]{3,2,0,1:T(8,128)(2,1)S(1)}, u32[]{:S(2)}, u32[]{:S(2)}) collective-permute-start(bf16[6,4,32,128]{3,2,0,1:T(8,128)(2,1)S(1)} %get-tuple-element.21), channel_id=1, source_target_pairs={{0,16},{1,17},{2,18},{3,19},{4,20},{5,21},{6,22},{7,23},{8,24},{9,... | collective-permute-start | bytes 589832 | tf_op jit(solution)/shard_map/ppermute | solution.py:27
  4.7 4.9 %collective-permute-start.6 = (bf16[6,4,32,128]{3,2,0,1:T(8,128)(2,1)S(1)}, bf16[6,4,32,128]{3,2,0,1:T(8,128)(2,1)S(1)}, u32[]{:S(2)}, u32[]{:S(2)}) collective-permute-start(bf16[6,4,32,128]{3,2,0,1:T(8,128)(2,1)S(1)} %get-tuple-element.17), channel_id=1, source_target_pairs={{0,112},{1,113},{2,114},{3,115},{4,116},{5,117},{6,118},{7,119},{8... | collective-permute-start | bytes 589832 | tf_op jit(solution)/shard_map/ppermute | solution.py:27
  9.5 0.4 collective-permute-start.5
  10.0 1.2 collective-permute-start.4
  11.2 3.9 %collective-permute-start.3 = (bf16[6,4,32,128]{3,2,0,1:T(8,128)(2,1)S(1)}, bf16[6,4,32,128]{3,2,0,1:T(8,128)(2,1)S(1)}, u32[]{:S(2)}, u32[]{:S(2)}) collective-permute-start(bf16[6,4,32,128]{3,2,0,1:T(8,128)(2,1)S(1)} %get-tuple-element.19), channel_id=1, source_target_pairs={{0,64},{1,65},{2,66},{3,67},{4,68},{5,69},{6,70},{7,71},{8,72},{9,... | collective-permute-start | bytes 589832 | tf_op jit(solution)/shard_map/ppermute | solution.py:27
  15.1 1.6 collective-permute-start.1
  16.7 0.7 bitcast_dynamic-update-slice_fusion.6
  17.4 10.1 %collective-permute-done.1 = bf16[6,4,32,128]{3,2,0,1:T(8,128)(2,1)S(1)} collective-permute-done((bf16[6,4,32,128]{3,2,0,1:T(8,128)(2,1)S(1)}, bf16[6,4,32,128]{3,2,0,1:T(8,128)(2,1)S(1)}, u32[]{:S(2)}, u32[]{:S(2)}) %collective-permute-start.1) | collective-permute-done | bytes 196640 | tf_op jit(solution)/shard_map/ppermute | solution.py:27
  27.5 2.3 %collective-permute-start.2 = (bf16[6,4,32,128]{3,2,0,1:T(8,128)(2,1)S(1)}, bf16[6,4,32,128]{3,2,0,1:T(8,128)(2,1)S(1)}, u32[]{:S(2)}, u32[]{:S(2)}) collective-permute-start(bf16[6,4,32,128]{3,2,0,1:T(8,128)(2,1)S(1)} %get-tuple-element.20), channel_id=1, source_target_pairs={{0,48},{1,49},{2,50},{3,51},{4,52},{5,53},{6,54},{7,55},{8,56},{9,... | collective-permute-start | bytes 589832 | tf_op jit(solution)/shard_map/ppermute | solution.py:27
  29.7 0.7 bitcast_dynamic-update-slice_fusion.2
  30.5 6.9 %collective-permute-done.2 = bf16[6,4,32,128]{3,2,0,1:T(8,128)(2,1)S(1)} collective-permute-done((bf16[6,4,32,128]{3,2,0,1:T(8,128)(2,1)S(1)}, bf16[6,4,32,128]{3,2,0,1:T(8,128)(2,1)S(1)}, u32[]{:S(2)}, u32[]{:S(2)}) %collective-permute-start.2) | collective-permute-done | bytes 196640 | tf_op jit(solution)/shard_map/ppermute | solution.py:27
  37.3 0.7 bitcast_dynamic-update-slice_fusion.5
  38.1 0.7 bitcast_dynamic-update-slice_fusion.1
  38.8 0.7 bitcast_dynamic-update-slice_fusion.4
  39.5 0.7 bitcast_dynamic-update-slice_fusion
  40.2 0.7 bitcast_dynamic-update-slice_fusion.3
  41.0 0.5 copy.100
  41.6 2.4 %collective-permute-start.20 = (bf16[1,2,8,512]{3,0,2,1:T(2,128)(2,1)S(1)}, bf16[1,2,8,512]{3,0,2,1:T(2,128)(2,1)S(1)}, u32[]{:S(2)}, u32[]{:S(2)}) collective-permute-start(bf16[1,2,8,512]{3,0,2,1:T(2,128)(2,1)S(1)} %get-tuple-element.15), channel_id=1, source_target_pairs={{0,8},{1,9},{2,10},{3,11},{4,12},{5,13},{6,14},{7,15},{8,16},{9,17... | collective-permute-start | bytes 49160 | tf_op jit(solution)/shard_map/ppermute | solution.py:27
  44.0 1.3 collective-permute-start.21
  45.3 1.9 %slice_bitcast_fusion = (bf16[8,6,32,128]{3,2,1,0:T(8,128)(2,1)}, bf16[8,6,32,128]{3,2,1,0:T(8,128)(2,1)S(1)}) fusion(bf16[8,6,4,32,128]{4,3,1,0,2:T(8,128)(2,1)} %bitcast_dynamic-update-slice_fusion.3), kind=kLoop, calls=%fused_computation.10 | loop fusion | bytes 1572864 | tf_op jit(solution)/shard_map/squeeze | solution.py:281
  47.2 6.0 %collective-permute-start.10 = (bf16[8,6,32,128]{3,2,1,0:T(8,128)(2,1)}, bf16[8,6,32,128]{3,2,1,0:T(8,128)(2,1)}, u32[]{:S(2)}, u32[]{:S(2)}) collective-permute-start(bf16[8,6,32,128]{3,2,1,0:T(8,128)(2,1)} %get-tuple-element.9), channel_id=1, source_target_pairs={{1,0},{2,1},{3,2},{4,3},{5,4},{6,5},{7,6},{9,8},{10,9},{11,10},{12... | collective-permute-start | bytes 1179656 | tf_op jit(solution)/shard_map/ppermute | solution.py:27
  53.4 1.9 %collective-permute-start.22 = (bf16[62,2,1,512]{3,0,2,1:T(8,128)(2,1)S(1)}, bf16[62,2,1,512]{3,0,2,1:T(8,128)(2,1)S(1)}, u32[]{:S(2)}, u32[]{:S(2)}) collective-permute-start(bf16[62,2,1,512]{3,0,2,1:T(8,128)(2,1)S(1)} %get-tuple-element.13), channel_id=1, source_target_pairs={{0,1},{1,2},{2,3},{3,4},{4,5},{5,6},{6,7},{8,9},{9,10},{10,11},{11... | collective-permute-start | bytes 380936 | tf_op jit(solution)/shard_map/ppermute | solution.py:27
  55.3 6.0 %collective-permute-start.23 = (bf16[62,2,1,512]{3,0,2,1:T(8,128)(2,1)S(1)}, bf16[62,2,1,512]{3,0,2,1:T(8,128)(2,1)S(1)}, u32[]{:S(2)}, u32[]{:S(2)}) collective-permute-start(bf16[62,2,1,512]{3,0,2,1:T(8,128)(2,1)S(1)} %get-tuple-element.14), channel_id=1, source_target_pairs={{1,0},{2,1},{3,2},{4,3},{5,4},{6,5},{7,6},{9,8},{10,9},{11,10},{12... | collective-permute-start | bytes 380936 | tf_op jit(solution)/shard_map/ppermute | solution.py:27
  61.3 6.4 %collective-permute-start.13 = (bf16[3,3,3,32,512]{4,3,2,1,0:T(8,128)(2,1)}, bf16[3,3,3,32,512]{4,3,2,1,0:T(8,128)(2,1)}, u32[]{:S(2)}, u32[]{:S(2)}) collective-permute-start(bf16[3,3,3,32,512]{4,3,2,1,0:T(8,128)(2,1)} %bitcast.32), channel_id=1, source_target_pairs={{0,64},{1,65},{2,66},{3,67},{4,68},{5,69},{6,70},{7,71},{8,72},{9,... | collective-permute-start | bytes 2654216 | tf_op jit(solution)/shard_map/ppermute | solution.py:27
  68.3 0.7 stack.111.place
  68.9 3.0 %copy-done.1 = bf16[3,3,3,512,256]{4,3,2,1,0:T(8,128)(2,1)S(1)} copy-done((bf16[3,3,3,512,256]{4,3,2,1,0:T(8,128)(2,1)S(1)}, bf16[3,3,3,512,256]{4,3,2,1,0:T(8,128)(2,1)}, u32[]{:S(2)}) %copy-start.1) | copy-done | bytes 7077912
  72.0 3.4 %collapse.1 = bf16[3,2,2,2,2,4,4,32,256]{8,7,6,5,4,3,2,1,0:T(8,128)(2,1)S(1)} custom-call(bf16[3,3,3,4,4,32,256]{6,5,4,3,2,1,0:T(8,128)(2,1)S(1)} %bitcast.97), custom_call_target="tpu_custom_call" | custom-call | flops 30000000 | bytes 20000000 | tf_op jit(solution)/shard_map/collapse/pallas_call | solution.py:131
  75.4 4.5 %copy-done = bf16[3,2,2,2,2,4,4,32,256]{8,7,6,5,4,3,2,1,0:T(8,128)(2,1)} copy-done((bf16[3,2,2,2,2,4,4,32,256]{8,7,6,5,4,3,2,1,0:T(8,128)(2,1)}, bf16[3,2,2,2,2,4,4,32,256]{8,7,6,5,4,3,2,1,0:T(8,128)(2,1)S(1)}, u32[]{:S(2)}) %copy-start) | copy-done | bytes 12582936
  79.9 0.6 pad_add_fusion.place
  80.6 1.9 %collective-permute-start.8 = (bf16[8,6,32,128]{3,2,1,0:T(8,128)(2,1)S(1)}, bf16[8,6,32,128]{3,2,1,0:T(8,128)(2,1)}, u32[]{:S(2)}, u32[]{:S(2)}) collective-permute-start(bf16[8,6,32,128]{3,2,1,0:T(8,128)(2,1)S(1)} %get-tuple-element.10), channel_id=1, source_target_pairs={{0,1},{1,2},{2,3},{3,4},{4,5},{5,6},{6,7},{8,9},{9,10},{10,11},{11... | collective-permute-start | bytes 1179656 | tf_op jit(solution)/shard_map/ppermute | solution.py:27
  82.5 1.7 maximum_bitcast_fusion
  84.2 3.3 %reshape.93 = bf16[2,10,31,1024]{3,2,1,0:T(8,128)(2,1)} reshape(bf16[2,10,62,512]{3,2,1,0:T(8,128)(2,1)} %maximum_bitcast_fusion) | data formatting | bytes 2539520 | tf_op jit(solution)/shard_map/reshape | solution.py:245
  87.5 3.2 %collective-permute-start.14 = (bf16[3,3,3,32,512]{4,3,2,1,0:T(8,128)(2,1)}, bf16[3,3,3,32,512]{4,3,2,1,0:T(8,128)(2,1)S(1)}, u32[]{:S(2)}, u32[]{:S(2)}) collective-permute-start(bf16[3,3,3,32,512]{4,3,2,1,0:T(8,128)(2,1)} %bitcast.32), channel_id=1, source_target_pairs={{0,96},{1,97},{2,98},{3,99},{4,100},{5,101},{6,102},{7,103},{8,104... | collective-permute-start | bytes 2654216 | tf_op jit(solution)/shard_map/ppermute | solution.py:27
  90.7 2.3 %fusion.6 = (bf16[2,10,30,1024]{3,2,1,0:T(8,128)(2,1)S(1)}, bf16[2,10,30,1024]{3,2,1,0:T(8,128)(2,1)S(1)}) fusion(bf16[2,10,31,1024]{3,2,1,0:T(8,128)(2,1)} %reshape.93), kind=kLoop, calls=%fused_computation.49 | loop fusion | bytes 4915200 | tf_op jit(solution)/shard_map/slice | solution.py:246
  93.2 0.5 collective-permute-start.9
  93.7 0.4 fusion.2.rim
  94.1 3.8 %conv_rim.1.rim = f32[2,2,2,4,32,256]{5,4,3,2,1,0:T(8,128)S(1)} custom-call(bf16[2,10,32,2048]{3,2,1,0:T(8,128)(2,1)S(1)} %fusion.2.rim, bf16[3,3,1536,256]{3,2,1,0:T(8,128)(2,1)S(1)} %bitcast.100), custom_call_target="tpu_custom_call" | custom-call | flops 3600000000 | bytes 9500000 | tf_op jit(solution)/shard_map/conv_rim/pallas_call | solution.py:159
  98.0 3.4 %copy.92.main = bf16[8,6,4,32,128]{4,3,2,1,0:T(8,128)(2,1)} copy(bf16[8,6,4,32,128]{4,3,1,0,2:T(8,128)(2,1)} %bitcast_dynamic-update-slice_fusion.3) | data formatting | bytes 3145728 | tf_op jit(solution)/shard_map/stack | solution.py:280
  101.4 3.0 %copy.93.other = bf16[8,6,4,32,128]{4,3,2,1,0:T(8,128)(2,1)} copy(bf16[8,6,4,32,128]{4,3,1,0,2:T(8,128)(2,1)} %collective-permute-done.7) | data formatting | bytes 3145728 | tf_op jit(solution)/shard_map/ppermute | solution.py:27
  104.3 1.2 collective-permute-done.14
  105.6 0.8 broadcast_in_dim.19.bias
  106.7 14.8 %conv_in.1 = (bf16[4,4,4,32,128]{4,3,2,1,0:T(8,128)(2,1)}, f32[2,8,128]{2,1,0:T(8,128)}) custom-call(s32[3]{0:T(128)} %pad_add_fusion.place, bf16[8,6,4,32,128]{4,3,2,1,0:T(8,128)(2,1)} %copy.92.main, bf16[8,6,4,32,128]{4,3,2,1,0:T(8,128)(2,1)} %copy.93.other, bf16[8,6,32,128]{3,2,1,0:T(8,128)(2,1)} %collective-permute-done.8.up, ...), custom_call_target="tpu_custom_call" | custom-call | flops 7200000000 | bytes 9000000 | tf_op jit(solution)/shard_map/conv_in/pallas_call | solution.py:96
  121.5 0.8 slice_reduce_fusion.1
  122.4 0.7 broadcast_in_dim.20
  123.1 9.5 %all-to-all-start = ((f32[128,1,128]{2,1,0:T(1,128)}), f32[128,1,128]{2,1,0:T(1,128)S(1)}, u32[]{:S(2)}, u32[]{:S(2)}) async-start(f32[128,1,128]{2,1,0:T(1,128)} %broadcast_in_dim.20), calls=%async_computation | async-start | bytes 131072 | tf_op jit(solution)/shard_map/all_to_all | solution.py:300
  132.6 0.9 constant_dynamic-slice_fusion.3
  133.5 1.1 constant_dynamic-slice_fusion.2
  134.6 2.1 %collective-permute-start.16 = (bf16[4,4,32,128]{3,2,0,1:T(8,128)(2,1)S(1)}, bf16[4,4,32,128]{3,2,0,1:T(8,128)(2,1)S(1)}, u32[]{:S(2)}, u32[]{:S(2)}) collective-permute-start(bf16[4,4,32,128]{3,2,0,1:T(8,128)(2,1)S(1)} %bitcast.107), channel_id=1, source_target_pairs={{0,16},{1,17},{2,18},{3,19},{4,20},{5,21},{6,22},{7,23},{8,24},{9,... | collective-permute-start | bytes 393224 | tf_op jit(solution)/shard_map/ppermute | solution.py:27
  136.8 0.9 collective-permute-start.17
  137.7 0.6 collective-permute-start.15
  138.4 3.1 %all-to-all-done = f32[128,1,128]{2,1,0:T(1,128)S(1)} async-done(((f32[128,1,128]{2,1,0:T(1,128)}), f32[128,1,128]{2,1,0:T(1,128)S(1)}, u32[]{:S(2)}, u32[]{:S(2)}) %all-to-all-start) | async-done | bytes 65568 | tf_op jit(solution)/shard_map/all_to_all | solution.py:300
  141.7 0.5 collective-permute-done.16
  142.2 2.0 %collective-permute-done.17 = bf16[4,4,32,128]{3,2,0,1:T(8,128)(2,1)S(1)} collective-permute-done((bf16[4,4,32,128]{3,2,0,1:T(8,128)(2,1)S(1)}, bf16[4,4,32,128]{3,2,0,1:T(8,128)(2,1)S(1)}, u32[]{:S(2)}, u32[]{:S(2)}) %collective-permute-start.17) | collective-permute-done | bytes 131104 | tf_op jit(solution)/shard_map/ppermute | solution.py:27
  144.3 5.5 %collective-permute-start.19 = (bf16[4,4,32,128]{3,2,1,0:T(8,128)(2,1)S(1)}, bf16[4,4,32,128]{3,2,1,0:T(8,128)(2,1)S(1)}, u32[]{:S(2)}, u32[]{:S(2)}) collective-permute-start(bf16[4,4,32,128]{3,2,1,0:T(8,128)(2,1)S(1)} %get-tuple-element.26), channel_id=1, source_target_pairs={{1,0},{2,1},{3,2},{4,3},{5,4},{6,5},{7,6},{9,8},{10,9},{11,10},{12... | collective-permute-start | bytes 393224 | tf_op jit(solution)/shard_map/ppermute | solution.py:27
  149.7 1.9 %collective-permute-start.18 = (bf16[4,4,32,128]{3,2,1,0:T(8,128)(2,1)S(1)}, bf16[4,4,32,128]{3,2,1,0:T(8,128)(2,1)S(1)}, u32[]{:S(2)}, u32[]{:S(2)}) collective-permute-start(bf16[4,4,32,128]{3,2,1,0:T(8,128)(2,1)S(1)} %get-tuple-element.27), channel_id=1, source_target_pairs={{0,1},{1,2},{2,3},{3,4},{4,5},{5,6},{6,7},{8,9},{9,10},{10,11},{11... | collective-permute-start | bytes 393224 | tf_op jit(solution)/shard_map/ppermute | solution.py:27
  151.8 0.6 stack.134.vectors
  152.5 0.9 copy.103.main
  153.3 5.6 %collective-permute-done.18.up = bf16[4,4,32,128]{3,2,1,0:T(8,128)(2,1)S(1)} collective-permute-done((bf16[4,4,32,128]{3,2,1,0:T(8,128)(2,1)S(1)}, bf16[4,4,32,128]{3,2,1,0:T(8,128)(2,1)S(1)}, u32[]{:S(2)}, u32[]{:S(2)}) %collective-permute-start.18) | collective-permute-done | bytes 131104 | tf_op jit(solution)/shard_map/ppermute | solution.py:27
  159.0 0.7 copy-done.11
  159.6 14.8 %conv_out.1 = bf16[2,2,4,4,32,256]{5,4,3,2,1,0:T(8,128)(2,1)} custom-call(s32[5]{0:T(128)} %stack.111.place, bf16[4,4,4,32,128]{4,3,2,1,0:T(8,128)(2,1)} %copy.103.main, bf16[4,4,32,128]{3,2,1,0:T(8,128)(2,1)} %copy-done.11, bf16[4,4,32,128]{3,2,1,0:T(8,128)(2,1)} %copy-done.10, f32[4,8,128]{2,1,0:T(8,128)} %stack.134.vectors, ...), custom_call_target="tpu_custom_call" | custom-call | flops 4899999744 | bytes 18000000 | tf_op jit(solution)/shard_map/conv_out/pallas_call | solution.py:226
  174.4 2.0 %copy.104 = bf16[30,2,4,4,2,256]{5,2,4,3,1,0:T(4,128)(2,1)S(1)} copy(bf16[30,2,4,4,2,256]{5,0,3,2,4,1:T(8,128)(2,1)} %bitcast.103) | data formatting | bytes 1966080 | tf_op jit(solution)/shard_map/slice | solution.py:315
  176.4 1.1 copy.105
  (78 shorter events, 2.3 us)
Async XLA Ops:
  2.6 38.4 %copy-start.3 = (bf16[60,2,8,512]{3,2,1,0:T(8,128)(2,1)S(1)}, bf16[60,2,8,512]{3,2,1,0:T(8,128)(2,1)}, u32[]{:S(2)}) copy-start(bf16[60,2,8,512]{3,2,1,0:T(8,128)(2,1)} %param.13) | copy-start | bytes 2949124
  2.6 12.5 %collective-permute-start = (bf16[6,4,32,128]{3,2,0,1:T(8,128)(2,1)S(1)}, bf16[6,4,32,128]{3,2,0,1:T(8,128)(2,1)S(1)}, u32[]{:S(2)}, u32[]{:S(2)}) collective-permute-start(bf16[6,4,32,128]{3,2,0,1:T(8,128)(2,1)S(1)} %get-tuple-element.21), channel_id=1, source_target_pairs={{0,16},{1,17},{2,18},{3,19},{4,20},{5,21},{6,22},{7,23},{8,24},{9,... | collective-permute-start | bytes 589832 | tf_op jit(solution)/shard_map/ppermute | solution.py:27
  4.7 35.6 %collective-permute-start.6 = (bf16[6,4,32,128]{3,2,0,1:T(8,128)(2,1)S(1)}, bf16[6,4,32,128]{3,2,0,1:T(8,128)(2,1)S(1)}, u32[]{:S(2)}, u32[]{:S(2)}) collective-permute-start(bf16[6,4,32,128]{3,2,0,1:T(8,128)(2,1)S(1)} %get-tuple-element.17), channel_id=1, source_target_pairs={{0,112},{1,113},{2,114},{3,115},{4,116},{5,117},{6,118},{7,119},{8... | collective-permute-start | bytes 589832 | tf_op jit(solution)/shard_map/ppermute | solution.py:27
  9.5 30.0 %collective-permute-start.5 = (bf16[6,4,32,128]{3,2,0,1:T(8,128)(2,1)S(1)}, bf16[6,4,32,128]{3,2,0,1:T(8,128)(2,1)S(1)}, u32[]{:S(2)}, u32[]{:S(2)}) collective-permute-start(bf16[6,4,32,128]{3,2,0,1:T(8,128)(2,1)S(1)} %get-tuple-element.17), channel_id=1, source_target_pairs={{0,96},{1,97},{2,98},{3,99},{4,100},{5,101},{6,102},{7,103},{8,104... | collective-permute-start | bytes 589832 | tf_op jit(solution)/shard_map/ppermute | solution.py:27
  10.0 28.8 %collective-permute-start.4 = (bf16[6,4,32,128]{3,2,0,1:T(8,128)(2,1)S(1)}, bf16[6,4,32,128]{3,2,0,1:T(8,128)(2,1)S(1)}, u32[]{:S(2)}, u32[]{:S(2)}) collective-permute-start(bf16[6,4,32,128]{3,2,0,1:T(8,128)(2,1)S(1)} %get-tuple-element.19), channel_id=1, source_target_pairs={{0,80},{1,81},{2,82},{3,83},{4,84},{5,85},{6,86},{7,87},{8,88},{9,... | collective-permute-start | bytes 589832 | tf_op jit(solution)/shard_map/ppermute | solution.py:27
  11.2 26.9 %collective-permute-start.3 = (bf16[6,4,32,128]{3,2,0,1:T(8,128)(2,1)S(1)}, bf16[6,4,32,128]{3,2,0,1:T(8,128)(2,1)S(1)}, u32[]{:S(2)}, u32[]{:S(2)}) collective-permute-start(bf16[6,4,32,128]{3,2,0,1:T(8,128)(2,1)S(1)} %get-tuple-element.19), channel_id=1, source_target_pairs={{0,64},{1,65},{2,66},{3,67},{4,68},{5,69},{6,70},{7,71},{8,72},{9,... | collective-permute-start | bytes 589832 | tf_op jit(solution)/shard_map/ppermute | solution.py:27
  15.1 12.4 %collective-permute-start.1 = (bf16[6,4,32,128]{3,2,0,1:T(8,128)(2,1)S(1)}, bf16[6,4,32,128]{3,2,0,1:T(8,128)(2,1)S(1)}, u32[]{:S(2)}, u32[]{:S(2)}) collective-permute-start(bf16[6,4,32,128]{3,2,0,1:T(8,128)(2,1)S(1)} %get-tuple-element.20), channel_id=1, source_target_pairs={{0,32},{1,33},{2,34},{3,35},{4,36},{5,37},{6,38},{7,39},{8,40},{9,... | collective-permute-start | bytes 589832 | tf_op jit(solution)/shard_map/ppermute | solution.py:27
  27.5 9.9 %collective-permute-start.2 = (bf16[6,4,32,128]{3,2,0,1:T(8,128)(2,1)S(1)}, bf16[6,4,32,128]{3,2,0,1:T(8,128)(2,1)S(1)}, u32[]{:S(2)}, u32[]{:S(2)}) collective-permute-start(bf16[6,4,32,128]{3,2,0,1:T(8,128)(2,1)S(1)} %get-tuple-element.20), channel_id=1, source_target_pairs={{0,48},{1,49},{2,50},{3,51},{4,52},{5,53},{6,54},{7,55},{8,56},{9,... | collective-permute-start | bytes 589832 | tf_op jit(solution)/shard_map/ppermute | solution.py:27
  40.9 52.2 %collective-permute-start.7 = (bf16[8,6,4,32,128]{4,3,1,0,2:T(8,128)(2,1)}, bf16[8,6,4,32,128]{4,3,1,0,2:T(8,128)(2,1)}, u32[]{:S(2)}, u32[]{:S(2)}) collective-permute-start(bf16[8,6,4,32,128]{4,3,1,0,2:T(8,128)(2,1)} %bitcast_dynamic-update-slice_fusion.3), channel_id=1, source_target_pairs={{0,8},{1,9},{2,10},{3,11},{4,12},{5,13},{6,14},{7,15},{8,0},{9,1},... | collective-permute-start | bytes 4718600 | tf_op jit(solution)/shard_map/ppermute | solution.py:27
  41.5 26.2 %copy-start.4 = (f32[512]{0:T(512)S(1)}, f32[512]{0:T(512)}, u32[]{:S(2)}) copy-start(f32[512]{0:T(512)} %param.10) | copy-start | bytes 6148
  41.5 26.4 %copy-start.5 = (f32[512]{0:T(512)S(1)}, f32[512]{0:T(512)}, u32[]{:S(2)}) copy-start(f32[512]{0:T(512)} %param.11) | copy-start | bytes 6148
  41.6 26.5 %copy-start.6 = (f32[512]{0:T(512)S(1)}, f32[512]{0:T(512)}, u32[]{:S(2)}) copy-start(f32[512]{0:T(512)} %param.12) | copy-start | bytes 6148
  41.6 11.6 %collective-permute-start.20 = (bf16[1,2,8,512]{3,0,2,1:T(2,128)(2,1)S(1)}, bf16[1,2,8,512]{3,0,2,1:T(2,128)(2,1)S(1)}, u32[]{:S(2)}, u32[]{:S(2)}) collective-permute-start(bf16[1,2,8,512]{3,0,2,1:T(2,128)(2,1)S(1)} %get-tuple-element.15), channel_id=1, source_target_pairs={{0,8},{1,9},{2,10},{3,11},{4,12},{5,13},{6,14},{7,15},{8,16},{9,17... | collective-permute-start | bytes 49160 | tf_op jit(solution)/shard_map/ppermute | solution.py:27
  44.0 9.2 %collective-permute-start.21 = (bf16[1,2,8,512]{3,0,2,1:T(2,128)(2,1)S(1)}, bf16[1,2,8,512]{3,0,2,1:T(2,128)(2,1)S(1)}, u32[]{:S(2)}, u32[]{:S(2)}) collective-permute-start(bf16[1,2,8,512]{3,0,2,1:T(2,128)(2,1)S(1)} %get-tuple-element.16), channel_id=1, source_target_pairs={{8,0},{9,1},{10,2},{11,3},{12,4},{13,5},{14,6},{15,7},{16,8},{17,9... | collective-permute-start | bytes 49160 | tf_op jit(solution)/shard_map/ppermute | solution.py:27
  47.2 40.2 %collective-permute-start.10 = (bf16[8,6,32,128]{3,2,1,0:T(8,128)(2,1)}, bf16[8,6,32,128]{3,2,1,0:T(8,128)(2,1)}, u32[]{:S(2)}, u32[]{:S(2)}) collective-permute-start(bf16[8,6,32,128]{3,2,1,0:T(8,128)(2,1)} %get-tuple-element.9), channel_id=1, source_target_pairs={{1,0},{2,1},{3,2},{4,3},{5,4},{6,5},{7,6},{9,8},{10,9},{11,10},{12... | collective-permute-start | bytes 1179656 | tf_op jit(solution)/shard_map/ppermute | solution.py:27
  53.4 27.2 %collective-permute-start.22 = (bf16[62,2,1,512]{3,0,2,1:T(8,128)(2,1)S(1)}, bf16[62,2,1,512]{3,0,2,1:T(8,128)(2,1)S(1)}, u32[]{:S(2)}, u32[]{:S(2)}) collective-permute-start(bf16[62,2,1,512]{3,0,2,1:T(8,128)(2,1)S(1)} %get-tuple-element.13), channel_id=1, source_target_pairs={{0,1},{1,2},{2,3},{3,4},{4,5},{5,6},{6,7},{8,9},{9,10},{10,11},{11... | collective-permute-start | bytes 380936 | tf_op jit(solution)/shard_map/ppermute | solution.py:27
  55.3 25.3 %collective-permute-start.23 = (bf16[62,2,1,512]{3,0,2,1:T(8,128)(2,1)S(1)}, bf16[62,2,1,512]{3,0,2,1:T(8,128)(2,1)S(1)}, u32[]{:S(2)}, u32[]{:S(2)}) collective-permute-start(bf16[62,2,1,512]{3,0,2,1:T(8,128)(2,1)S(1)} %get-tuple-element.14), channel_id=1, source_target_pairs={{1,0},{2,1},{3,2},{4,3},{5,4},{6,5},{7,6},{9,8},{10,9},{11,10},{12... | collective-permute-start | bytes 380936 | tf_op jit(solution)/shard_map/ppermute | solution.py:27
  61.3 43.0 %collective-permute-start.13 = (bf16[3,3,3,32,512]{4,3,2,1,0:T(8,128)(2,1)}, bf16[3,3,3,32,512]{4,3,2,1,0:T(8,128)(2,1)}, u32[]{:S(2)}, u32[]{:S(2)}) collective-permute-start(bf16[3,3,3,32,512]{4,3,2,1,0:T(8,128)(2,1)} %bitcast.32), channel_id=1, source_target_pairs={{0,64},{1,65},{2,66},{3,67},{4,68},{5,69},{6,70},{7,71},{8,72},{9,... | collective-permute-start | bytes 2654216 | tf_op jit(solution)/shard_map/ppermute | solution.py:27
  68.9 3.0 %copy-start.1 = (bf16[3,3,3,512,256]{4,3,2,1,0:T(8,128)(2,1)S(1)}, bf16[3,3,3,512,256]{4,3,2,1,0:T(8,128)(2,1)}, u32[]{:S(2)}) copy-start(bf16[3,3,3,512,256]{4,3,2,1,0:T(8,128)(2,1)} %param.14) | copy-start | bytes 21233668
  75.4 4.5 %copy-start = (bf16[3,2,2,2,2,4,4,32,256]{8,7,6,5,4,3,2,1,0:T(8,128)(2,1)}, bf16[3,2,2,2,2,4,4,32,256]{8,7,6,5,4,3,2,1,0:T(8,128)(2,1)S(1)}, u32[]{:S(2)}) copy-start(bf16[3,2,2,2,2,4,4,32,256]{8,7,6,5,4,3,2,1,0:T(8,128)(2,1)S(1)} %collapse.1) | copy-start | bytes 37748740
  80.5 23.8 %collective-permute-start.12 = (bf16[3,3,3,32,512]{4,3,2,1,0:T(8,128)(2,1)}, bf16[3,3,3,32,512]{4,3,2,1,0:T(8,128)(2,1)}, u32[]{:S(2)}, u32[]{:S(2)}) collective-permute-start(bf16[3,3,3,32,512]{4,3,2,1,0:T(8,128)(2,1)} %bitcast.32), channel_id=1, source_target_pairs={{0,32},{1,33},{2,34},{3,35},{4,36},{5,37},{6,38},{7,39},{8,40},{9,... | collective-permute-start | bytes 2654216 | tf_op jit(solution)/shard_map/ppermute | solution.py:27
  80.6 12.5 %collective-permute-start.8 = (bf16[8,6,32,128]{3,2,1,0:T(8,128)(2,1)S(1)}, bf16[8,6,32,128]{3,2,1,0:T(8,128)(2,1)}, u32[]{:S(2)}, u32[]{:S(2)}) collective-permute-start(bf16[8,6,32,128]{3,2,1,0:T(8,128)(2,1)S(1)} %get-tuple-element.10), channel_id=1, source_target_pairs={{0,1},{1,2},{2,3},{3,4},{4,5},{5,6},{6,7},{8,9},{9,10},{10,11},{11... | collective-permute-start | bytes 1179656 | tf_op jit(solution)/shard_map/ppermute | solution.py:27
  84.2 9.9 %slice-start = ((s8[7077888]{0:T(1024)(128)(4,1)}), s8[2883584]{0:T(1024)(128)(4,1)S(1)}, s32[]{:S(2)}) async-start(s8[7077888]{0:T(1024)(128)(4,1)} %bitcast.98), calls=%async_computation.1 | async-start | bytes 5767168
  87.5 6.6 %slice-start.1 = ((s8[7077888]{0:T(1024)(128)(4,1)}), s8[4194304]{0:T(1024)(128)(4,1)S(1)}, s32[]{:S(2)}) async-start(s8[7077888]{0:T(1024)(128)(4,1)} %bitcast.98), calls=%async_computation.2 | async-start | bytes 8388608
  87.5 18.1 %collective-permute-start.14 = (bf16[3,3,3,32,512]{4,3,2,1,0:T(8,128)(2,1)}, bf16[3,3,3,32,512]{4,3,2,1,0:T(8,128)(2,1)S(1)}, u32[]{:S(2)}, u32[]{:S(2)}) collective-permute-start(bf16[3,3,3,32,512]{4,3,2,1,0:T(8,128)(2,1)} %bitcast.32), channel_id=1, source_target_pairs={{0,96},{1,97},{2,98},{3,99},{4,100},{5,101},{6,102},{7,103},{8,104... | collective-permute-start | bytes 2654216 | tf_op jit(solution)/shard_map/ppermute | solution.py:27
  93.1 12.5 %collective-permute-start.11 = (bf16[8,6,32,128]{3,2,1,0:T(8,128)(2,1)}, bf16[8,6,32,128]{3,2,1,0:T(8,128)(2,1)S(1)}, u32[]{:S(2)}, u32[]{:S(2)}) collective-permute-start(bf16[8,6,32,128]{3,2,1,0:T(8,128)(2,1)} %collective-permute-done.10.down), channel_id=1, source_target_pairs={{0,8},{1,9},{2,10},{3,11},{4,12},{5,13},{6,14},{7,15},{8,0},{9,1},... | collective-permute-start | bytes 1179656 | tf_op jit(solution)/shard_map/ppermute | solution.py:27
  93.2 12.4 %collective-permute-start.9 = (bf16[8,6,32,128]{3,2,1,0:T(8,128)(2,1)}, bf16[8,6,32,128]{3,2,1,0:T(8,128)(2,1)S(1)}, u32[]{:S(2)}, u32[]{:S(2)}) collective-permute-start(bf16[8,6,32,128]{3,2,1,0:T(8,128)(2,1)} %collective-permute-done.8.up), channel_id=1, source_target_pairs={{0,8},{1,9},{2,10},{3,11},{4,12},{5,13},{6,14},{7,15},{8,0},{9,1},... | collective-permute-start | bytes 1179656 | tf_op jit(solution)/shard_map/ppermute | solution.py:27
  98.0 3.4 %copy-start.2 = (f32[2,2,2,4,32,256]{5,4,3,2,1,0:T(8,128)}, f32[2,2,2,4,32,256]{5,4,3,2,1,0:T(8,128)S(1)}, u32[]{:S(2)}) copy-start(f32[2,2,2,4,32,256]{5,4,3,2,1,0:T(8,128)S(1)} %conv_rim.1.rim) | copy-start | bytes 3145732
  105.6 1.1 copy-start.7
  105.6 1.2 copy-start.8
  105.6 1.1 copy-start.9
  123.1 18.4 %all-to-all-start = ((f32[128,1,128]{2,1,0:T(1,128)}), f32[128,1,128]{2,1,0:T(1,128)S(1)}, u32[]{:S(2)}, u32[]{:S(2)}) async-start(f32[128,1,128]{2,1,0:T(1,128)} %broadcast_in_dim.20), calls=%async_computation | async-start | bytes 131072 | tf_op jit(solution)/shard_map/all_to_all | solution.py:300
  134.6 7.6 %collective-permute-start.16 = (bf16[4,4,32,128]{3,2,0,1:T(8,128)(2,1)S(1)}, bf16[4,4,32,128]{3,2,0,1:T(8,128)(2,1)S(1)}, u32[]{:S(2)}, u32[]{:S(2)}) collective-permute-start(bf16[4,4,32,128]{3,2,0,1:T(8,128)(2,1)S(1)} %bitcast.107), channel_id=1, source_target_pairs={{0,16},{1,17},{2,18},{3,19},{4,20},{5,21},{6,22},{7,23},{8,24},{9,... | collective-permute-start | bytes 393224 | tf_op jit(solution)/shard_map/ppermute | solution.py:27
  136.8 7.4 %collective-permute-start.17 = (bf16[4,4,32,128]{3,2,0,1:T(8,128)(2,1)S(1)}, bf16[4,4,32,128]{3,2,0,1:T(8,128)(2,1)S(1)}, u32[]{:S(2)}, u32[]{:S(2)}) collective-permute-start(bf16[4,4,32,128]{3,2,0,1:T(8,128)(2,1)S(1)} %bitcast.106), channel_id=1, source_target_pairs={{0,24},{1,25},{2,26},{3,27},{4,28},{5,29},{6,30},{7,31},{8,16},{9,... | collective-permute-start | bytes 393224 | tf_op jit(solution)/shard_map/ppermute | solution.py:27
  137.7 6.4 %collective-permute-start.15 = (bf16[4,4,32,128]{3,2,0,1:T(8,128)(2,1)S(1)}, bf16[4,4,32,128]{3,2,0,1:T(8,128)(2,1)S(1)}, u32[]{:S(2)}, u32[]{:S(2)}) collective-permute-start(bf16[4,4,32,128]{3,2,0,1:T(8,128)(2,1)S(1)} %bitcast.105), channel_id=1, source_target_pairs={{0,8},{1,9},{2,10},{3,11},{4,12},{5,13},{6,14},{7,15},{8,0},{9,1},... | collective-permute-start | bytes 393224 | tf_op jit(solution)/shard_map/ppermute | solution.py:27
  144.3 9.1 %collective-permute-start.19 = (bf16[4,4,32,128]{3,2,1,0:T(8,128)(2,1)S(1)}, bf16[4,4,32,128]{3,2,1,0:T(8,128)(2,1)S(1)}, u32[]{:S(2)}, u32[]{:S(2)}) collective-permute-start(bf16[4,4,32,128]{3,2,1,0:T(8,128)(2,1)S(1)} %get-tuple-element.26), channel_id=1, source_target_pairs={{1,0},{2,1},{3,2},{4,3},{5,4},{6,5},{7,6},{9,8},{10,9},{11,10},{12... | collective-permute-start | bytes 393224 | tf_op jit(solution)/shard_map/ppermute | solution.py:27
  149.7 9.2 %collective-permute-start.18 = (bf16[4,4,32,128]{3,2,1,0:T(8,128)(2,1)S(1)}, bf16[4,4,32,128]{3,2,1,0:T(8,128)(2,1)S(1)}, u32[]{:S(2)}, u32[]{:S(2)}) collective-permute-start(bf16[4,4,32,128]{3,2,1,0:T(8,128)(2,1)S(1)} %get-tuple-element.27), channel_id=1, source_target_pairs={{0,1},{1,2},{2,3},{3,4},{4,5},{5,6},{6,7},{8,9},{9,10},{10,11},{11... | collective-permute-start | bytes 393224 | tf_op jit(solution)/shard_map/ppermute | solution.py:27
  153.3 5.6 %copy-start.10 = (bf16[4,4,32,128]{3,2,1,0:T(8,128)(2,1)}, bf16[4,4,32,128]{3,2,1,0:T(8,128)(2,1)S(1)}, u32[]{:S(2)}) copy-start(bf16[4,4,32,128]{3,2,1,0:T(8,128)(2,1)S(1)} %collective-permute-done.19.down) | copy-start | bytes 393220
  159.0 0.7 copy-start.11
where the time goes:
time: 178 us
  starting transfers between devices  66.7 us (37%)
  local copies, waits for them, and re-layouts  41.2 us (23%)
  Pallas kernels  36.8 us (21%)
  waiting for transfers between devices  29.3 us (16%)
  other arithmetic  3.03 us (2%)
    ppermute x24, starting transfers between devices, send(): return lax.ppermute(array, BOTH, device_perm(move))  57.2 us
    ppermute x24, waiting for transfers between devices, send(): return lax.ppermute(array, BOTH, device_perm(move))  26.3 us
    pallas_call x1, Pallas kernels, conv_in(): pl.pallas_call(conv_in_kernel, out_shape=(jax.ShapeDtypeStruct((4, 4, 4,...  14.8 us
    pallas_call x1, Pallas kernels, conv_out(): pl.pallas_call(conv_out_kernel, grid=(12,), out_shape=jax.ShapeDtypeStruc...  14.8 us
    unnamed x36, local copies, waits for them, and re-layouts  14.6 us
    all_to_all x1, starting transfers between devices, body(): lax.all_to_all(sent, BOTH, split_axis=0, concat_axis=0, tiled=True)  9.5 us
    another operation x2, local copies, waits for them, and re-layouts, body(): main = jnp.stack(got)  4.11 us
    pallas_call x1, Pallas kernels, conv_rim(): pl.pallas_call(rim_kernel, grid=(1,), out_shape=jax.ShapeDtypeStruct((2,...  3.8 us
  transfers between devices with their start and end apart: 25, of which 7 were waited for; matrix products, arithmetic and copies ran while one was open for 15% of the time, Pallas kernels for 4%

commit v1 on v0

v1 whole, which is shorter than its diff:
```python
import jax
import jax.numpy as jnp
from jax import lax
from jax.experimental import pallas as pl
from jax.experimental.pallas import tpu as pltpu
from jax.sharding import PartitionSpec as P

GROUPS = 32
BOTH = ("chan", "rows")
BF16 = jnp.bfloat16
F32 = jnp.float32


def device_perm(move):
    pairs = []
    for d in range(128):
        chan, row = divmod(d, 8)
        to = move(chan // 4, chan // 2 % 2, chan % 2, row)
        if to is not None:
            z, half, core, row = to
            pairs.append((d, ((z % 4) * 4 + half * 2 + core) * 8 + row))
    return pairs


def send(array, move):
    return lax.ppermute(array, BOTH, device_perm(move))


def to_row(step):
    return lambda z, half, core, row: (z, half, core, row + step) if 0 <= row + step < 8 else None


def to_chan(step):
    def move(z, half, core, row):
        chan = z * 4 + half * 2 + core + step
        return (chan // 4, chan // 2 % 2, chan % 2, row) if 0 <= chan < 16 else None

    return move


def conv_in_kernel(place, own, other, own_swap, other_swap, w0, w1, w3, near, far, bias,
                   strips, stats, x, w, turned, moments, sems):
    z, half, core, odd = (place[i] for i in range(4))

    def fetch(i, source, target):
        return pltpu.make_async_copy(source, target, sems.at[i])

    early, late = [], []
    for source, dh, owner in ((own, 0, core), (other, 1, core), (own_swap, 0, 1 - core), (other_swap, 1, 1 - core)):
        for dz in range(4):
            start = (((z + 4 - dz) % 4) * 4 + (half + dh) % 2 * 2 + owner) * 32
            rows = pl.ds(pl.multiple_of(start, 32), 32)
            for group, frames in ((early, pl.ds(0, 3)), (late, pl.ds(3, 3))):
                group.append((source.at[dz, :, frames], x.at[:, frames, rows, :]))
    for dz, source in ((0, w0), (1, w1), (3, w3)):
        early.append((source, w.at[:, :, (z + 4 - dz) % 4]))
    for which, source in ((odd, near), (1 - odd, far)):
        columns = pl.ds(pl.multiple_of(which * 256, 256), 256)
        early.append((source, w.at[:, :, (z + 2) % 4, :, columns]))
    early = [fetch(i, *pair) for i, pair in enumerate(early)]
    late = [fetch(i + len(early), *pair) for i, pair in enumerate(late)]
    for copy in early + late:
        copy.start()
    moments[...] = jnp.zeros_like(moments)
    lane = lax.broadcasted_iota(jnp.int32, (128, 128), 1)
    inside = (lane >= 4) & (lane < 124)

    def frame(t, _):
        for g in range(2):
            summed = None
            for a in range(3):
                for b in range(3):
                    rhs = jnp.concatenate([x[b + g * 2 + h, t + a] for h in range(2)], axis=1)
                    lhs = w[a * 3 + b].reshape(384, 512)
                    term = jnp.dot(lhs, rhs, preferred_element_type=F32)
                    summed = term if summed is None else summed + term
            for h in range(2):
                part = summed[:, h * 128 : (h + 1) * 128]
                value = pltpu.roll(part[0:128], 1, 1) + part[128:256] + pltpu.roll(part[256:384], 127, 1)
                value = (value + bias[...]).astype(BF16).astype(F32)
                kept = jnp.where(inside, value, 0.0)
                moments[0] += kept
                moments[1] += kept * kept
                turned[...] = value.T
                for s in range(4):
                    strips[s, t, g * 2 + h] = turned[3 + 30 * s : 35 + 30 * s, :].astype(BF16)
        return 0

    for copy in early:
        copy.wait()
    frame(0, 0)
    for copy in late:
        copy.wait()
    lax.fori_loop(1, 4, frame, 0)
    for i in range(2):
        grouped = jnp.sum(moments[i].reshape(8, 16, 128), axis=1)
        stats[i] = jnp.broadcast_to(jnp.sum(grouped, axis=1, keepdims=True), (8, 128))


def conv_in(place, parts, weights, bias):
    return pl.pallas_call(
        conv_in_kernel,
        out_shape=(jax.ShapeDtypeStruct((4, 4, 4, 32, 128), BF16), jax.ShapeDtypeStruct((2, 8, 128), F32)),
        in_specs=[pl.BlockSpec(memory_space=pltpu.SMEM)] + [pl.BlockSpec(memory_space=pl.ANY)] * 9
        + [pl.BlockSpec(memory_space=pltpu.VMEM)],
        out_specs=(pl.BlockSpec(memory_space=pltpu.VMEM), pl.BlockSpec(memory_space=pltpu.VMEM)),
        scratch_shapes=[
            pltpu.VMEM((6, 6, 512, 128), BF16),
            pltpu.VMEM((9, 3, 4, 32, 512), BF16),
            pltpu.VMEM((128, 128), F32),
            pltpu.VMEM((2, 128, 128), F32),
            pltpu.SemaphoreType.DMA((37,)),
        ],
        compiler_params=pltpu.CompilerParams(vmem_limit_bytes=24 * 1024 * 1024),
        cost_estimate=pl.CostEstimate(flops=7_200_000_000, bytes_accessed=9_000_000, transcendentals=0),
        name="conv_in",
    )(place, *parts, *weights, bias)


def collapse_kernel(taps, out):
    def pairs(t0, t1, t2):
        return ((t0, t1 + t2), (t0 + t1, t2))

    for z in range(4):
        wide = [[taps[0, b, c, z, 0].astype(F32) for c in range(3)] for b in range(3)]
        by_col = [pairs(*row) for row in wide]
        for pw in range(2):
            for i in range(2):
                by_row = pairs(by_col[0][pw][i], by_col[1][pw][i], by_col[2][pw][i])
                for ph in range(2):
                    for j in range(2):
                        out[0, ph, j, pw, i, 0, z] = by_row[ph][j].astype(BF16)


def collapse(weight):
    def kernel(taps, out):
        pltpu.emit_pipeline(
            collapse_kernel,
            grid=(3, 4),
            in_specs=[pl.BlockSpec((1, 3, 3, 4, 1, 32, 256), lambda a, p: (a, 0, 0, 0, p, 0, 0))],
            out_specs=[pl.BlockSpec((1, 2, 2, 2, 2, 1, 4, 32, 256), lambda a, p: (a, 0, 0, 0, 0, p, 0, 0, 0))],
        )(taps, out)

    out = pl.pallas_call(
        kernel,
        out_shape=jax.ShapeDtypeStruct((3, 2, 2, 2, 2, 4, 4, 32, 256), BF16),
        in_specs=[pl.BlockSpec(memory_space=pltpu.HBM)],
        out_specs=pl.BlockSpec(memory_space=pltpu.HBM),
        compiler_params=pltpu.CompilerParams(vmem_limit_bytes=50 * 1024 * 1024),
        cost_estimate=pl.CostEstimate(flops=0, bytes_accessed=0, transcendentals=0),
        name="collapse",
    )(weight.reshape(3, 3, 3, 4, 4, 32, 256))
    return out.reshape(12, 2, 1024, 256)


def rim_kernel(rim, weight, out, w, wide, fine, sem):
    fetch = pltpu.make_async_copy(weight.at[0:2], w, sem)
    fetch.start()
    for t in range(2):
        for h in range(10):
            line = rim[t, h].astype(F32)
            for s in range(3):
                moved = line if s == 0 else pltpu.roll(line, 64 - s, 0)
                wide[t, h, :, s * 512 : s * 512 + 512] = moved.astype(BF16)
    fetch.wait()
    for t in range(2):
        summed = None
        for a in range(2 - t):
            for b in range(3):
                lhs = wide[t + a, b : b + 8].reshape(512, 1536)
                term = jnp.dot(lhs, w[a, b], preferred_element_type=F32)
                summed = term if summed is None else summed + term
        for c in range(2):
            fine[...] = summed[:, c * 128 : c * 128 + 128].reshape(8, 64, 128)
            for r in range(8):
                for pw in range(2):
                    out[pw, r % 2, t, r // 2, :, c * 128 : c * 128 + 128] = fine[r, pl.ds(pw, 32, stride=2), :]


def conv_rim(tall, weight):
    return pl.pallas_call(
        rim_kernel,
        out_shape=jax.ShapeDtypeStruct((2, 2, 2, 4, 32, 256), F32),
        in_specs=[pl.BlockSpec(memory_space=pltpu.VMEM), pl.BlockSpec(memory_space=pltpu.HBM)],
        out_specs=pl.BlockSpec(memory_space=pltpu.VMEM),
        scratch_shapes=[
            pltpu.VMEM((2, 3, 1536, 256), BF16),
            pltpu.VMEM((2, 10, 64, 1536), BF16),
            pltpu.VMEM((8, 64, 128), F32),
            pltpu.SemaphoreType.DMA,
        ],
        compiler_params=pltpu.CompilerParams(vmem_limit_bytes=50 * 1024 * 1024),
        cost_estimate=pl.CostEstimate(flops=0, bytes_accessed=0, transcendentals=0),
        name="conv_rim",
    )(tall, weight.reshape(3, 3, 1536, 256))


def conv_out_kernel(place, main, up, down, vectors, rim, bias, weight, out, n, acc, w, sems):
    fetches = [pltpu.make_async_copy(weight.at[tap], w.at[tap], sems.at[tap]) for tap in range(3)]
    for fetch in fetches:
        fetch.start()
    own, left, right, top, bottom = (place[i] for i in range(5))
    row = lax.broadcasted_iota(jnp.int32, (32, 128), 0)
    keep_col = jnp.where(
        ((row == 0) & (left == 1)) | ((row == 31) & (right == 1)), 0.0, 1.0)
    keep = [keep_col] * 6
    keep[0] = keep_col * jnp.where(top == 1, 0.0, 1.0)
    keep[5] = keep_col * jnp.where(bottom == 1, 0.0, 1.0)

    def frame(t, _):
        for r in range(4):
            p = own ^ r
            vec = vectors[p]
            for h in range(6):
                raw = up[r, t] if h == 0 else down[r, t] if h == 5 else main[r, t, h - 1]
                v = (raw.astype(F32) - vec[0:1]) * vec[1:2] + vec[2:3]
                v = v / (1.0 + jnp.exp(-v)) * keep[h]
                for s in range(3):
                    moved = v if s == 0 else pltpu.roll(v, 32 - s, 0)
                    start = pl.multiple_of(s * 512 + p * 128, 128)
                    n[t, h, :, pl.ds(start, 128)] = moved.astype(BF16)
        return 0

    lax.fori_loop(0, 4, frame, 0)
    whole = jnp.broadcast_to(bias[...], (32, 256))
    for pw in range(2):
        for ph in range(2):
            for t in range(4):
                for h in range(4):
                    acc[pw, ph, t, h] = rim[pw, ph, t, h] + whole if t < 2 else whole

    for tap in range(3):
        fetches[tap].wait()
        frames = 2 + tap
        for ph in range(2):
            for j in range(2):
                for pw in range(2):
                    lhs = n[0:frames, ph + j : ph + j + 4, :, pw * 512 : pw * 512 + 1024]
                    term = jnp.dot(lhs.reshape(frames * 128, 1024), w[tap, ph * 2 + j, pw],
                                   preferred_element_type=F32)
                    acc[pw, ph, 4 - frames : 4] += term.reshape(frames, 4, 32, 256)
    out[...] = acc[...].astype(BF16)


def conv_out(place, main, up, down, vectors, rim, bias, weight):
    whole = pl.BlockSpec(memory_space=pltpu.VMEM)
    return pl.pallas_call(
        conv_out_kernel,
        out_shape=jax.ShapeDtypeStruct((2, 2, 4, 4, 32, 256), BF16),
        in_specs=[pl.BlockSpec(memory_space=pltpu.SMEM)] + [whole] * 6 + [pl.BlockSpec(memory_space=pltpu.HBM)],
        out_specs=whole,
        scratch_shapes=[
            pltpu.VMEM((4, 6, 32, 1536), BF16),
            pltpu.VMEM((2, 2, 4, 4, 32, 256), F32),
            pltpu.VMEM((3, 4, 2, 1024, 256), BF16),
            pltpu.SemaphoreType.DMA((3,)),
        ],
        compiler_params=pltpu.CompilerParams(vmem_limit_bytes=52 * 1024 * 1024),
        cost_estimate=pl.CostEstimate(flops=4_900_000_000, bytes_accessed=18_000_000, transcendentals=400_000),
        name="conv_out",
    )(place, main, up, down, vectors, rim, bias, weight.reshape(3, 4, 2, 1024, 256))


def body(
    latents,
    conv_in_weight,
    conv_in_bias,
    norm_gain,
    norm_shift,
    hidden_rim,
    conv_out_weight,
    conv_out_bias,
):
    chan, row = lax.axis_index("chan"), lax.axis_index("rows")
    z, half, core = chan // 4, chan // 2 % 2, chan % 2
    strip = chan % 4
    flip_core = lambda z, half, core, row: (z, half, 1 - core, row)

    flip_half = lambda z, half, core, row: (z, 1 - half, core, row)
    along_z = lambda dz: lambda z, half, core, row: (z + dz, half, core, row)

    weights = conv_in_weight.swapaxes(3, 4).reshape(9, 3, 32, 512)
    padded = jnp.pad(latents.transpose(2, 1, 3, 0), ((0, 0), (0, 0), (0, 0), (4, 28)))
    from_edge = lambda i, j: jnp.concatenate([padded[i].reshape(192, 512), hidden_rim[:, :, j].reshape(120, 512)])
    above, below = send(from_edge(3, 7), to_row(1)), send(from_edge(0, 0), to_row(-1))
    tall = jnp.concatenate([above[:192].reshape(1, 6, 32, 512), padded, below[:192].reshape(1, 6, 32, 512)])
    rim = jnp.concatenate([above[192:].reshape(60, 2, 1, 512), hidden_rim, below[192:].reshape(60, 2, 1, 512)], axis=2)

    pieces = jnp.stack([tall[..., 120 * i : 120 * i + 128] for i in range(4)])
    own = []
    for dz in range(4):
        piece = lax.dynamic_index_in_dim(pieces, (z + dz) % 4, 0, keepdims=False)
        own.append(send(piece, along_z(dz)) if dz else piece)
    own = jnp.stack(own)
    before, after = send(rim[59:60], to_chan(1)), send(rim[0:1], to_chan(-1))
    rim = jnp.concatenate([before, rim, after, jnp.zeros((2, 2, 10, 512), BF16)], axis=0).transpose(1, 2, 0, 3)

    own, rim, weights, conv_out_weight = lax.optimization_barrier((own, rim, weights, conv_out_weight))
    other = send(own, flip_half)
    odd = row % 2
    near = send(lax.dynamic_slice_in_dim(weights, odd * 256, 256, axis=3), along_z(2))
    own_swap = send(own, flip_core)
    collapsed = collapse(conv_out_weight)
    near_first, rim, collapsed = lax.optimization_barrier((near, rim, collapsed))
    far = send(near_first, lambda z, half, core, row: (z, half, core, row ^ 1))
    rim = conv_rim(rim, conv_out_weight)
    weights = [weights, send(weights, along_z(1)), send(weights, along_z(3)), near_first, far]
    other, collapsed, rim, weights = lax.optimization_barrier((other, collapsed, rim, weights))
    parts = [own, other, own_swap, send(other, flip_core)]

    by_owner = conv_in_bias.reshape(4, 4, 32)
    bias = lax.dynamic_index_in_dim(by_owner, strip, 1, keepdims=False).reshape(128, 1)
    place = jnp.stack([z, half, core, odd]).astype(jnp.int32)
    strips, stats = conv_in(place, parts, weights, jnp.broadcast_to(bias, (128, 128)))

    parts = []
    for r in range(4):
        part = lax.dynamic_index_in_dim(strips, strip ^ r, 0, keepdims=False)
        if r:
            part = send(part, lambda z, half, core, row: (z, half ^ (r // 2), core ^ (r % 2), row))
        parts.append(part)
    stats, parts[1] = lax.optimization_barrier((stats, parts[1]))
    sent = jnp.broadcast_to(jnp.pad(stats[:, :, 0].reshape(1, 16), ((0, 0), (0, 112))), (128, 128))
    first = jnp.stack(parts)
    above, below = send(first[:, :, 3], to_row(1)), send(first[:, :, 0], to_row(-1))
    gathered = lax.all_to_all(sent, BOTH, split_axis=0, concat_axis=0, tiled=True)
    sums, squares = gathered.reshape(4, 4, 8, 128)[..., :16].sum(axis=(0, 2)).reshape(4, 2, 8).swapaxes(0, 1)
    counted = float(480 * 4 * 32 * 16)
    mean = sums / counted
    var = squares / counted - mean * mean
    inv = 1.0 / jnp.sqrt(var + 1e-06)
    by_place = lambda vector: vector.reshape(4, 4, 32).swapaxes(0, 1).reshape(4, 128)
    vectors = jnp.stack(
        [jnp.repeat(mean, 16, axis=1), jnp.repeat(inv, 16, axis=1) * by_place(norm_gain), by_place(norm_shift)]
        + [jnp.zeros((4, 128), F32)] * 5, axis=1)

    edges = jnp.stack([strip, chan == 0, chan == 15, row == 0, row == 7]).astype(jnp.int32)
    decoded = conv_out(edges, first, above, below, vectors, rim, conv_out_bias.reshape(1, 256),
                       collapsed)
    return decoded.transpose(4, 0, 2, 3, 1, 5)[:30].reshape(60, 4, 8, 256)


def solution(mesh):
    return jax.shard_map(
        body,
        mesh=mesh,
        in_specs=(
            P(None, None, "rows", "chan"),
            P(None, None, None, None, "chan"),
            P(),
            P(),
            P(),
            P("chan", None, "rows", None),
            P(),
            P(),
        ),
        out_specs=P("chan", None, "rows", None),
        check_vma=False,
    )
```

time: 178 us -> 134 us (0.75); the launches traced: 178 us -> 132 us
  starting transfers between devices: 66.7 us -> 38.3 us
  local copies, waits for them, and re-layouts: 41.2 us -> 18.1 us
  waiting for transfers between devices: 29.3 us -> 33.6 us
    ppermute x24 -> x19, starting transfers between devices: 57.2 us -> 34.5 us  [send(): return lax.ppermute(array, BOTH, device_perm(move))]
    ppermute x24 -> x19, waiting for transfers between devices: 26.3 us -> 33.5 us  [send(): return lax.ppermute(array, BOTH, device_perm(move))]
    unnamed x36 -> x37, local copies, waits for them, and re-layouts: 14.6 us -> 8.64 us
    all_to_all x1, starting transfers between devices: 9.5 us -> 3.82 us  [body(): lax.all_to_all(sent, BOTH, split_axis=0, concat_axis=0, tiled=True)]
    another operation x4, local copies, waits for them, and re-layouts: 5.09 us -> 0.55 us  [the longest x1 0.35 us: body(): pieces = jnp.stack([tall[..., 120 * i:120 * i + 128] for i in range(4)])]
    pallas_call x3, Pallas kernels: 22 us -> 26.5 us  [the longest x1 11.5 us: collapse(): pl.pallas_call(kernel, out_shape=jax.ShapeDtypeStruct((3, 2, 2, 2, 2, 4,...]
    reshape x1 -> x2, local copies, waits for them, and re-layouts: 3.31 us -> 0.11 us  [the longest x1 0.05 us: body(): above[192:].reshape(60, 2, 1, 512)]
    pallas_call x1, Pallas kernels: 14.8 us -> 11.8 us  [conv_in(): pl.pallas_call(conv_in_kernel, out_shape=(jax.ShapeDtypeStruct((4, 4, 4,...]
  transfers between devices with their start and end apart: 25 -> 20, of which waited for: 7 -> 13; matrix products, arithmetic and copies ran while one was open for 15% -> 3% of each run, Pallas kernels for 4% -> 14%
where the time goes in v1:
time: 134 us; the launch traced here: 132 us
  starting transfers between devices  38.3 us (29%)
  Pallas kernels  38.3 us (29%)
  waiting for transfers between devices  33.6 us (25%)
  local copies, waits for them, and re-layouts  18.1 us (14%)
  other arithmetic  2.79 us (2%)
    ppermute x19, starting transfers between devices, send(): return lax.ppermute(array, BOTH, device_perm(move))  34.5 us
    ppermute x19, waiting for transfers between devices, send(): return lax.ppermute(array, BOTH, device_perm(move))  33.5 us
    pallas_call x1, Pallas kernels, conv_in(): pl.pallas_call(conv_in_kernel, out_shape=(jax.ShapeDtypeStruct((4, 4, 4,...  11.8 us
    pallas_call x1, Pallas kernels, collapse(): pl.pallas_call(kernel, out_shape=jax.ShapeDtypeStruct((3, 2, 2, 2, 2, 4,...  11.5 us
    pallas_call x1, Pallas kernels, conv_out(): pl.pallas_call(conv_out_kernel, out_shape=jax.ShapeDtypeStruct((2, 2, 4,...  8.72 us
    unnamed x37, local copies, waits for them, and re-layouts  8.64 us
    pallas_call x1, Pallas kernels, conv_rim(): pl.pallas_call(rim_kernel, out_shape=jax.ShapeDtypeStruct((2, 2, 2, 4, 32...  6.35 us
    all_to_all x1, starting transfers between devices, body(): lax.all_to_all(sent, BOTH, split_axis=0, concat_axis=0, tiled=True)  3.82 us
  transfers between devices with their start and end apart: 20, of which 13 were waited for; matrix products, arithmetic and copies ran while one was open for 3% of the time, Pallas kernels for 14%

profile of v1, /device:TPU:2, one launch (start us, length us, event | category | flops | bytes accessed | tf_op | source)
XLA Modules:
  0.0 131.7 jit_solution(11342573958231130135)
XLA Ops:
  0.0 2.9 %slice_reduce_fusion.1 = (bf16[60,2,512]{2,1,0:T(2,128)(2,1)S(1)}, bf16[60,2,512]{2,1,0:T(2,128)(2,1)S(1)}) fusion(bf16[60,2,8,512]{3,2,1,0:T(8,128)(2,1)} %param.13), kind=kLoop, calls=%fused_computation.17 | loop fusion | bytes 491520 | tf_op jit(solution)/shard_map/slice | solution.py:284
  3.0 0.2 pad_slice_fusion.1
  3.2 4.9 %collective-permute-start.1 = (bf16[312,512]{1,0:T(8,128)(2,1)S(1)}, bf16[312,512]{1,0:T(8,128)(2,1)S(1)}, u32[]{:S(2)}, u32[]{:S(2)}) collective-permute-start(bf16[312,512]{1,0:T(8,128)(2,1)S(1)} %pad_maximum_fusion.5), channel_id=1, source_target_pairs={{1,0},{2,1},{3,2},{4,3},{5,4},{6,5},{7,6},{9,8},{10,9},{11,10},{12... | collective-permute-start | bytes 958472 | tf_op jit(solution)/shard_map/ppermute | solution.py:26
  8.2 1.9 %collective-permute-start = (bf16[312,512]{1,0:T(8,128)(2,1)S(1)}, bf16[312,512]{1,0:T(8,128)(2,1)S(1)}, u32[]{:S(2)}, u32[]{:S(2)}) collective-permute-start(bf16[312,512]{1,0:T(8,128)(2,1)S(1)} %pad_maximum_fusion.4), channel_id=1, source_target_pairs={{0,1},{1,2},{2,3},{3,4},{4,5},{5,6},{6,7},{8,9},{9,10},{10,11},{11... | collective-permute-start | bytes 958472 | tf_op jit(solution)/shard_map/ppermute | solution.py:26
  10.3 0.5 pad.10
  10.8 4.2 %collective-permute-done.1 = bf16[312,512]{1,0:T(8,128)(2,1)S(1)} collective-permute-done((bf16[312,512]{1,0:T(8,128)(2,1)S(1)}, bf16[312,512]{1,0:T(8,128)(2,1)S(1)}, u32[]{:S(2)}, u32[]{:S(2)}) %collective-permute-start.1) | collective-permute-done | bytes 319520 | tf_op jit(solution)/shard_map/ppermute | solution.py:26
  14.9 6.3 %collective-permute-done = bf16[312,512]{1,0:T(8,128)(2,1)S(1)} collective-permute-done((bf16[312,512]{1,0:T(8,128)(2,1)S(1)}, bf16[312,512]{1,0:T(8,128)(2,1)S(1)}, u32[]{:S(2)}, u32[]{:S(2)}) %collective-permute-start) | collective-permute-done | bytes 319520 | tf_op jit(solution)/shard_map/ppermute | solution.py:26
  21.3 0.1 pad_maximum_fusion
  21.4 0.4 slice_bitcast_fusion.3
  21.8 0.2 pad_maximum_fusion.1
  21.9 1.0 constant_dynamic-slice_fusion.6
  23.0 4.0 %collective-permute-start.4 = (bf16[6,6,32,128]{3,2,1,0:T(8,128)(2,1)}, bf16[6,6,32,128]{3,2,1,0:T(8,128)(2,1)}, u32[]{:S(2)}, u32[]{:S(2)}) collective-permute-start(bf16[6,6,32,128]{3,2,1,0:T(8,128)(2,1)} %get-tuple-element.48), channel_id=1, source_target_pairs={{0,96},{1,97},{2,98},{3,99},{4,100},{5,101},{6,102},{7,103},{8,104... | collective-permute-start | bytes 884744 | tf_op jit(solution)/shard_map/ppermute | solution.py:26
  27.0 1.3 collective-permute-start.2
  28.4 0.5 copy_dynamic-update-slice_fusion
  29.1 1.3 collective-permute-start.6
  30.4 3.0 %collective-permute-start.5 = (bf16[1,2,10,512]{3,0,2,1:T(2,128)(2,1)S(1)}, bf16[1,2,10,512]{3,0,2,1:T(2,128)(2,1)S(1)}, u32[]{:S(2)}, u32[]{:S(2)}) collective-permute-start(bf16[1,2,10,512]{3,0,2,1:T(2,128)(2,1)S(1)} %get-tuple-element.45), channel_id=1, source_target_pairs={{0,8},{1,9},{2,10},{3,11},{4,12},{5,13},{6,14},{7,15},{8,16},{9,17... | collective-permute-start | bytes 61448 | tf_op jit(solution)/shard_map/ppermute | solution.py:26
  33.6 0.8 collective-permute-done.5
  34.3 0.9 maximum_bitcast_fusion.rim
  35.2 3.5 %collective-permute-done.4 = bf16[6,6,32,128]{3,2,1,0:T(8,128)(2,1)} collective-permute-done((bf16[6,6,32,128]{3,2,1,0:T(8,128)(2,1)}, bf16[6,6,32,128]{3,2,1,0:T(8,128)(2,1)}, u32[]{:S(2)}, u32[]{:S(2)}) %collective-permute-start.4) | collective-permute-done | bytes 294944 | tf_op jit(solution)/shard_map/ppermute | solution.py:26
  38.8 3.4 %collective-permute-done.2 = bf16[6,6,32,128]{3,2,1,0:T(8,128)(2,1)} collective-permute-done((bf16[6,6,32,128]{3,2,1,0:T(8,128)(2,1)}, bf16[6,6,32,128]{3,2,1,0:T(8,128)(2,1)}, u32[]{:S(2)}, u32[]{:S(2)}) %collective-permute-start.2) | collective-permute-done | bytes 294944 | tf_op jit(solution)/shard_map/ppermute | solution.py:26
  42.2 1.4 %pad_maximum_fusion.2.own = bf16[4,6,6,32,128]{4,3,2,1,0:T(8,128)(2,1)S(1)} fusion(bf16[1,6,6,32,128]{4,3,2,1,0:T(8,128)(2,1)} %bitcast.23, bf16[1,6,6,32,128]{4,3,2,1,0:T(8,128)(2,1)} %bitcast.21, bf16[1,6,6,32,128]{4,3,2,1,0:T(8,128)(2,1)} %bitcast.19, bf16[1,6,6,32,128]{4,3,2,1,0:T(8,128)(2,1)S(1)} %copy-done.12), kind=kLoop, calls=%fused_computation.3 | loop fusion | flops 1769472 | bytes 2359296 | tf_op jit(solution)/shard_map/stack | solution.py:294
  43.5 2.5 %collective-permute-start.7 = (bf16[4,6,6,32,128]{4,3,2,1,0:T(8,128)(2,1)S(1)}, bf16[4,6,6,32,128]{4,3,2,1,0:T(8,128)(2,1)}, u32[]{:S(2)}, u32[]{:S(2)}) collective-permute-start(bf16[4,6,6,32,128]{4,3,2,1,0:T(8,128)(2,1)S(1)} %pad_maximum_fusion.2.own), channel_id=1, source_target_pairs={{0,16},{1,17},{2,18},{3,19},{4,20},{5,21},{6,22},{7,23},{8,24},{9,... | collective-permute-start | bytes 3538952 | tf_op jit(solution)/shard_map/ppermute | solution.py:26
  46.1 0.7 collective-permute-start.8
  46.7 1.2 collective-permute-start.9
  47.9 2.1 %collective-permute-start.10 = (bf16[9,3,32,512]{3,2,1,0:T(8,128)(2,1)S(1)}, bf16[9,3,32,512]{3,2,1,0:T(8,128)(2,1)S(1)}, u32[]{:S(2)}, u32[]{:S(2)}) collective-permute-start(bf16[9,3,32,512]{3,2,1,0:T(8,128)(2,1)S(1)} %bitcast.73), channel_id=1, source_target_pairs={{0,96},{1,97},{2,98},{3,99},{4,100},{5,101},{6,102},{7,103},{8,104... | collective-permute-start | bytes 2654216 | tf_op jit(solution)/shard_map/ppermute | solution.py:26
  50.0 11.5 %collapse.1 = bf16[3,2,2,2,2,4,4,32,256]{8,7,6,5,4,3,2,1,0:T(8,128)(2,1)} custom-call(bf16[3,3,3,4,4,32,256]{6,5,4,3,2,1,0:T(8,128)(2,1)} %bitcast.76), custom_call_target="tpu_custom_call" | custom-call | tf_op jit(solution)/shard_map/collapse/pallas_call | solution.py:144
  61.6 6.3 %conv_rim.1.rim = f32[2,2,2,4,32,256]{5,4,3,2,1,0:T(8,128)S(1)} custom-call(bf16[2,10,64,512]{3,2,1,0:T(8,128)(2,1)S(1)} %maximum_bitcast_fusion.rim, bf16[3,3,1536,256]{3,2,1,0:T(8,128)(2,1)} %bitcast.77), custom_call_target="tpu_custom_call" | custom-call | tf_op jit(solution)/shard_map/conv_rim/pallas_call | solution.py:181
  67.9 1.0 copy-done
  68.9 9.2 %collective-permute-done.9.w1 = bf16[9,3,32,512]{3,2,1,0:T(8,128)(2,1)S(1)} collective-permute-done((bf16[9,3,32,512]{3,2,1,0:T(8,128)(2,1)S(1)}, bf16[9,3,32,512]{3,2,1,0:T(8,128)(2,1)S(1)}, u32[]{:S(2)}, u32[]{:S(2)}) %collective-permute-start.9) | collective-permute-done | bytes 884768 | tf_op jit(solution)/shard_map/ppermute | solution.py:26
  78.1 0.9 copy-done.2
  79.0 1.0 copy-done.4
  79.9 0.8 copy-done.8
  80.7 0.1 reshape.93
  80.8 0.1 broadcast_in_dim.22
  80.9 0.1 reshape.97
  81.0 0.1 reshape.98
  81.1 0.1 reshape.99
  81.2 0.1 stack_reshape.7
  81.3 0.1 stack.102.place
  81.4 2.5 %collective-permute-done.13.other_swap = bf16[4,6,6,32,128]{4,3,2,1,0:T(8,128)(2,1)} collective-permute-done((bf16[4,6,6,32,128]{4,3,2,1,0:T(8,128)(2,1)}, bf16[4,6,6,32,128]{4,3,2,1,0:T(8,128)(2,1)}, u32[]{:S(2)}, u32[]{:S(2)}) %collective-permute-start.13) | collective-permute-done | bytes 1179680 | tf_op jit(solution)/shard_map/ppermute | solution.py:26
  84.0 1.2 copy-done.3
  85.2 1.2 copy-done.5
  86.3 1.0 copy-done.7
  87.3 1.0 copy-done.9
  88.3 11.8 %conv_in.1 = (bf16[4,4,4,32,128]{4,3,2,1,0:T(8,128)(2,1)S(1)}, f32[2,8,128]{2,1,0:T(8,128)S(1)}) custom-call(s32[4]{0:T(128)S(1)} %pad_add_fusion.place, bf16[4,6,6,32,128]{4,3,2,1,0:T(8,128)(2,1)S(1)} %pad_maximum_fusion.2.own, bf16[4,6,6,32,128]{4,3,2,1,0:T(8,128)(2,1)} %collective-permute-done.7.other, ...), custom_call_target="tpu_custom_call" | custom-call | flops 7200000000 | bytes 9000000 | tf_op jit(solution)/shard_map/conv_in/pallas_call | solution.py:101
  100.2 0.9 collective-permute-start.16
  101.1 2.5 %collective-permute-start.15 = (bf16[4,4,32,128]{3,2,0,1:T(8,128)(2,1)S(1)}, bf16[4,4,32,128]{3,2,0,1:T(8,128)(2,1)S(1)}, u32[]{:S(2)}, u32[]{:S(2)}) collective-permute-start(bf16[4,4,32,128]{3,2,0,1:T(8,128)(2,1)S(1)} %bitcast.88), channel_id=1, source_target_pairs={{0,16},{1,17},{2,18},{3,19},{4,20},{5,21},{6,22},{7,23},{8,24},{9,... | collective-permute-start | bytes 393224 | tf_op jit(solution)/shard_map/ppermute | solution.py:26
  103.7 0.2 collective-permute-start.14
  103.8 1.3 collective-permute-done.14
  105.1 0.1 slice_reduce_fusion.3
  105.2 0.1 reshape_squeeze.19
  105.3 0.7 broadcast_in_dim.24
  105.9 3.8 %all-to-all-start = ((f32[128,1,128]{2,1,0:T(1,128)}), f32[128,1,128]{2,1,0:T(1,128)S(1)}, u32[]{:S(2)}, u32[]{:S(2)}) async-start(f32[128,1,128]{2,1,0:T(1,128)} %broadcast_in_dim.24), calls=%async_computation | async-start | bytes 131072 | tf_op jit(solution)/shard_map/all_to_all | solution.py:326
  109.8 0.6 collective-permute-done.15
  110.5 2.8 %collective-permute-start.17 = (bf16[4,4,32,128]{3,2,1,0:T(8,128)(2,1)S(1)}, bf16[4,4,32,128]{3,2,1,0:T(8,128)(2,1)S(1)}, u32[]{:S(2)}, u32[]{:S(2)}) collective-permute-start(bf16[4,4,32,128]{3,2,1,0:T(8,128)(2,1)S(1)} %get-tuple-element.58), channel_id=1, source_target_pairs={{0,1},{1,2},{2,3},{3,4},{4,5},{5,6},{6,7},{8,9},{9,10},{10,11},{11... | collective-permute-start | bytes 393224 | tf_op jit(solution)/shard_map/ppermute | solution.py:26
  113.3 5.2 %collective-permute-start.18 = (bf16[4,4,32,128]{3,2,1,0:T(8,128)(2,1)S(1)}, bf16[4,4,32,128]{3,2,1,0:T(8,128)(2,1)S(1)}, u32[]{:S(2)}, u32[]{:S(2)}) collective-permute-start(bf16[4,4,32,128]{3,2,1,0:T(8,128)(2,1)S(1)} %get-tuple-element.57), channel_id=1, source_target_pairs={{1,0},{2,1},{3,2},{4,3},{5,4},{6,5},{7,6},{9,8},{10,9},{11,10},{12... | collective-permute-start | bytes 393224 | tf_op jit(solution)/shard_map/ppermute | solution.py:26
  118.5 0.1 all-to-all-done
  118.6 0.1 reshape.95
  118.8 0.1 stack_reshape.6
  119.1 0.6 collective-permute-done.17.up
  119.7 1.3 collective-permute-done.18.down
  121.0 8.7 %conv_out.1 = bf16[2,2,4,4,32,256]{5,4,3,2,1,0:T(8,128)(2,1)S(1)} custom-call(s32[5]{0:T(128)S(1)} %stack.102.place, bf16[4,4,4,32,128]{4,3,2,1,0:T(8,128)(2,1)S(1)} %copy.52.main, bf16[4,4,32,128]{3,2,1,0:T(8,128)(2,1)S(1)} %collective-permute-done.17.up, bf16[4,4,32,128]{3,2,1,0:T(8,128)(2,1)S(1)} %collective-permute-done.18.down, ...), custom_call_target="tpu_custom_call" | custom-call | flops 4899999744 | bytes 18000000 | tf_op jit(solution)/shard_map/conv_out/pallas_call | solution.py:247
  129.7 0.8 copy.53
  130.5 1.1 copy.54
  (79 shorter events, 1.5 us)
Async XLA Ops:
  0.0 2.9 %copy-start.13 = (bf16[480,6,4,32]{0,3,2,1:T(8,128)(2,1)S(1)}, bf16[480,6,4,32]{0,3,2,1:T(8,128)(2,1)}, u32[]{:S(2)}) copy-start(bf16[480,6,4,32]{0,3,2,1:T(8,128)(2,1)} %param.8) | copy-start | bytes 2211844
  3.2 11.7 %collective-permute-start.1 = (bf16[312,512]{1,0:T(8,128)(2,1)S(1)}, bf16[312,512]{1,0:T(8,128)(2,1)S(1)}, u32[]{:S(2)}, u32[]{:S(2)}) collective-permute-start(bf16[312,512]{1,0:T(8,128)(2,1)S(1)} %pad_maximum_fusion.5), channel_id=1, source_target_pairs={{1,0},{2,1},{3,2},{4,3},{5,4},{6,5},{7,6},{9,8},{10,9},{11,10},{12... | collective-permute-start | bytes 958472 | tf_op jit(solution)/shard_map/ppermute | solution.py:26
  8.2 13.0 %collective-permute-start = (bf16[312,512]{1,0:T(8,128)(2,1)S(1)}, bf16[312,512]{1,0:T(8,128)(2,1)S(1)}, u32[]{:S(2)}, u32[]{:S(2)}) collective-permute-start(bf16[312,512]{1,0:T(8,128)(2,1)S(1)} %pad_maximum_fusion.4), channel_id=1, source_target_pairs={{0,1},{1,2},{2,3},{3,4},{4,5},{5,6},{6,7},{8,9},{9,10},{10,11},{11... | collective-permute-start | bytes 958472 | tf_op jit(solution)/shard_map/ppermute | solution.py:26
  21.9 6.5 %copy-start.11 = (bf16[60,2,8,512]{3,2,1,0:T(8,128)(2,1)S(1)}, bf16[60,2,8,512]{3,2,1,0:T(8,128)(2,1)}, u32[]{:S(2)}) copy-start(bf16[60,2,8,512]{3,2,1,0:T(8,128)(2,1)} %param.13) | copy-start | bytes 2949124
  23.0 15.8 %collective-permute-start.4 = (bf16[6,6,32,128]{3,2,1,0:T(8,128)(2,1)}, bf16[6,6,32,128]{3,2,1,0:T(8,128)(2,1)}, u32[]{:S(2)}, u32[]{:S(2)}) collective-permute-start(bf16[6,6,32,128]{3,2,1,0:T(8,128)(2,1)} %get-tuple-element.48), channel_id=1, source_target_pairs={{0,96},{1,97},{2,98},{3,99},{4,100},{5,101},{6,102},{7,103},{8,104... | collective-permute-start | bytes 884744 | tf_op jit(solution)/shard_map/ppermute | solution.py:26
  27.0 11.8 %collective-permute-start.3 = (bf16[6,6,32,128]{3,2,1,0:T(8,128)(2,1)}, bf16[6,6,32,128]{3,2,1,0:T(8,128)(2,1)}, u32[]{:S(2)}, u32[]{:S(2)}) collective-permute-start(bf16[6,6,32,128]{3,2,1,0:T(8,128)(2,1)} %get-tuple-element.49), channel_id=1, source_target_pairs={{0,64},{1,65},{2,66},{3,67},{4,68},{5,69},{6,70},{7,71},{8,72},{9,... | collective-permute-start | bytes 884744 | tf_op jit(solution)/shard_map/ppermute | solution.py:26
  27.0 15.1 %collective-permute-start.2 = (bf16[6,6,32,128]{3,2,1,0:T(8,128)(2,1)}, bf16[6,6,32,128]{3,2,1,0:T(8,128)(2,1)}, u32[]{:S(2)}, u32[]{:S(2)}) collective-permute-start(bf16[6,6,32,128]{3,2,1,0:T(8,128)(2,1)} %get-tuple-element.50), channel_id=1, source_target_pairs={{0,32},{1,33},{2,34},{3,35},{4,36},{5,37},{6,38},{7,39},{8,40},{9,... | collective-permute-start | bytes 884744 | tf_op jit(solution)/shard_map/ppermute | solution.py:26
  29.1 4.4 %collective-permute-start.6 = (bf16[1,2,10,512]{3,0,2,1:T(2,128)(2,1)S(1)}, bf16[1,2,10,512]{3,0,2,1:T(2,128)(2,1)S(1)}, u32[]{:S(2)}, u32[]{:S(2)}) collective-permute-start(bf16[1,2,10,512]{3,0,2,1:T(2,128)(2,1)S(1)} %get-tuple-element.46), channel_id=1, source_target_pairs={{8,0},{9,1},{10,2},{11,3},{12,4},{13,5},{14,6},{15,7},{16,8},{17,9... | collective-permute-start | bytes 61448 | tf_op jit(solution)/shard_map/ppermute | solution.py:26
  30.4 3.9 %collective-permute-start.5 = (bf16[1,2,10,512]{3,0,2,1:T(2,128)(2,1)S(1)}, bf16[1,2,10,512]{3,0,2,1:T(2,128)(2,1)S(1)}, u32[]{:S(2)}, u32[]{:S(2)}) collective-permute-start(bf16[1,2,10,512]{3,0,2,1:T(2,128)(2,1)S(1)} %get-tuple-element.45), channel_id=1, source_target_pairs={{0,8},{1,9},{2,10},{3,11},{4,12},{5,13},{6,14},{7,15},{8,16},{9,17... | collective-permute-start | bytes 61448 | tf_op jit(solution)/shard_map/ppermute | solution.py:26
  33.5 8.6 %copy-start.12 = (bf16[1,6,6,32,128]{4,3,2,1,0:T(8,128)(2,1)S(1)}, bf16[1,6,6,32,128]{4,3,2,1,0:T(8,128)(2,1)}, u32[]{:S(2)}) copy-start(bf16[1,6,6,32,128]{4,3,2,1,0:T(8,128)(2,1)} %get-tuple-element.47) | copy-start | bytes 884740
  42.1 3.9 %copy-start.1 = (bf16[3,3,3,512,32]{3,4,2,1,0:T(8,128)(2,1)S(1)}, bf16[3,3,3,512,32]{3,4,2,1,0:T(8,128)(2,1)}, u32[]{:S(2)}) copy-start(bf16[3,3,3,512,32]{3,4,2,1,0:T(8,128)(2,1)} %param.9) | copy-start | bytes 2654212
  43.5 37.2 %collective-permute-start.7 = (bf16[4,6,6,32,128]{4,3,2,1,0:T(8,128)(2,1)S(1)}, bf16[4,6,6,32,128]{4,3,2,1,0:T(8,128)(2,1)}, u32[]{:S(2)}, u32[]{:S(2)}) collective-permute-start(bf16[4,6,6,32,128]{4,3,2,1,0:T(8,128)(2,1)S(1)} %pad_maximum_fusion.2.own), channel_id=1, source_target_pairs={{0,16},{1,17},{2,18},{3,19},{4,20},{5,21},{6,22},{7,23},{8,24},{9,... | collective-permute-start | bytes 3538952 | tf_op jit(solution)/shard_map/ppermute | solution.py:26
  46.1 15.4 %collective-permute-start.8 = (bf16[9,3,32,256]{3,2,1,0:T(8,128)(2,1)S(1)}, bf16[9,3,32,256]{3,2,1,0:T(8,128)(2,1)S(1)}, u32[]{:S(2)}, u32[]{:S(2)}) collective-permute-start(bf16[9,3,32,256]{3,2,1,0:T(8,128)(2,1)S(1)} %constant_dynamic-slice_fusion.5), channel_id=1, source_target_pairs={{0,64},{1,65},{2,66},{3,67},{4,68},{5,69},{6,70},{7,71},{8,72},{9,... | collective-permute-start | bytes 1327112 | tf_op jit(solution)/shard_map/ppermute | solution.py:26
  46.7 31.3 %collective-permute-start.9 = (bf16[9,3,32,512]{3,2,1,0:T(8,128)(2,1)S(1)}, bf16[9,3,32,512]{3,2,1,0:T(8,128)(2,1)S(1)}, u32[]{:S(2)}, u32[]{:S(2)}) collective-permute-start(bf16[9,3,32,512]{3,2,1,0:T(8,128)(2,1)S(1)} %bitcast.72), channel_id=1, source_target_pairs={{0,32},{1,33},{2,34},{3,35},{4,36},{5,37},{6,38},{7,39},{8,40},{9,... | collective-permute-start | bytes 2654216 | tf_op jit(solution)/shard_map/ppermute | solution.py:26
  47.9 31.1 %collective-permute-start.10 = (bf16[9,3,32,512]{3,2,1,0:T(8,128)(2,1)S(1)}, bf16[9,3,32,512]{3,2,1,0:T(8,128)(2,1)S(1)}, u32[]{:S(2)}, u32[]{:S(2)}) collective-permute-start(bf16[9,3,32,512]{3,2,1,0:T(8,128)(2,1)S(1)} %bitcast.73), channel_id=1, source_target_pairs={{0,96},{1,97},{2,98},{3,99},{4,100},{5,101},{6,102},{7,103},{8,104... | collective-permute-start | bytes 2654216 | tf_op jit(solution)/shard_map/ppermute | solution.py:26
  61.4 6.5 %copy-start.6 = (bf16[9,3,32,256]{3,2,1,0:T(8,128)(2,1)}, bf16[9,3,32,256]{3,2,1,0:T(8,128)(2,1)S(1)}, u32[]{:S(2)}) copy-start(bf16[9,3,32,256]{3,2,1,0:T(8,128)(2,1)S(1)} %collective-permute-done.8.near) | copy-start | bytes 1327108
  61.4 18.5 %collective-permute-start.11 = (bf16[9,3,32,256]{3,2,1,0:T(8,128)(2,1)S(1)}, bf16[9,3,32,256]{3,2,1,0:T(8,128)(2,1)S(1)}, u32[]{:S(2)}, u32[]{:S(2)}) collective-permute-start(bf16[9,3,32,256]{3,2,1,0:T(8,128)(2,1)S(1)} %collective-permute-done.8.near), channel_id=1, source_target_pairs={{0,1},{1,0},{2,3},{3,2},{4,5},{5,4},{6,7},{7,6},{8,9},{9,8},{10,11... | collective-permute-start | bytes 1327112 | tf_op jit(solution)/shard_map/ppermute | solution.py:26
  61.4 20.0 %collective-permute-start.12 = (bf16[4,6,6,32,128]{4,3,2,1,0:T(8,128)(2,1)S(1)}, bf16[4,6,6,32,128]{4,3,2,1,0:T(8,128)(2,1)}, u32[]{:S(2)}, u32[]{:S(2)}) collective-permute-start(bf16[4,6,6,32,128]{4,3,2,1,0:T(8,128)(2,1)S(1)} %pad_maximum_fusion.2.own), channel_id=1, source_target_pairs={{0,8},{1,9},{2,10},{3,11},{4,12},{5,13},{6,14},{7,15},{8,0},{9,1},... | collective-permute-start | bytes 3538952 | tf_op jit(solution)/shard_map/ppermute | solution.py:26
  61.5 19.2 %copy-start.14 = (f32[512]{0:T(512)S(1)}, f32[512]{0:T(512)}, u32[]{:S(2)}) copy-start(f32[512]{0:T(512)} %param.10) | copy-start | bytes 6148
  61.5 19.4 %copy-start.15 = (f32[512]{0:T(512)S(1)}, f32[512]{0:T(512)}, u32[]{:S(2)}) copy-start(f32[512]{0:T(512)} %param.11) | copy-start | bytes 6148
  61.5 19.6 %copy-start.16 = (f32[512]{0:T(512)S(1)}, f32[512]{0:T(512)}, u32[]{:S(2)}) copy-start(f32[512]{0:T(512)} %param.12) | copy-start | bytes 6148
  67.9 1.0 copy-start
  78.1 0.9 copy-start.2
  79.0 1.0 copy-start.4
  79.9 0.8 copy-start.8
  80.7 3.2 %collective-permute-start.13 = (bf16[4,6,6,32,128]{4,3,2,1,0:T(8,128)(2,1)}, bf16[4,6,6,32,128]{4,3,2,1,0:T(8,128)(2,1)}, u32[]{:S(2)}, u32[]{:S(2)}) collective-permute-start(bf16[4,6,6,32,128]{4,3,2,1,0:T(8,128)(2,1)} %collective-permute-done.7.other), channel_id=1, source_target_pairs={{0,8},{1,9},{2,10},{3,11},{4,12},{5,13},{6,14},{7,15},{8,0},{9,1},... | collective-permute-start | bytes 3538952 | tf_op jit(solution)/shard_map/ppermute | solution.py:26
  84.0 1.2 copy-start.3
  85.1 1.2 copy-start.5
  86.3 1.0 copy-start.7
  87.3 1.0 copy-start.9
  100.2 9.6 %collective-permute-start.16 = (bf16[4,4,32,128]{3,2,0,1:T(8,128)(2,1)S(1)}, bf16[4,4,32,128]{3,2,0,1:T(8,128)(2,1)S(1)}, u32[]{:S(2)}, u32[]{:S(2)}) collective-permute-start(bf16[4,4,32,128]{3,2,0,1:T(8,128)(2,1)S(1)} %bitcast.87), channel_id=1, source_target_pairs={{0,24},{1,25},{2,26},{3,27},{4,28},{5,29},{6,30},{7,31},{8,16},{9,... | collective-permute-start | bytes 393224 | tf_op jit(solution)/shard_map/ppermute | solution.py:26
  101.1 9.3 %collective-permute-start.15 = (bf16[4,4,32,128]{3,2,0,1:T(8,128)(2,1)S(1)}, bf16[4,4,32,128]{3,2,0,1:T(8,128)(2,1)S(1)}, u32[]{:S(2)}, u32[]{:S(2)}) collective-permute-start(bf16[4,4,32,128]{3,2,0,1:T(8,128)(2,1)S(1)} %bitcast.88), channel_id=1, source_target_pairs={{0,16},{1,17},{2,18},{3,19},{4,20},{5,21},{6,22},{7,23},{8,24},{9,... | collective-permute-start | bytes 393224 | tf_op jit(solution)/shard_map/ppermute | solution.py:26
  103.7 1.4 %collective-permute-start.14 = (bf16[4,4,32,128]{3,2,0,1:T(8,128)(2,1)S(1)}, bf16[4,4,32,128]{3,2,0,1:T(8,128)(2,1)S(1)}, u32[]{:S(2)}, u32[]{:S(2)}) collective-permute-start(bf16[4,4,32,128]{3,2,0,1:T(8,128)(2,1)S(1)} %bitcast.89), channel_id=1, source_target_pairs={{0,8},{1,9},{2,10},{3,11},{4,12},{5,13},{6,14},{7,15},{8,0},{9,1},... | collective-permute-start | bytes 393224 | tf_op jit(solution)/shard_map/ppermute | solution.py:26
  105.9 12.7 %all-to-all-start = ((f32[128,1,128]{2,1,0:T(1,128)}), f32[128,1,128]{2,1,0:T(1,128)S(1)}, u32[]{:S(2)}, u32[]{:S(2)}) async-start(f32[128,1,128]{2,1,0:T(1,128)} %broadcast_in_dim.24), calls=%async_computation | async-start | bytes 131072 | tf_op jit(solution)/shard_map/all_to_all | solution.py:326
  110.4 10.6 %copy-start.10 = (f32[256]{0:T(256)S(1)}, f32[256]{0:T(256)}, u32[]{:S(2)}) copy-start(f32[256]{0:T(256)} %param.15) | copy-start | bytes 3076
  110.5 9.2 %collective-permute-start.17 = (bf16[4,4,32,128]{3,2,1,0:T(8,128)(2,1)S(1)}, bf16[4,4,32,128]{3,2,1,0:T(8,128)(2,1)S(1)}, u32[]{:S(2)}, u32[]{:S(2)}) collective-permute-start(bf16[4,4,32,128]{3,2,1,0:T(8,128)(2,1)S(1)} %get-tuple-element.58), channel_id=1, source_target_pairs={{0,1},{1,2},{2,3},{3,4},{4,5},{5,6},{6,7},{8,9},{9,10},{10,11},{11... | collective-permute-start | bytes 393224 | tf_op jit(solution)/shard_map/ppermute | solution.py:26
  113.3 7.7 %collective-permute-start.18 = (bf16[4,4,32,128]{3,2,1,0:T(8,128)(2,1)S(1)}, bf16[4,4,32,128]{3,2,1,0:T(8,128)(2,1)S(1)}, u32[]{:S(2)}, u32[]{:S(2)}) collective-permute-start(bf16[4,4,32,128]{3,2,1,0:T(8,128)(2,1)S(1)} %get-tuple-element.57), channel_id=1, source_target_pairs={{1,0},{2,1},{3,2},{4,3},{5,4},{6,5},{7,6},{9,8},{10,9},{11,10},{12... | collective-permute-start | bytes 393224 | tf_op jit(solution)/shard_map/ppermute | solution.py:26

commit v2 on v1

v2 whole, which is shorter than its diff:
```python
import jax
import jax.numpy as jnp
from jax import lax
from jax.experimental import pallas as pl
from jax.experimental.pallas import tpu as pltpu
from jax.sharding import PartitionSpec as P

GROUPS = 32
BOTH = ("chan", "rows")
BF16 = jnp.bfloat16
F32 = jnp.float32


def device_perm(move):
    pairs = []
    for d in range(128):
        chan, row = divmod(d, 8)
        to = move(chan // 4, chan // 2 % 2, chan % 2, row)
        if to is not None:
            z, half, core, row = to
            pairs.append((d, ((z % 4) * 4 + half * 2 + core) * 8 + row))
    return pairs


def send(array, move):
    return lax.ppermute(array, BOTH, device_perm(move))


def to_row(step):
    return lambda z, half, core, row: (z, half, core, row + step) if 0 <= row + step < 8 else None


def to_chan(step):
    def move(z, half, core, row):
        chan = z * 4 + half * 2 + core + step
        return (chan // 4, chan // 2 % 2, chan % 2, row) if 0 <= chan < 16 else None

    return move


def conv_in_kernel(place, own, other, own_swap, other_swap, own_edge, other_edge, own_edge_swap, other_edge_swap,
                   w0, w1, w3, near, far, bias, strip0, strip1, strip2, strip3, stats,
                   x, w, acc, turned, moments, sems):
    z, half, core, odd = (place[i] for i in range(4))

    def fetch(i, source, target):
        return pltpu.make_async_copy(source, target, sems.at[i])

    groups = []
    for tap, frames in ((0, pl.ds(0, 1)), (1, pl.ds(1, 1)), (2, pl.ds(2, 1)), (None, pl.ds(3, 3))):
        group = []
        for source, ends, dh, owner in (
            (own, own_edge, 0, core), (other, other_edge, 1, core),
            (own_swap, own_edge_swap, 0, 1 - core), (other_swap, other_edge_swap, 1, 1 - core),
        ):
            block = (half + dh) % 2 * 2 + owner
            group.append((source.at[:, :, frames], x.at[:, 1:5, frames, block]))
            for side in range(2):
                group.append((ends.at[:, side, frames], x.at[:, 5 * side, frames, block]))
        if tap is not None:
            taps = pl.ds(3 * tap, 3)
            for dz, source in ((0, w0), (1, w1), (3, w3)):
                group.append((source.at[taps], w.at[taps, :, (z + 4 - dz) % 4]))
            for which, source in ((odd, near), (1 - odd, far)):
                columns = pl.ds(pl.multiple_of(which * 256, 256), 256)
                group.append((source.at[taps], w.at[taps, :, (z + 2) % 4, :, columns]))
        start = sum(len(g) for g in groups)
        groups.append([fetch(start + i, *pair) for i, pair in enumerate(group)])
    for group in groups:
        for copy in group:
            copy.start()
    moments[...] = jnp.zeros_like(moments)
    lane = lax.broadcasted_iota(jnp.int32, (128, 128), 1)
    inside = (lane >= 4) & (lane < 124)

    def frame_tap(t, g, a):
        summed = None
        for b in range(3):
            rhs = jnp.concatenate([x[:, b + g * 2 + h, t + a].reshape(512, 128) for h in range(2)], axis=1)
            lhs = w[a * 3 + b].reshape(384, 512)
            term = jnp.dot(lhs, rhs, preferred_element_type=F32)
            summed = term if summed is None else summed + term
        return summed

    def finish(t, g, summed):
        for h in range(2):
            part = summed[:, h * 128 : (h + 1) * 128]
            value = pltpu.roll(part[0:128], 1, 1) + part[128:256] + pltpu.roll(part[256:384], 127, 1)
            value = (value + bias[...]).astype(BF16).astype(F32)
            kept = jnp.where(inside, value, 0.0)
            moments[0] += kept
            moments[1] += kept * kept
            turned[...] = value.T
            for r, strip in enumerate((strip0, strip1, strip2, strip3)):
                strip[g * 2 + h, t] = turned[pl.ds(3 + 30 * ((half * 2 + core) ^ r), 32), :].astype(BF16)

    def frame(t, _):
        for g in range(2):
            finish(t, g, frame_tap(t, g, 0) + frame_tap(t, g, 1) + frame_tap(t, g, 2))
        return 0

    for a in range(3):
        for copy in groups[a]:
            copy.wait()
        for g in range(2):
            term = frame_tap(0, g, a)
            if a == 0:
                acc[g] = term
            elif a == 1:
                acc[g] += term
            else:
                finish(0, g, acc[g] + term)
    for copy in groups[3]:
        copy.wait()
    lax.fori_loop(1, 4, frame, 0)
    lane, group = (lax.broadcasted_iota(jnp.int32, (8, 128), i) for i in (1, 0))
    row = jnp.zeros((1, 128), F32)
    for i in range(2):
        grouped = jnp.sum(moments[i].reshape(8, 16, 128), axis=1)
        totals = jnp.sum(grouped, axis=1, keepdims=True)
        row += jnp.sum(jnp.where(lane == group + 8 * i, totals, 0.0), axis=0, keepdims=True)
    stats[...] = jnp.broadcast_to(row, (128, 128))


def conv_in(place, parts, weights, bias):
    return pl.pallas_call(
        conv_in_kernel,
        out_shape=[jax.ShapeDtypeStruct((4, 4, 32, 128), BF16)] * 4 + [jax.ShapeDtypeStruct((128, 128), F32)],
        in_specs=[pl.BlockSpec(memory_space=pltpu.SMEM)] + [pl.BlockSpec(memory_space=pl.ANY)] * 13
        + [pl.BlockSpec(memory_space=pltpu.VMEM)],
        out_specs=[pl.BlockSpec(memory_space=pltpu.VMEM)] * 5,
        scratch_shapes=[
            pltpu.VMEM((4, 6, 6, 4, 32, 128), BF16),
            pltpu.VMEM((9, 3, 4, 32, 512), BF16),
            pltpu.VMEM((2, 384, 256), F32),
            pltpu.VMEM((128, 128), F32),
            pltpu.VMEM((2, 128, 128), F32),
            pltpu.SemaphoreType.DMA((63,)),
        ],
        compiler_params=pltpu.CompilerParams(vmem_limit_bytes=56 * 1024 * 1024),
        cost_estimate=pl.CostEstimate(flops=7_200_000_000, bytes_accessed=9_000_000, transcendentals=0),
        name="conv_in",
    )(place, *parts, *weights, bias)


def collapse(taps, out):
    def pairs(t0, t1, t2):
        return ((t0, t1 + t2), (t0 + t1, t2))

    for z in range(4):
        for p in range(4):
            source = z * 128 + p * 32
            target = p * 128 + z * 32
            wide = [[taps[b, c, source : source + 32, :].astype(F32) for c in range(3)] for b in range(3)]
            by_col = [pairs(*row) for row in wide]
            for pw in range(2):
                for side in range(2):
                    by_row = pairs(by_col[0][pw][side], by_col[1][pw][side], by_col[2][pw][side])
                    for ph in range(2):
                        for j in range(2):
                            out[ph, j, pw, side * 512 + target : side * 512 + target + 32, :] = by_row[ph][j].astype(BF16)


def rim_kernel(rim, above, below, before, after, weight, out, w, wide, fine, sem):
    fetch = pltpu.make_async_copy(weight.at[0:2], w, sem)
    fetch.start()
    column = lax.broadcasted_iota(jnp.int32, (64, 512), 0)
    for t in range(2):
        for h in range(10):
            line = above[t] if h == 0 else below[t] if h == 9 else rim[t, h - 1]
            line = pltpu.roll(line.astype(F32), 1, 0)
            line = jnp.where(column == 0, before[t, h : h + 1].astype(F32), line)
            line = jnp.where(column == 61, after[t, h : h + 1].astype(F32), line)
            for s in range(3):
                moved = line if s == 0 else pltpu.roll(line, 64 - s, 0)
                wide[t, h, :, s * 512 : s * 512 + 512] = moved.astype(BF16)
    fetch.wait()
    for t in range(2):
        summed = None
        for a in range(2 - t):
            for b in range(3):
                lhs = wide[t + a, b : b + 8].reshape(512, 1536)
                term = jnp.dot(lhs, w[a, b], preferred_element_type=F32)
                summed = term if summed is None else summed + term
        for c in range(2):
            fine[...] = summed[:, c * 128 : c * 128 + 128].reshape(8, 64, 128)
            for r in range(8):
                for pw in range(2):
                    out[pw, r % 2, t, r // 2, :, c * 128 : c * 128 + 128] = fine[r, pl.ds(pw, 32, stride=2), :]


def conv_rim(rim, above, below, before, after, weight):
    return pl.pallas_call(
        rim_kernel,
        out_shape=jax.ShapeDtypeStruct((2, 2, 2, 4, 32, 256), F32),
        in_specs=[pl.BlockSpec(memory_space=pltpu.VMEM)] * 5 + [pl.BlockSpec(memory_space=pltpu.HBM)],
        out_specs=pl.BlockSpec(memory_space=pltpu.VMEM),
        scratch_shapes=[
            pltpu.VMEM((2, 3, 1536, 256), BF16),
            pltpu.VMEM((2, 10, 64, 1536), BF16),
            pltpu.VMEM((8, 64, 128), F32),
            pltpu.SemaphoreType.DMA,
        ],
        compiler_params=pltpu.CompilerParams(vmem_limit_bytes=50 * 1024 * 1024),
        cost_estimate=pl.CostEstimate(flops=0, bytes_accessed=0, transcendentals=0),
        name="conv_rim",
    )(rim, above, below, before, after, weight.reshape(3, 3, 1536, 256))


def conv_out_kernel(place, main, up, down, vectors, rim, bias, weight, out, n, acc, raw, w0, w1, w2, sems):
    fetches = [pltpu.make_async_copy(weight.at[tap], raw.at[tap], sems.at[tap]) for tap in range(3)]
    for fetch in fetches:
        fetch.start()
    own, left, right, top, bottom = (place[i] for i in range(5))
    row = lax.broadcasted_iota(jnp.int32, (32, 128), 0)
    keep_col = jnp.where(
        ((row == 0) & (left == 1)) | ((row == 31) & (right == 1)), 0.0, 1.0)
    keep = [keep_col] * 6
    keep[0] = keep_col * jnp.where(top == 1, 0.0, 1.0)
    keep[5] = keep_col * jnp.where(bottom == 1, 0.0, 1.0)

    def frame(t, _):
        for r in range(4):
            p = own ^ r
            vec = vectors[p]
            for h in range(6):
                raw = up[r, t] if h == 0 else down[r, t] if h == 5 else main[r, h - 1, t]
                v = (raw.astype(F32) - vec[0:1]) * vec[1:2] + vec[2:3]
                v = v / (1.0 + jnp.exp(-v)) * keep[h]
                for s in range(3):
                    moved = v if s == 0 else pltpu.roll(v, 32 - s, 0)
                    start = pl.multiple_of(s * 512 + p * 128, 128)
                    n[t, h, :, pl.ds(start, 128)] = moved.astype(BF16)
        return 0

    lax.fori_loop(0, 4, frame, 0)
    whole = jnp.broadcast_to(bias[...], (32, 256))
    for pw in range(2):
        for ph in range(2):
            for t in range(4):
                for h in range(4):
                    acc[pw, ph, t, h] = rim[pw, ph, t, h] + whole if t < 2 else whole

    def multiply(tap, w):
        frames = 2 + tap
        for ph in range(2):
            for j in range(2):
                for pw in range(2):
                    lhs = n[0:frames, ph + j : ph + j + 4, :, pw * 512 : pw * 512 + 1024]
                    term = jnp.dot(lhs.reshape(frames * 128, 1024), w[ph, j, pw], preferred_element_type=F32)
                    acc[pw, ph, 4 - frames : 4] += term.reshape(frames, 4, 32, 256)

    for fetch in fetches:
        fetch.wait()
    collapse(raw.at[2], w2)
    multiply(2, w2)
    collapse(raw.at[1], w1)
    multiply(1, w1)
    collapse(raw.at[0], w0)
    multiply(0, w0)
    out[...] = acc[...].astype(BF16)


def conv_out(place, main, up, down, vectors, rim, bias, weight):
    whole = pl.BlockSpec(memory_space=pltpu.VMEM)
    return pl.pallas_call(
        conv_out_kernel,
        out_shape=jax.ShapeDtypeStruct((2, 2, 4, 4, 32, 256), BF16),
        in_specs=[pl.BlockSpec(memory_space=pltpu.SMEM)] + [whole] * 6 + [pl.BlockSpec(memory_space=pltpu.HBM)],
        out_specs=whole,
        scratch_shapes=[
            pltpu.VMEM((4, 6, 32, 1536), BF16),
            pltpu.VMEM((2, 2, 4, 4, 32, 256), F32),
            pltpu.VMEM((3, 3, 3, 512, 256), BF16),
            pltpu.VMEM((2, 2, 2, 1024, 256), BF16),
            pltpu.VMEM((2, 2, 2, 1024, 256), BF16),
            pltpu.VMEM((2, 2, 2, 1024, 256), BF16),
            pltpu.SemaphoreType.DMA((3,)),
        ],
        compiler_params=pltpu.CompilerParams(vmem_limit_bytes=52 * 1024 * 1024),
        cost_estimate=pl.CostEstimate(flops=4_900_000_000, bytes_accessed=18_000_000, transcendentals=400_000),
        name="conv_out",
    )(place, main, up, down, vectors, rim, bias, weight)


def body(
    latents,
    conv_in_weight,
    conv_in_bias,
    norm_gain,
    norm_shift,
    hidden_rim,
    conv_out_weight,
    conv_out_bias,
):
    chan, row = lax.axis_index("chan"), lax.axis_index("rows")
    z, half, core = chan // 4, chan // 2 % 2, chan % 2
    strip = chan % 4
    flip_core = lambda z, half, core, row: (z, half, 1 - core, row)

    flip_half = lambda z, half, core, row: (z, 1 - half, core, row)
    along_z = lambda dz: lambda z, half, core, row: (z + dz, half, core, row)

    weights = conv_in_weight.swapaxes(3, 4).reshape(9, 3, 32, 512)
    zones = [[c, c + 4, c + 8, c + 12] for c in range(4)]

    def to_zones(array):
        pieces = jnp.stack([array[..., 120 * i : 120 * i + 128] for i in range(4)])
        return lax.all_to_all(pieces, "chan", split_axis=0, concat_axis=0, axis_index_groups=zones, tiled=True)

    padded = jnp.pad(latents.transpose(2, 1, 3, 0), ((0, 0), (0, 0), (0, 0), (4, 28)))
    own = to_zones(padded)
    rim = jnp.pad(hidden_rim, ((0, 4), (0, 0), (0, 0), (0, 0))).transpose(1, 2, 0, 3)
    edge_rows = lambda i, j: jnp.concatenate([padded[i].reshape(192, 512), rim[:, j].reshape(128, 512)])
    above, below = send(edge_rows(3, 7), to_row(1)), send(edge_rows(0, 0), to_row(-1))
    odd = row % 2
    near = send(lax.dynamic_slice_in_dim(weights, odd * 256, 256, axis=3), along_z(2))
    own, above, below, weights, near = lax.optimization_barrier((own, above, below, weights, near))

    other = send(own, flip_half)
    w1, w3 = send(weights, along_z(1)), send(weights, along_z(3))
    far = send(near, lambda z, half, core, row: (z, half, core, row ^ 1))
    own_edge = to_zones(jnp.stack([above[:192].reshape(6, 32, 512), below[:192].reshape(6, 32, 512)]))
    other_edge = send(own_edge, flip_half)
    rim_above, rim_below = above[192:].reshape(2, 64, 512), below[192:].reshape(2, 64, 512)
    column = lambda i: jnp.concatenate([rim_above[:, None, i], rim[:, :, i], rim_below[:, None, i]], axis=1)
    before, after = send(column(59), to_chan(1)), send(column(0), to_chan(-1))
    rim = conv_rim(rim, rim_above, rim_below, before, after, conv_out_weight)
    other, other_edge, w1, w3, far, rim = lax.optimization_barrier((other, other_edge, w1, w3, far, rim))
    parts = [own, other, send(own, flip_core), send(other, flip_core),
             own_edge, other_edge, send(own_edge, flip_core), send(other_edge, flip_core)]
    weights = [weights, w1, w3, near, far]

    by_owner = conv_in_bias.reshape(4, 4, 32)
    bias = lax.dynamic_index_in_dim(by_owner, strip, 1, keepdims=False).reshape(128, 1)
    place = jnp.stack([z, half, core, odd]).astype(jnp.int32)
    *strips, stats = conv_in(place, parts, weights, jnp.broadcast_to(bias, (128, 128)))

    parts = strips[:1] + [
        send(strips[r], lambda z, half, core, row: (z, half ^ (r // 2), core ^ (r % 2), row)) for r in range(1, 4)]
    stats, parts[1] = lax.optimization_barrier((stats, parts[1]))
    first = jnp.stack(parts)
    above, below = send(first[:, 3], to_row(1)), send(first[:, 0], to_row(-1))
    gathered = lax.all_to_all(stats, BOTH, split_axis=0, concat_axis=0, tiled=True)
    sums, squares = gathered.reshape(4, 4, 8, 128)[..., :16].sum(axis=(0, 2)).reshape(4, 2, 8).swapaxes(0, 1)
    counted = float(480 * 4 * 32 * 16)
    mean = sums / counted
    var = squares / counted - mean * mean
    inv = 1.0 / jnp.sqrt(var + 1e-06)
    by_place = lambda vector: vector.reshape(4, 4, 32).swapaxes(0, 1).reshape(4, 128)
    vectors = jnp.stack(
        [jnp.repeat(mean, 16, axis=1), jnp.repeat(inv, 16, axis=1) * by_place(norm_gain), by_place(norm_shift)]
        + [jnp.zeros((4, 128), F32)] * 5, axis=1)
    edges = jnp.stack([strip, chan == 0, chan == 15, row == 0, row == 7]).astype(jnp.int32)
    decoded = conv_out(edges, first, above, below, vectors, rim, conv_out_bias.reshape(1, 256),
                       conv_out_weight)
    return decoded.transpose(4, 0, 2, 3, 1, 5)[:30].reshape(60, 4, 8, 256)


def solution(mesh):
    return jax.shard_map(
        body,
        mesh=mesh,
        in_specs=(
            P(None, None, "rows", "chan"),
            P(None, None, None, None, "chan"),
            P(),
            P(),
            P(),
            P("chan", None, "rows", None),
            P(),
            P(),
        ),
        out_specs=P("chan", None, "rows", None),
        check_vma=False,
    )
```

time: 134 us -> 124 us (0.925)
  starting transfers between devices: 38.3 us -> 52.2 us
  Pallas kernels: 38.3 us -> 29.1 us
  local copies, waits for them, and re-layouts: 18.1 us -> 8.92 us
  waiting for transfers between devices: 33.6 us -> 27 us
  other arithmetic: 2.79 us -> 4.39 us
    all_to_all x1 -> x3, starting transfers between devices: 3.82 us -> 16.6 us  [the longest x2 8.76 us: to_zones(): lax.all_to_all(pieces, 'chan', split_axis=0, concat_axis=0, axis_index_gr...]
    ppermute x19, waiting for transfers between devices: 33.5 us -> 22 us  [send(): return lax.ppermute(array, BOTH, device_perm(move))]
    pallas_call x2 -> x1, Pallas kernels: 23.2 us -> 13.2 us  [conv_in(): pl.pallas_call(conv_in_kernel, out_shape=[jax.ShapeDtypeStruct((4, 4, 32,...]
    unnamed x37 -> x25, local copies, waits for them, and re-layouts: 8.64 us -> 2.38 us
    all_to_all x1 -> x3, waiting for transfers between devices: 0.11 us -> 5.02 us  [the longest x2 5.02 us: to_zones(): lax.all_to_all(pieces, 'chan', split_axis=0, concat_axis=0, axis_index_gr...]
    slice x7 -> x8, local copies, waits for them, and re-layouts: 3.08 us -> 0.5 us  [the longest x3 0.43 us: body(): rim[:, j].reshape(128, 512)]
  transfers between devices with their start and end apart: 20 -> 22, of which waited for: 13 -> 11; matrix products, arithmetic and copies ran while one was open for 3% -> 6% of each run, Pallas kernels for 14% -> 5%
where the time goes in v2:
time: 124 us; the launch traced here: 122 us
  starting transfers between devices  52.2 us (42%)
  Pallas kernels  29.1 us (23%)
  waiting for transfers between devices  27 us (22%)
  local copies, waits for them, and re-layouts  8.92 us (7%)
  other arithmetic  4.39 us (4%)
    ppermute x19, starting transfers between devices, send(): return lax.ppermute(array, BOTH, device_perm(move))  35.5 us
    ppermute x19, waiting for transfers between devices, send(): return lax.ppermute(array, BOTH, device_perm(move))  22 us
    pallas_call x1, Pallas kernels, conv_in(): pl.pallas_call(conv_in_kernel, out_shape=[jax.ShapeDtypeStruct((4, 4, 32,...  13.2 us
    pallas_call x1, Pallas kernels, conv_out(): pl.pallas_call(conv_out_kernel, out_shape=jax.ShapeDtypeStruct((2, 2, 4,...  9.59 us
    all_to_all x2, starting transfers between devices, to_zones(): lax.all_to_all(pieces, 'chan', split_axis=0, concat_axis=0, axis_index_gr...  8.76 us
    all_to_all x1, starting transfers between devices, body(): lax.all_to_all(stats, BOTH, split_axis=0, concat_axis=0, tiled=True)  7.85 us
    pallas_call x1, Pallas kernels, conv_rim(): pl.pallas_call(rim_kernel, out_shape=jax.ShapeDtypeStruct((2, 2, 2, 4, 32...  6.27 us
    all_to_all x2, waiting for transfers between devices, to_zones(): lax.all_to_all(pieces, 'chan', split_axis=0, concat_axis=0, axis_index_gr...  5.02 us
  transfers between devices with their start and end apart: 22, of which 11 were waited for; matrix products, arithmetic and copies ran while one was open for 6% of the time, Pallas kernels for 5%

profile of v2, /device:TPU:2, one launch (start us, length us, event | category | flops | bytes accessed | tf_op | source)
XLA Modules:
  0.0 121.9 jit_solution(4404880972607607199)
XLA Ops:
  0.0 1.3 %copy.32 = bf16[480,6,4,32]{0,3,1,2:T(8,128)(2,1)S(1)} copy(bf16[480,6,4,32]{0,3,2,1:T(8,128)(2,1)} %param.8) | data formatting | bytes 1474560 | tf_op args[0]
  1.3 0.3 fusion
  1.6 1.0 pad_maximum_fusion
  2.6 5.3 %all-to-all-start = ((bf16[4,4,6,32,128]{4,3,2,1,0:T(8,128)(2,1)}), bf16[4,4,6,32,128]{4,3,2,1,0:T(8,128)(2,1)S(1)}, u32[]{:S(2)}, u32[]{:S(2)}) async-start(bf16[4,4,6,32,128]{4,3,2,1,0:T(8,128)(2,1)} %pad_maximum_fusion), calls=%async_computation | async-start | bytes 1572864 | tf_op jit(solution)/shard_map/all_to_all | solution.py:309
  7.9 0.2 pad_slice_fusion
  8.1 0.1 pad_bitcast_fusion
  8.2 0.3 fusion.9
  8.6 0.8 pad_maximum_fusion.3
  9.3 3.5 %collective-permute-start = (bf16[320,512]{1,0:T(8,128)(2,1)}, bf16[320,512]{1,0:T(8,128)(2,1)S(1)}, u32[]{:S(2)}, u32[]{:S(2)}) collective-permute-start(bf16[320,512]{1,0:T(8,128)(2,1)} %pad_maximum_fusion.3), channel_id=1, source_target_pairs={{0,1},{1,2},{2,3},{3,4},{4,5},{5,6},{6,7},{8,9},{9,10},{10,11},{11... | collective-permute-start | bytes 983048 | tf_op jit(solution)/shard_map/ppermute | solution.py:26
  12.8 1.0 constant_dynamic-slice_fusion
  13.9 3.6 %collective-permute-start.2 = (bf16[9,3,32,256]{3,2,1,0:T(8,128)(2,1)S(1)}, bf16[9,3,32,256]{3,2,1,0:T(8,128)(2,1)S(1)}, u32[]{:S(2)}, u32[]{:S(2)}) collective-permute-start(bf16[9,3,32,256]{3,2,1,0:T(8,128)(2,1)S(1)} %constant_dynamic-slice_fusion), channel_id=1, source_target_pairs={{0,64},{1,65},{2,66},{3,67},{4,68},{5,69},{6,70},{7,71},{8,72},{9,... | collective-permute-start | bytes 1327112 | tf_op jit(solution)/shard_map/ppermute | solution.py:26
  17.5 4.5 %collective-permute-start.1 = (bf16[320,512]{1,0:T(8,128)(2,1)S(1)}, bf16[320,512]{1,0:T(8,128)(2,1)S(1)}, u32[]{:S(2)}, u32[]{:S(2)}) collective-permute-start(bf16[320,512]{1,0:T(8,128)(2,1)S(1)} %pad_maximum_fusion.4), channel_id=1, source_target_pairs={{1,0},{2,1},{3,2},{4,3},{5,4},{6,5},{7,6},{9,8},{10,9},{11,10},{12... | collective-permute-start | bytes 983048 | tf_op jit(solution)/shard_map/ppermute | solution.py:26
  22.0 0.7 collective-permute-done
  22.7 5.2 %collective-permute-done.1 = bf16[320,512]{1,0:T(8,128)(2,1)S(1)} collective-permute-done((bf16[320,512]{1,0:T(8,128)(2,1)S(1)}, bf16[320,512]{1,0:T(8,128)(2,1)S(1)}, u32[]{:S(2)}, u32[]{:S(2)}) %collective-permute-start.1) | collective-permute-done | bytes 327712 | tf_op jit(solution)/shard_map/ppermute | solution.py:26
  27.9 1.8 %collective-permute-done.2.near = bf16[9,3,32,256]{3,2,1,0:T(8,128)(2,1)S(1)} collective-permute-done((bf16[9,3,32,256]{3,2,1,0:T(8,128)(2,1)S(1)}, bf16[9,3,32,256]{3,2,1,0:T(8,128)(2,1)S(1)}, u32[]{:S(2)}, u32[]{:S(2)}) %collective-permute-start.2) | collective-permute-done | bytes 442400 | tf_op jit(solution)/shard_map/ppermute | solution.py:26
  29.7 0.6 collective-permute-start.5
  30.3 2.7 %collective-permute-start.6 = (bf16[9,3,32,512]{3,2,1,0:T(8,128)(2,1)}, bf16[9,3,32,512]{3,2,1,0:T(8,128)(2,1)}, u32[]{:S(2)}, u32[]{:S(2)}) collective-permute-start(bf16[9,3,32,512]{3,2,1,0:T(8,128)(2,1)} %bitcast.86), channel_id=1, source_target_pairs={{0,96},{1,97},{2,98},{3,99},{4,100},{5,101},{6,102},{7,103},{8,104... | collective-permute-start | bytes 2654216 | tf_op jit(solution)/shard_map/ppermute | solution.py:26
  33.0 2.2 %collective-permute-start.3 = (bf16[4,4,6,32,128]{4,3,2,1,0:T(8,128)(2,1)S(1)}, bf16[4,4,6,32,128]{4,3,2,1,0:T(8,128)(2,1)}, u32[]{:S(2)}, u32[]{:S(2)}) collective-permute-start(bf16[4,4,6,32,128]{4,3,2,1,0:T(8,128)(2,1)S(1)} %all-to-all-done.own), channel_id=1, source_target_pairs={{0,16},{1,17},{2,18},{3,19},{4,20},{5,21},{6,22},{7,23},{8,24},{9,... | collective-permute-start | bytes 2359304 | tf_op jit(solution)/shard_map/ppermute | solution.py:26
  35.2 0.1 fusion.5
  35.4 0.8 pad_maximum_fusion.2
  36.2 3.5 %all-to-all-start.1 = ((bf16[4,2,6,32,128]{4,3,2,1,0:T(8,128)(2,1)}), bf16[4,2,6,32,128]{4,3,2,1,0:T(8,128)(2,1)S(1)}, u32[]{:S(2)}, u32[]{:S(2)}) async-start(bf16[4,2,6,32,128]{4,3,2,1,0:T(8,128)(2,1)} %pad_maximum_fusion.2), calls=%async_computation.1 | async-start | bytes 786432 | tf_op jit(solution)/shard_map/all_to_all | solution.py:309
  39.7 1.7 %collective-permute-start.7 = (bf16[9,3,32,256]{3,2,1,0:T(8,128)(2,1)S(1)}, bf16[9,3,32,256]{3,2,1,0:T(8,128)(2,1)}, u32[]{:S(2)}, u32[]{:S(2)}) collective-permute-start(bf16[9,3,32,256]{3,2,1,0:T(8,128)(2,1)S(1)} %collective-permute-done.2.near), channel_id=1, source_target_pairs={{0,1},{1,0},{2,3},{3,2},{4,5},{5,4},{6,7},{7,6},{8,9},{9,8},{10,11... | collective-permute-start | bytes 1327112 | tf_op jit(solution)/shard_map/ppermute | solution.py:26
  41.4 1.3 %collective-permute-start.8 = (bf16[2,10,512]{2,1,0:T(8,128)(2,1)S(1)}, bf16[2,10,512]{2,1,0:T(8,128)(2,1)S(1)}, u32[]{:S(2)}, u32[]{:S(2)}) collective-permute-start(bf16[2,10,512]{2,1,0:T(8,128)(2,1)S(1)} %pad_maximum_fusion.6), channel_id=1, source_target_pairs={{0,8},{1,9},{2,10},{3,11},{4,12},{5,13},{6,14},{7,15},{8,16},{9,17... | collective-permute-start | bytes 61448 | tf_op jit(solution)/shard_map/ppermute | solution.py:26
  42.7 0.8 collective-permute-done.8.before
  43.5 1.3 %collective-permute-start.9 = (bf16[2,10,512]{2,1,0:T(8,128)(2,1)S(1)}, bf16[2,10,512]{2,1,0:T(8,128)(2,1)S(1)}, u32[]{:S(2)}, u32[]{:S(2)}) collective-permute-start(bf16[2,10,512]{2,1,0:T(8,128)(2,1)S(1)} %pad_maximum_fusion.7), channel_id=1, source_target_pairs={{8,0},{9,1},{10,2},{11,3},{12,4},{13,5},{14,6},{15,7},{16,8},{17,9... | collective-permute-start | bytes 61448 | tf_op jit(solution)/shard_map/ppermute | solution.py:26
  44.8 6.0 %collective-permute-done.9.after = bf16[2,10,512]{2,1,0:T(8,128)(2,1)S(1)} collective-permute-done((bf16[2,10,512]{2,1,0:T(8,128)(2,1)S(1)}, bf16[2,10,512]{2,1,0:T(8,128)(2,1)S(1)}, u32[]{:S(2)}, u32[]{:S(2)}) %collective-permute-start.9) | collective-permute-done | bytes 20512 | tf_op jit(solution)/shard_map/ppermute | solution.py:26
  50.8 5.0 %all-to-all-done.1.own_edge = bf16[4,2,6,32,128]{4,3,2,1,0:T(8,128)(2,1)S(1)} async-done(((bf16[4,2,6,32,128]{4,3,2,1,0:T(8,128)(2,1)}), bf16[4,2,6,32,128]{4,3,2,1,0:T(8,128)(2,1)S(1)}, u32[]{:S(2)}, u32[]{:S(2)}) %all-to-all-start.1) | async-done | bytes 393248 | tf_op jit(solution)/shard_map/all_to_all | solution.py:309
  55.8 1.9 %collective-permute-start.4 = (bf16[4,2,6,32,128]{4,3,2,1,0:T(8,128)(2,1)S(1)}, bf16[4,2,6,32,128]{4,3,2,1,0:T(8,128)(2,1)}, u32[]{:S(2)}, u32[]{:S(2)}) collective-permute-start(bf16[4,2,6,32,128]{4,3,2,1,0:T(8,128)(2,1)S(1)} %all-to-all-done.1.own_edge), channel_id=1, source_target_pairs={{0,16},{1,17},{2,18},{3,19},{4,20},{5,21},{6,22},{7,23},{8,24},{9,... | collective-permute-start | bytes 1179656 | tf_op jit(solution)/shard_map/ppermute | solution.py:26
  57.7 0.6 copy.24.rim
  58.3 6.3 %conv_rim.1.rim = f32[2,2,2,4,32,256]{5,4,3,2,1,0:T(8,128)S(1)} custom-call(bf16[2,8,64,512]{3,2,1,0:T(8,128)(2,1)S(1)} %copy.24.rim, bf16[2,64,512]{2,1,0:T(8,128)(2,1)S(1)} %bitcast.69, bf16[2,64,512]{2,1,0:T(8,128)(2,1)S(1)} %bitcast.71, bf16[2,10,512]{2,1,0:T(8,128)(2,1)S(1)} %collective-permute-done.8.before, ...), custom_call_target="tpu_custom_call" | custom-call | tf_op jit(solution)/shard_map/conv_rim/pallas_call | solution.py:193
  64.6 1.0 copy-done
  65.5 3.0 %collective-permute-done.4.other_edge = bf16[4,2,6,32,128]{4,3,2,1,0:T(8,128)(2,1)} collective-permute-done((bf16[4,2,6,32,128]{4,3,2,1,0:T(8,128)(2,1)S(1)}, bf16[4,2,6,32,128]{4,3,2,1,0:T(8,128)(2,1)}, u32[]{:S(2)}, u32[]{:S(2)}) %collective-permute-start.4) | collective-permute-done | bytes 393248 | tf_op jit(solution)/shard_map/ppermute | solution.py:26
  68.5 0.1 collective-permute-start.11
  68.6 0.5 collective-permute-start.12
  69.1 0.1 collective-permute-start.13
  69.2 0.1 reshape.70
  69.3 0.1 broadcast_in_dim.13
  69.4 0.6 pad_add_fusion.place
  70.0 1.8 %collective-permute-done.12.own_edge_swap = bf16[4,2,6,32,128]{4,3,2,1,0:T(8,128)(2,1)S(1)} collective-permute-done((bf16[4,2,6,32,128]{4,3,2,1,0:T(8,128)(2,1)S(1)}, bf16[4,2,6,32,128]{4,3,2,1,0:T(8,128)(2,1)S(1)}, u32[]{:S(2)}, u32[]{:S(2)}) %collective-permute-start.12) | collective-permute-done | bytes 393248 | tf_op jit(solution)/shard_map/ppermute | solution.py:26
  71.8 0.5 collective-permute-done.13.other_edge_swap
  72.4 0.8 broadcast_in_dim.14.bias
  73.2 0.1 copy-done.9
  73.3 13.2 %conv_in.1 = (bf16[4,4,32,128]{3,2,1,0:T(8,128)(2,1)}, bf16[4,4,32,128]{3,2,1,0:T(8,128)(2,1)}, bf16[4,4,32,128]{3,2,1,0:T(8,128)(2,1)}, bf16[4,4,32,128]{3,2,1,0:T(8,128)(2,1)}, f32[128,128]{1,0:T(8,128)}) custom-call(s32[4]{0:T(128)} %pad_add_fusion.place, bf16[4,4,6,32,128]{4,3,2,1,0:T(8,128)(2,1)} %copy-done.3, ...), custom_call_target="tpu_custom_call" | custom-call | flops 7200000000 | bytes 9000000 | tf_op jit(solution)/shard_map/conv_in/pallas_call | solution.py:126
  86.5 0.2 collective-permute-start.14
  86.8 2.0 %collective-permute-start.16 = (bf16[4,4,32,128]{3,2,1,0:T(8,128)(2,1)}, bf16[4,4,32,128]{3,2,1,0:T(8,128)(2,1)S(1)}, u32[]{:S(2)}, u32[]{:S(2)}) collective-permute-start(bf16[4,4,32,128]{3,2,1,0:T(8,128)(2,1)} %get-tuple-element.38), channel_id=1, source_target_pairs={{0,24},{1,25},{2,26},{3,27},{4,28},{5,29},{6,30},{7,31},{8,16},{9,... | collective-permute-start | bytes 393224 | tf_op jit(solution)/shard_map/ppermute | solution.py:26
  88.8 1.5 %collective-permute-start.15 = (bf16[4,4,32,128]{3,2,1,0:T(8,128)(2,1)}, bf16[4,4,32,128]{3,2,1,0:T(8,128)(2,1)S(1)}, u32[]{:S(2)}, u32[]{:S(2)}) collective-permute-start(bf16[4,4,32,128]{3,2,1,0:T(8,128)(2,1)} %get-tuple-element.37), channel_id=1, source_target_pairs={{0,16},{1,17},{2,18},{3,19},{4,20},{5,21},{6,22},{7,23},{8,24},{9,... | collective-permute-start | bytes 393224 | tf_op jit(solution)/shard_map/ppermute | solution.py:26
  90.3 0.1 reshape.74
  90.4 0.1 reshape.75
  90.4 0.1 reshape.76
  90.5 0.1 stack_reshape.15
  90.6 0.1 stack.109.place
  90.7 7.9 %all-to-all-start.2 = ((f32[128,1,128]{2,1,0:T(1,128)}), f32[128,1,128]{2,1,0:T(1,128)S(1)}, u32[]{:S(2)}, u32[]{:S(2)}) async-start(f32[128,1,128]{2,1,0:T(1,128)} %bitcast.92), calls=%async_computation.2 | async-start | bytes 131072 | tf_op jit(solution)/shard_map/all_to_all | solution.py:344
  98.6 1.0 pad_maximum_fusion.1
  99.6 3.4 %collective-permute-start.17 = (bf16[4,4,32,128]{3,2,1,0:T(8,128)(2,1)S(1)}, bf16[4,4,32,128]{3,2,1,0:T(8,128)(2,1)S(1)}, u32[]{:S(2)}, u32[]{:S(2)}) collective-permute-start(bf16[4,4,32,128]{3,2,1,0:T(8,128)(2,1)S(1)} %get-tuple-element.52), channel_id=1, source_target_pairs={{0,1},{1,2},{2,3},{3,4},{4,5},{5,6},{6,7},{8,9},{9,10},{10,11},{11... | collective-permute-start | bytes 393224 | tf_op jit(solution)/shard_map/ppermute | solution.py:26
  103.0 4.6 %collective-permute-start.18 = (bf16[4,4,32,128]{3,2,1,0:T(8,128)(2,1)S(1)}, bf16[4,4,32,128]{3,2,1,0:T(8,128)(2,1)S(1)}, u32[]{:S(2)}, u32[]{:S(2)}) collective-permute-start(bf16[4,4,32,128]{3,2,1,0:T(8,128)(2,1)S(1)} %get-tuple-element.51), channel_id=1, source_target_pairs={{1,0},{2,1},{3,2},{4,3},{5,4},{6,5},{7,6},{9,8},{10,9},{11,10},{12... | collective-permute-start | bytes 393224 | tf_op jit(solution)/shard_map/ppermute | solution.py:26
  107.6 0.1 reshape.72
  107.8 0.1 stack_reshape.14
  107.9 0.1 broadcast_in_dim.16
  108.0 0.1 reshape.73
  108.1 1.1 collective-permute-done.17.up
  109.2 1.2 collective-permute-done.18.down
  110.4 9.6 %conv_out.1 = bf16[2,2,4,4,32,256]{5,4,3,2,1,0:T(8,128)(2,1)S(1)} custom-call(s32[5]{0:T(128)S(1)} %stack.109.place, bf16[4,4,4,32,128]{4,3,2,1,0:T(8,128)(2,1)S(1)} %copy.28.main, bf16[4,4,32,128]{3,2,1,0:T(8,128)(2,1)S(1)} %collective-permute-done.17.up, bf16[4,4,32,128]{3,2,1,0:T(8,128)(2,1)S(1)} %collective-permute-done.18.down, ...), custom_call_target="tpu_custom_call" | custom-call | flops 4899999744 | bytes 18000000 | tf_op jit(solution)/shard_map/conv_out/pallas_call | solution.py:266
  120.0 0.8 copy.29
  120.7 1.1 copy.30
  (58 shorter events, 0.5 us)
Async XLA Ops:
  0.0 8.1 %copy-start.2 = (bf16[60,2,8,512]{3,2,1,0:T(8,128)(2,1)S(1)}, bf16[60,2,8,512]{3,2,1,0:T(8,128)(2,1)}, u32[]{:S(2)}) copy-start(bf16[60,2,8,512]{3,2,1,0:T(8,128)(2,1)} %param.13) | copy-start | bytes 2949124
  2.6 27.1 %all-to-all-start = ((bf16[4,4,6,32,128]{4,3,2,1,0:T(8,128)(2,1)}), bf16[4,4,6,32,128]{4,3,2,1,0:T(8,128)(2,1)S(1)}, u32[]{:S(2)}, u32[]{:S(2)}) async-start(bf16[4,4,6,32,128]{4,3,2,1,0:T(8,128)(2,1)} %pad_maximum_fusion), calls=%async_computation | async-start | bytes 1572864 | tf_op jit(solution)/shard_map/all_to_all | solution.py:309
  9.3 13.4 %collective-permute-start = (bf16[320,512]{1,0:T(8,128)(2,1)}, bf16[320,512]{1,0:T(8,128)(2,1)S(1)}, u32[]{:S(2)}, u32[]{:S(2)}) collective-permute-start(bf16[320,512]{1,0:T(8,128)(2,1)} %pad_maximum_fusion.3), channel_id=1, source_target_pairs={{0,1},{1,2},{2,3},{3,4},{4,5},{5,6},{6,7},{8,9},{9,10},{10,11},{11... | collective-permute-start | bytes 983048 | tf_op jit(solution)/shard_map/ppermute | solution.py:26
  13.9 15.8 %collective-permute-start.2 = (bf16[9,3,32,256]{3,2,1,0:T(8,128)(2,1)S(1)}, bf16[9,3,32,256]{3,2,1,0:T(8,128)(2,1)S(1)}, u32[]{:S(2)}, u32[]{:S(2)}) collective-permute-start(bf16[9,3,32,256]{3,2,1,0:T(8,128)(2,1)S(1)} %constant_dynamic-slice_fusion), channel_id=1, source_target_pairs={{0,64},{1,65},{2,66},{3,67},{4,68},{5,69},{6,70},{7,71},{8,72},{9,... | collective-permute-start | bytes 1327112 | tf_op jit(solution)/shard_map/ppermute | solution.py:26
  17.5 10.3 %collective-permute-start.1 = (bf16[320,512]{1,0:T(8,128)(2,1)S(1)}, bf16[320,512]{1,0:T(8,128)(2,1)S(1)}, u32[]{:S(2)}, u32[]{:S(2)}) collective-permute-start(bf16[320,512]{1,0:T(8,128)(2,1)S(1)} %pad_maximum_fusion.4), channel_id=1, source_target_pairs={{1,0},{2,1},{3,2},{4,3},{5,4},{6,5},{7,6},{9,8},{10,9},{11,10},{12... | collective-permute-start | bytes 983048 | tf_op jit(solution)/shard_map/ppermute | solution.py:26
  29.7 34.9 %copy-start.10 = (bf16[9,3,32,256]{3,2,1,0:T(8,128)(2,1)}, bf16[9,3,32,256]{3,2,1,0:T(8,128)(2,1)S(1)}, u32[]{:S(2)}) copy-start(bf16[9,3,32,256]{3,2,1,0:T(8,128)(2,1)S(1)} %collective-permute-done.2.near) | copy-start | bytes 1327108
  29.7 35.9 %copy-start.3 = (bf16[4,4,6,32,128]{4,3,2,1,0:T(8,128)(2,1)}, bf16[4,4,6,32,128]{4,3,2,1,0:T(8,128)(2,1)S(1)}, u32[]{:S(2)}) copy-start(bf16[4,4,6,32,128]{4,3,2,1,0:T(8,128)(2,1)S(1)} %all-to-all-done.own) | copy-start | bytes 2359300
  29.7 38.9 %collective-permute-start.5 = (bf16[9,3,32,512]{3,2,1,0:T(8,128)(2,1)}, bf16[9,3,32,512]{3,2,1,0:T(8,128)(2,1)}, u32[]{:S(2)}, u32[]{:S(2)}) collective-permute-start(bf16[9,3,32,512]{3,2,1,0:T(8,128)(2,1)} %bitcast.85), channel_id=1, source_target_pairs={{0,32},{1,33},{2,34},{3,35},{4,36},{5,37},{6,38},{7,39},{8,40},{9,... | collective-permute-start | bytes 2654216 | tf_op jit(solution)/shard_map/ppermute | solution.py:26
  30.3 38.2 %collective-permute-start.6 = (bf16[9,3,32,512]{3,2,1,0:T(8,128)(2,1)}, bf16[9,3,32,512]{3,2,1,0:T(8,128)(2,1)}, u32[]{:S(2)}, u32[]{:S(2)}) collective-permute-start(bf16[9,3,32,512]{3,2,1,0:T(8,128)(2,1)} %bitcast.86), channel_id=1, source_target_pairs={{0,96},{1,97},{2,98},{3,99},{4,100},{5,101},{6,102},{7,103},{8,104... | collective-permute-start | bytes 2654216 | tf_op jit(solution)/shard_map/ppermute | solution.py:26
  33.0 35.5 %collective-permute-start.3 = (bf16[4,4,6,32,128]{4,3,2,1,0:T(8,128)(2,1)S(1)}, bf16[4,4,6,32,128]{4,3,2,1,0:T(8,128)(2,1)}, u32[]{:S(2)}, u32[]{:S(2)}) collective-permute-start(bf16[4,4,6,32,128]{4,3,2,1,0:T(8,128)(2,1)S(1)} %all-to-all-done.own), channel_id=1, source_target_pairs={{0,16},{1,17},{2,18},{3,19},{4,20},{5,21},{6,22},{7,23},{8,24},{9,... | collective-permute-start | bytes 2359304 | tf_op jit(solution)/shard_map/ppermute | solution.py:26
  35.2 34.0 %copy-start.5 = (f32[512]{0:T(512)S(1)}, f32[512]{0:T(512)}, u32[]{:S(2)}) copy-start(f32[512]{0:T(512)} %param.10) | copy-start | bytes 6148
  36.2 19.6 %all-to-all-start.1 = ((bf16[4,2,6,32,128]{4,3,2,1,0:T(8,128)(2,1)}), bf16[4,2,6,32,128]{4,3,2,1,0:T(8,128)(2,1)S(1)}, u32[]{:S(2)}, u32[]{:S(2)}) async-start(bf16[4,2,6,32,128]{4,3,2,1,0:T(8,128)(2,1)} %pad_maximum_fusion.2), calls=%async_computation.1 | async-start | bytes 786432 | tf_op jit(solution)/shard_map/all_to_all | solution.py:309
  39.7 25.9 %collective-permute-start.7 = (bf16[9,3,32,256]{3,2,1,0:T(8,128)(2,1)S(1)}, bf16[9,3,32,256]{3,2,1,0:T(8,128)(2,1)}, u32[]{:S(2)}, u32[]{:S(2)}) collective-permute-start(bf16[9,3,32,256]{3,2,1,0:T(8,128)(2,1)S(1)} %collective-permute-done.2.near), channel_id=1, source_target_pairs={{0,1},{1,0},{2,3},{3,2},{4,5},{5,4},{6,7},{7,6},{8,9},{9,8},{10,11... | collective-permute-start | bytes 1327112 | tf_op jit(solution)/shard_map/ppermute | solution.py:26
  41.4 2.1 %collective-permute-start.8 = (bf16[2,10,512]{2,1,0:T(8,128)(2,1)S(1)}, bf16[2,10,512]{2,1,0:T(8,128)(2,1)S(1)}, u32[]{:S(2)}, u32[]{:S(2)}) collective-permute-start(bf16[2,10,512]{2,1,0:T(8,128)(2,1)S(1)} %pad_maximum_fusion.6), channel_id=1, source_target_pairs={{0,8},{1,9},{2,10},{3,11},{4,12},{5,13},{6,14},{7,15},{8,16},{9,17... | collective-permute-start | bytes 61448 | tf_op jit(solution)/shard_map/ppermute | solution.py:26
  43.5 7.2 %collective-permute-start.9 = (bf16[2,10,512]{2,1,0:T(8,128)(2,1)S(1)}, bf16[2,10,512]{2,1,0:T(8,128)(2,1)S(1)}, u32[]{:S(2)}, u32[]{:S(2)}) collective-permute-start(bf16[2,10,512]{2,1,0:T(8,128)(2,1)S(1)} %pad_maximum_fusion.7), channel_id=1, source_target_pairs={{8,0},{9,1},{10,2},{11,3},{12,4},{13,5},{14,6},{15,7},{16,8},{17,9... | collective-permute-start | bytes 61448 | tf_op jit(solution)/shard_map/ppermute | solution.py:26
  55.8 17.4 %copy-start.4 = (bf16[4,2,6,32,128]{4,3,2,1,0:T(8,128)(2,1)}, bf16[4,2,6,32,128]{4,3,2,1,0:T(8,128)(2,1)S(1)}, u32[]{:S(2)}) copy-start(bf16[4,2,6,32,128]{4,3,2,1,0:T(8,128)(2,1)S(1)} %all-to-all-done.1.own_edge) | copy-start | bytes 1179652
  55.8 12.7 %collective-permute-start.4 = (bf16[4,2,6,32,128]{4,3,2,1,0:T(8,128)(2,1)S(1)}, bf16[4,2,6,32,128]{4,3,2,1,0:T(8,128)(2,1)}, u32[]{:S(2)}, u32[]{:S(2)}) collective-permute-start(bf16[4,2,6,32,128]{4,3,2,1,0:T(8,128)(2,1)S(1)} %all-to-all-done.1.own_edge), channel_id=1, source_target_pairs={{0,16},{1,17},{2,18},{3,19},{4,20},{5,21},{6,22},{7,23},{8,24},{9,... | collective-permute-start | bytes 1179656 | tf_op jit(solution)/shard_map/ppermute | solution.py:26
  64.5 1.0 copy-start
  65.5 6.3 %collective-permute-start.10 = (bf16[4,4,6,32,128]{4,3,2,1,0:T(8,128)(2,1)S(1)}, bf16[4,4,6,32,128]{4,3,2,1,0:T(8,128)(2,1)S(1)}, u32[]{:S(2)}, u32[]{:S(2)}) collective-permute-start(bf16[4,4,6,32,128]{4,3,2,1,0:T(8,128)(2,1)S(1)} %all-to-all-done.own), channel_id=1, source_target_pairs={{0,8},{1,9},{2,10},{3,11},{4,12},{5,13},{6,14},{7,15},{8,0},{9,1},... | collective-permute-start | bytes 2359304 | tf_op jit(solution)/shard_map/ppermute | solution.py:26
  68.5 3.8 %collective-permute-start.11 = (bf16[4,4,6,32,128]{4,3,2,1,0:T(8,128)(2,1)}, bf16[4,4,6,32,128]{4,3,2,1,0:T(8,128)(2,1)S(1)}, u32[]{:S(2)}, u32[]{:S(2)}) collective-permute-start(bf16[4,4,6,32,128]{4,3,2,1,0:T(8,128)(2,1)} %collective-permute-done.3.other), channel_id=1, source_target_pairs={{0,8},{1,9},{2,10},{3,11},{4,12},{5,13},{6,14},{7,15},{8,0},{9,1},... | collective-permute-start | bytes 2359304 | tf_op jit(solution)/shard_map/ppermute | solution.py:26
  68.6 3.2 %collective-permute-start.12 = (bf16[4,2,6,32,128]{4,3,2,1,0:T(8,128)(2,1)S(1)}, bf16[4,2,6,32,128]{4,3,2,1,0:T(8,128)(2,1)S(1)}, u32[]{:S(2)}, u32[]{:S(2)}) collective-permute-start(bf16[4,2,6,32,128]{4,3,2,1,0:T(8,128)(2,1)S(1)} %all-to-all-done.1.own_edge), channel_id=1, source_target_pairs={{0,8},{1,9},{2,10},{3,11},{4,12},{5,13},{6,14},{7,15},{8,0},{9,1},... | collective-permute-start | bytes 1179656 | tf_op jit(solution)/shard_map/ppermute | solution.py:26
  69.1 3.2 %collective-permute-start.13 = (bf16[4,2,6,32,128]{4,3,2,1,0:T(8,128)(2,1)}, bf16[4,2,6,32,128]{4,3,2,1,0:T(8,128)(2,1)}, u32[]{:S(2)}, u32[]{:S(2)}) collective-permute-start(bf16[4,2,6,32,128]{4,3,2,1,0:T(8,128)(2,1)} %collective-permute-done.4.other_edge), channel_id=1, source_target_pairs={{0,8},{1,9},{2,10},{3,11},{4,12},{5,13},{6,14},{7,15},{8,0},{9,1},... | collective-permute-start | bytes 1179656 | tf_op jit(solution)/shard_map/ppermute | solution.py:26
  71.8 1.4 %copy-start.11 = (bf16[4,2,6,32,128]{4,3,2,1,0:T(8,128)(2,1)}, bf16[4,2,6,32,128]{4,3,2,1,0:T(8,128)(2,1)S(1)}, u32[]{:S(2)}) copy-start(bf16[4,2,6,32,128]{4,3,2,1,0:T(8,128)(2,1)S(1)} %collective-permute-done.12.own_edge_swap) | copy-start | bytes 1179652
  71.8 1.4 %copy-start.8 = (bf16[4,4,6,32,128]{4,3,2,1,0:T(8,128)(2,1)}, bf16[4,4,6,32,128]{4,3,2,1,0:T(8,128)(2,1)S(1)}, u32[]{:S(2)}) copy-start(bf16[4,4,6,32,128]{4,3,2,1,0:T(8,128)(2,1)S(1)} %collective-permute-done.10.own_swap) | copy-start | bytes 2359300
  72.4 0.9 copy-start.9
  73.3 17.0 %copy-start.6 = (f32[512]{0:T(512)S(1)}, f32[512]{0:T(512)}, u32[]{:S(2)}) copy-start(f32[512]{0:T(512)} %param.11) | copy-start | bytes 6148
  73.3 17.1 %copy-start.7 = (f32[512]{0:T(512)S(1)}, f32[512]{0:T(512)}, u32[]{:S(2)}) copy-start(f32[512]{0:T(512)} %param.12) | copy-start | bytes 6148
  73.3 37.1 %copy-start.1 = (f32[256]{0:T(256)S(1)}, f32[256]{0:T(256)}, u32[]{:S(2)}) copy-start(f32[256]{0:T(256)} %param.15) | copy-start | bytes 3076
  86.5 4.2 %collective-permute-start.14 = (bf16[4,4,32,128]{3,2,1,0:T(8,128)(2,1)}, bf16[4,4,32,128]{3,2,1,0:T(8,128)(2,1)S(1)}, u32[]{:S(2)}, u32[]{:S(2)}) collective-permute-start(bf16[4,4,32,128]{3,2,1,0:T(8,128)(2,1)} %get-tuple-element.35), channel_id=1, source_target_pairs={{0,8},{1,9},{2,10},{3,11},{4,12},{5,13},{6,14},{7,15},{8,0},{9,1},... | collective-permute-start | bytes 393224 | tf_op jit(solution)/shard_map/ppermute | solution.py:26
  86.8 11.8 %collective-permute-start.16 = (bf16[4,4,32,128]{3,2,1,0:T(8,128)(2,1)}, bf16[4,4,32,128]{3,2,1,0:T(8,128)(2,1)S(1)}, u32[]{:S(2)}, u32[]{:S(2)}) collective-permute-start(bf16[4,4,32,128]{3,2,1,0:T(8,128)(2,1)} %get-tuple-element.38), channel_id=1, source_target_pairs={{0,24},{1,25},{2,26},{3,27},{4,28},{5,29},{6,30},{7,31},{8,16},{9,... | collective-permute-start | bytes 393224 | tf_op jit(solution)/shard_map/ppermute | solution.py:26
  88.8 9.8 %collective-permute-start.15 = (bf16[4,4,32,128]{3,2,1,0:T(8,128)(2,1)}, bf16[4,4,32,128]{3,2,1,0:T(8,128)(2,1)S(1)}, u32[]{:S(2)}, u32[]{:S(2)}) collective-permute-start(bf16[4,4,32,128]{3,2,1,0:T(8,128)(2,1)} %get-tuple-element.37), channel_id=1, source_target_pairs={{0,16},{1,17},{2,18},{3,19},{4,20},{5,21},{6,22},{7,23},{8,24},{9,... | collective-permute-start | bytes 393224 | tf_op jit(solution)/shard_map/ppermute | solution.py:26
  90.7 16.9 %all-to-all-start.2 = ((f32[128,1,128]{2,1,0:T(1,128)}), f32[128,1,128]{2,1,0:T(1,128)S(1)}, u32[]{:S(2)}, u32[]{:S(2)}) async-start(f32[128,1,128]{2,1,0:T(1,128)} %bitcast.92), calls=%async_computation.2 | async-start | bytes 131072 | tf_op jit(solution)/shard_map/all_to_all | solution.py:344
  99.6 9.6 %collective-permute-start.17 = (bf16[4,4,32,128]{3,2,1,0:T(8,128)(2,1)S(1)}, bf16[4,4,32,128]{3,2,1,0:T(8,128)(2,1)S(1)}, u32[]{:S(2)}, u32[]{:S(2)}) collective-permute-start(bf16[4,4,32,128]{3,2,1,0:T(8,128)(2,1)S(1)} %get-tuple-element.52), channel_id=1, source_target_pairs={{0,1},{1,2},{2,3},{3,4},{4,5},{5,6},{6,7},{8,9},{9,10},{10,11},{11... | collective-permute-start | bytes 393224 | tf_op jit(solution)/shard_map/ppermute | solution.py:26
  103.0 7.4 %collective-permute-start.18 = (bf16[4,4,32,128]{3,2,1,0:T(8,128)(2,1)S(1)}, bf16[4,4,32,128]{3,2,1,0:T(8,128)(2,1)S(1)}, u32[]{:S(2)}, u32[]{:S(2)}) collective-permute-start(bf16[4,4,32,128]{3,2,1,0:T(8,128)(2,1)S(1)} %get-tuple-element.51), channel_id=1, source_target_pairs={{1,0},{2,1},{3,2},{4,3},{5,4},{6,5},{7,6},{9,8},{10,9},{11,10},{12... | collective-permute-start | bytes 393224 | tf_op jit(solution)/shard_map/ppermute | solution.py:26

commit v3 on v2

--- a/solution.py
+++ b/solution.py
@@ -202,7 +202,7 @@
             pltpu.SemaphoreType.DMA,
         ],
         compiler_params=pltpu.CompilerParams(vmem_limit_bytes=50 * 1024 * 1024),
-        cost_estimate=pl.CostEstimate(flops=0, bytes_accessed=0, transcendentals=0),
+        cost_estimate=pl.CostEstimate(flops=7_200_000_000, bytes_accessed=8_000_000, transcendentals=0),
         name="conv_rim",
     )(rim, above, below, before, after, weight.reshape(3, 3, 1536, 256))
 
@@ -315,7 +315,7 @@
     above, below = send(edge_rows(3, 7), to_row(1)), send(edge_rows(0, 0), to_row(-1))
     odd = row % 2
     near = send(lax.dynamic_slice_in_dim(weights, odd * 256, 256, axis=3), along_z(2))
-    own, above, below, weights, near = lax.optimization_barrier((own, above, below, weights, near))
+    own, weights = lax.optimization_barrier((own, weights))
 
     other = send(own, flip_half)
     w1, w3 = send(weights, along_z(1)), send(weights, along_z(3))
@@ -325,6 +325,7 @@
     rim_above, rim_below = above[192:].reshape(2, 64, 512), below[192:].reshape(2, 64, 512)
     column = lambda i: jnp.concatenate([rim_above[:, None, i], rim[:, :, i], rim_below[:, None, i]], axis=1)
     before, after = send(column(59), to_chan(1)), send(column(0), to_chan(-1))
+    other, before, after = lax.optimization_barrier((other, before, after))
     rim = conv_rim(rim, rim_above, rim_below, before, after, conv_out_weight)
     other, other_edge, w1, w3, far, rim = lax.optimization_barrier((other, other_edge, w1, w3, far, rim))
     parts = [own, other, send(own, flip_core), send(other, flip_core),

time: 124 us -> 118 us (0.952)
  waiting for transfers between devices: 27 us -> 12.5 us
  starting transfers between devices: 52.2 us -> 60.4 us
    ppermute x19, waiting for transfers between devices: 22 us -> 12.5 us  [send(): return lax.ppermute(array, BOTH, device_perm(move))]
    all_to_all x2, waiting for transfers between devices: 5.02 us -> 0.01 us  [to_zones(): lax.all_to_all(pieces, 'chan', split_axis=0, concat_axis=0, axis_index_gr...]
    ppermute x19, starting transfers between devices: 35.5 us -> 39.9 us  [send(): return lax.ppermute(array, BOTH, device_perm(move))]
    all_to_all x2, starting transfers between devices: 8.76 us -> 11.1 us  [to_zones(): lax.all_to_all(pieces, 'chan', split_axis=0, concat_axis=0, axis_index_gr...]
    all_to_all x1, starting transfers between devices: 7.85 us -> 9.45 us  [body(): lax.all_to_all(stats, BOTH, split_axis=0, concat_axis=0, tiled=True)]
    unnamed x25 -> x23, local copies, waits for them, and re-layouts: 2.38 us -> 3.19 us
  transfers between devices with their start and end apart: 22 -> 22, of which waited for: 11 -> 8; matrix products, arithmetic and copies ran while one was open for 6% -> 5% of each run, Pallas kernels for 5% -> 5%
where the time goes in v3:
time: 118 us; the launch traced here: 116 us
  starting transfers between devices  60.4 us (51%)
  Pallas kernels  29.1 us (25%)
  waiting for transfers between devices  12.5 us (11%)
  local copies, waits for them, and re-layouts  9.59 us (8%)
  other arithmetic  3.66 us (3%)
    ppermute x19, starting transfers between devices, send(): return lax.ppermute(array, BOTH, device_perm(move))  39.9 us
    pallas_call x1, Pallas kernels, conv_in(): pl.pallas_call(conv_in_kernel, out_shape=[jax.ShapeDtypeStruct((4, 4, 32,...  13.2 us
    ppermute x19, waiting for transfers between devices, send(): return lax.ppermute(array, BOTH, device_perm(move))  12.5 us
    all_to_all x2, starting transfers between devices, to_zones(): lax.all_to_all(pieces, 'chan', split_axis=0, concat_axis=0, axis_index_gr...  11.1 us
    pallas_call x1, Pallas kernels, conv_out(): pl.pallas_call(conv_out_kernel, out_shape=jax.ShapeDtypeStruct((2, 2, 4,...  9.59 us
    all_to_all x1, starting transfers between devices, body(): lax.all_to_all(stats, BOTH, split_axis=0, concat_axis=0, tiled=True)  9.45 us
    pallas_call x1, Pallas kernels, conv_rim(): pl.pallas_call(rim_kernel, out_shape=jax.ShapeDtypeStruct((2, 2, 2, 4, 32...  6.27 us
    unnamed x23, local copies, waits for them, and re-layouts  3.19 us
  transfers between devices with their start and end apart: 22, of which 8 were waited for; matrix products, arithmetic and copies ran while one was open for 5% of the time, Pallas kernels for 5%

profile of v3, /device:TPU:2, one launch (start us, length us, event | category | flops | bytes accessed | tf_op | source)
XLA Modules:
  0.0 115.6 jit_solution(500589872445495227)
XLA Ops:
  0.0 1.3 %copy.32 = bf16[480,6,4,32]{0,3,1,2:T(8,128)(2,1)S(1)} copy(bf16[480,6,4,32]{0,3,2,1:T(8,128)(2,1)} %param.8) | data formatting | bytes 1474560 | tf_op args[0]
  1.3 0.3 fusion
  1.6 1.0 pad_maximum_fusion
  2.6 5.3 %all-to-all-start = ((bf16[4,4,6,32,128]{4,3,2,1,0:T(8,128)(2,1)}), bf16[4,4,6,32,128]{4,3,2,1,0:T(8,128)(2,1)}, u32[]{:S(2)}, u32[]{:S(2)}) async-start(bf16[4,4,6,32,128]{4,3,2,1,0:T(8,128)(2,1)} %pad_maximum_fusion), calls=%async_computation | async-start | bytes 1572864 | tf_op jit(solution)/shard_map/all_to_all | solution.py:309
  7.9 0.1 pad_bitcast_fusion
  8.0 0.3 fusion.9
  8.4 0.2 pad_slice_fusion.1
  8.6 3.5 %collective-permute-start.1 = (bf16[320,512]{1,0:T(8,128)(2,1)S(1)}, bf16[320,512]{1,0:T(8,128)(2,1)S(1)}, u32[]{:S(2)}, u32[]{:S(2)}) collective-permute-start(bf16[320,512]{1,0:T(8,128)(2,1)S(1)} %pad_maximum_fusion.3), channel_id=1, source_target_pairs={{0,1},{1,2},{2,3},{3,4},{4,5},{5,6},{6,7},{8,9},{9,10},{10,11},{11... | collective-permute-start | bytes 983048 | tf_op jit(solution)/shard_map/ppermute | solution.py:26
  12.2 4.5 %collective-permute-start.2 = (bf16[320,512]{1,0:T(8,128)(2,1)S(1)}, bf16[320,512]{1,0:T(8,128)(2,1)S(1)}, u32[]{:S(2)}, u32[]{:S(2)}) collective-permute-start(bf16[320,512]{1,0:T(8,128)(2,1)S(1)} %pad_maximum_fusion.4), channel_id=1, source_target_pairs={{1,0},{2,1},{3,2},{4,3},{5,4},{6,5},{7,6},{9,8},{10,9},{11,10},{12... | collective-permute-start | bytes 983048 | tf_op jit(solution)/shard_map/ppermute | solution.py:26
  16.7 1.0 constant_dynamic-slice_fusion
  17.7 3.6 %collective-permute-start.8 = (bf16[9,3,32,256]{3,2,1,0:T(8,128)(2,1)S(1)}, bf16[9,3,32,256]{3,2,1,0:T(8,128)(2,1)}, u32[]{:S(2)}, u32[]{:S(2)}) collective-permute-start(bf16[9,3,32,256]{3,2,1,0:T(8,128)(2,1)S(1)} %constant_dynamic-slice_fusion), channel_id=1, source_target_pairs={{0,64},{1,65},{2,66},{3,67},{4,68},{5,69},{6,70},{7,71},{8,72},{9,... | collective-permute-start | bytes 1327112 | tf_op jit(solution)/shard_map/ppermute | solution.py:26
  21.3 2.1 %collective-permute-start = (bf16[4,4,6,32,128]{4,3,2,1,0:T(8,128)(2,1)}, bf16[4,4,6,32,128]{4,3,2,1,0:T(8,128)(2,1)}, u32[]{:S(2)}, u32[]{:S(2)}) collective-permute-start(bf16[4,4,6,32,128]{4,3,2,1,0:T(8,128)(2,1)} %all-to-all-done.own), channel_id=1, source_target_pairs={{0,16},{1,17},{2,18},{3,19},{4,20},{5,21},{6,22},{7,23},{8,24},{9,... | collective-permute-start | bytes 2359304 | tf_op jit(solution)/shard_map/ppermute | solution.py:26
  23.4 0.0 collective-permute-done.1
  23.5 0.3 collective-permute-done.2
  23.8 0.2 fusion.5
  24.0 0.8 pad_maximum_fusion.2
  24.8 5.8 %all-to-all-start.1 = ((bf16[4,2,6,32,128]{4,3,2,1,0:T(8,128)(2,1)}), bf16[4,2,6,32,128]{4,3,2,1,0:T(8,128)(2,1)S(1)}, u32[]{:S(2)}, u32[]{:S(2)}) async-start(bf16[4,2,6,32,128]{4,3,2,1,0:T(8,128)(2,1)} %pad_maximum_fusion.2), calls=%async_computation.1 | async-start | bytes 786432 | tf_op jit(solution)/shard_map/all_to_all | solution.py:309
  30.6 2.1 %collective-permute-start.6 = (bf16[9,3,32,512]{3,2,1,0:T(8,128)(2,1)}, bf16[9,3,32,512]{3,2,1,0:T(8,128)(2,1)}, u32[]{:S(2)}, u32[]{:S(2)}) collective-permute-start(bf16[9,3,32,512]{3,2,1,0:T(8,128)(2,1)} %bitcast.84), channel_id=1, source_target_pairs={{0,32},{1,33},{2,34},{3,35},{4,36},{5,37},{6,38},{7,39},{8,40},{9,... | collective-permute-start | bytes 2654216 | tf_op jit(solution)/shard_map/ppermute | solution.py:26
  32.7 1.3 %collective-permute-start.7 = (bf16[9,3,32,512]{3,2,1,0:T(8,128)(2,1)}, bf16[9,3,32,512]{3,2,1,0:T(8,128)(2,1)}, u32[]{:S(2)}, u32[]{:S(2)}) collective-permute-start(bf16[9,3,32,512]{3,2,1,0:T(8,128)(2,1)} %bitcast.85), channel_id=1, source_target_pairs={{0,96},{1,97},{2,98},{3,99},{4,100},{5,101},{6,102},{7,103},{8,104... | collective-permute-start | bytes 2654216 | tf_op jit(solution)/shard_map/ppermute | solution.py:26
  34.0 1.3 %collective-permute-start.3 = (bf16[2,10,512]{2,1,0:T(8,128)(2,1)S(1)}, bf16[2,10,512]{2,1,0:T(8,128)(2,1)S(1)}, u32[]{:S(2)}, u32[]{:S(2)}) collective-permute-start(bf16[2,10,512]{2,1,0:T(8,128)(2,1)S(1)} %pad_maximum_fusion.6), channel_id=1, source_target_pairs={{0,8},{1,9},{2,10},{3,11},{4,12},{5,13},{6,14},{7,15},{8,16},{9,17... | collective-permute-start | bytes 61448 | tf_op jit(solution)/shard_map/ppermute | solution.py:26
  35.4 0.8 collective-permute-done.3.before
  36.2 1.3 %collective-permute-start.4 = (bf16[2,10,512]{2,1,0:T(8,128)(2,1)S(1)}, bf16[2,10,512]{2,1,0:T(8,128)(2,1)S(1)}, u32[]{:S(2)}, u32[]{:S(2)}) collective-permute-start(bf16[2,10,512]{2,1,0:T(8,128)(2,1)S(1)} %pad_maximum_fusion.7), channel_id=1, source_target_pairs={{8,0},{9,1},{10,2},{11,3},{12,4},{13,5},{14,6},{15,7},{16,8},{17,9... | collective-permute-start | bytes 61448 | tf_op jit(solution)/shard_map/ppermute | solution.py:26
  37.5 0.6 copy.24.rim
  38.1 0.1 collective-permute-start.9
  38.1 3.9 %collective-permute-done.4.after = bf16[2,10,512]{2,1,0:T(8,128)(2,1)S(1)} collective-permute-done((bf16[2,10,512]{2,1,0:T(8,128)(2,1)S(1)}, bf16[2,10,512]{2,1,0:T(8,128)(2,1)S(1)}, u32[]{:S(2)}, u32[]{:S(2)}) %collective-permute-start.4) | collective-permute-done | bytes 20512 | tf_op jit(solution)/shard_map/ppermute | solution.py:26
  42.0 5.3 %collective-permute-start.10 = (bf16[4,4,6,32,128]{4,3,2,1,0:T(8,128)(2,1)}, bf16[4,4,6,32,128]{4,3,2,1,0:T(8,128)(2,1)S(1)}, u32[]{:S(2)}, u32[]{:S(2)}) collective-permute-start(bf16[4,4,6,32,128]{4,3,2,1,0:T(8,128)(2,1)} %all-to-all-done.own), channel_id=1, source_target_pairs={{0,8},{1,9},{2,10},{3,11},{4,12},{5,13},{6,14},{7,15},{8,0},{9,1},... | collective-permute-start | bytes 2359304 | tf_op jit(solution)/shard_map/ppermute | solution.py:26
  47.3 2.6 %collective-permute-start.5 = (bf16[4,2,6,32,128]{4,3,2,1,0:T(8,128)(2,1)S(1)}, bf16[4,2,6,32,128]{4,3,2,1,0:T(8,128)(2,1)}, u32[]{:S(2)}, u32[]{:S(2)}) collective-permute-start(bf16[4,2,6,32,128]{4,3,2,1,0:T(8,128)(2,1)S(1)} %all-to-all-done.1.own_edge), channel_id=1, source_target_pairs={{0,16},{1,17},{2,18},{3,19},{4,20},{5,21},{6,22},{7,23},{8,24},{9,... | collective-permute-start | bytes 1179656 | tf_op jit(solution)/shard_map/ppermute | solution.py:26
  49.9 6.3 %conv_rim.1.rim = f32[2,2,2,4,32,256]{5,4,3,2,1,0:T(8,128)S(1)} custom-call(bf16[2,8,64,512]{3,2,1,0:T(8,128)(2,1)S(1)} %copy.24.rim, bf16[2,64,512]{2,1,0:T(8,128)(2,1)S(1)} %bitcast.69, bf16[2,64,512]{2,1,0:T(8,128)(2,1)S(1)} %bitcast.71, bf16[2,10,512]{2,1,0:T(8,128)(2,1)S(1)} %collective-permute-done.3.before, ...), custom_call_target="tpu_custom_call" | custom-call | flops 7200000000 | bytes 8000000 | tf_op jit(solution)/shard_map/conv_rim/pallas_call | solution.py:193
  56.2 1.0 copy-done.1
  57.2 2.9 %collective-permute-done.5.other_edge = bf16[4,2,6,32,128]{4,3,2,1,0:T(8,128)(2,1)} collective-permute-done((bf16[4,2,6,32,128]{4,3,2,1,0:T(8,128)(2,1)S(1)}, bf16[4,2,6,32,128]{4,3,2,1,0:T(8,128)(2,1)}, u32[]{:S(2)}, u32[]{:S(2)}) %collective-permute-start.5) | collective-permute-done | bytes 393248 | tf_op jit(solution)/shard_map/ppermute | solution.py:26
  60.1 0.5 collective-permute-start.12
  60.6 0.1 collective-permute-start.13
  60.7 0.1 reshape.70
  60.8 0.1 broadcast_in_dim.13
  60.9 0.6 pad_add_fusion.place
  61.5 1.8 %collective-permute-done.12.own_edge_swap = bf16[4,2,6,32,128]{4,3,2,1,0:T(8,128)(2,1)S(1)} collective-permute-done((bf16[4,2,6,32,128]{4,3,2,1,0:T(8,128)(2,1)S(1)}, bf16[4,2,6,32,128]{4,3,2,1,0:T(8,128)(2,1)S(1)}, u32[]{:S(2)}, u32[]{:S(2)}) %collective-permute-start.12) | collective-permute-done | bytes 393248 | tf_op jit(solution)/shard_map/ppermute | solution.py:26
  63.3 0.5 collective-permute-done.13.other_edge_swap
  63.8 0.9 copy-done.8
  64.7 0.7 broadcast_in_dim.14.bias
  65.4 0.0 copy-start.6
  65.4 0.0 copy-start
  65.5 13.2 %conv_in.1 = (bf16[4,4,32,128]{3,2,1,0:T(8,128)(2,1)}, bf16[4,4,32,128]{3,2,1,0:T(8,128)(2,1)}, bf16[4,4,32,128]{3,2,1,0:T(8,128)(2,1)}, bf16[4,4,32,128]{3,2,1,0:T(8,128)(2,1)}, f32[128,128]{1,0:T(8,128)}) custom-call(s32[4]{0:T(128)} %pad_add_fusion.place, bf16[4,4,6,32,128]{4,3,2,1,0:T(8,128)(2,1)} %all-to-all-done.own, ...), custom_call_target="tpu_custom_call" | custom-call | flops 7200000000 | bytes 9000000 | tf_op jit(solution)/shard_map/conv_in/pallas_call | solution.py:126
  78.7 0.2 collective-permute-start.14
  78.9 2.5 %collective-permute-start.16 = (bf16[4,4,32,128]{3,2,1,0:T(8,128)(2,1)}, bf16[4,4,32,128]{3,2,1,0:T(8,128)(2,1)S(1)}, u32[]{:S(2)}, u32[]{:S(2)}) collective-permute-start(bf16[4,4,32,128]{3,2,1,0:T(8,128)(2,1)} %get-tuple-element.38), channel_id=1, source_target_pairs={{0,24},{1,25},{2,26},{3,27},{4,28},{5,29},{6,30},{7,31},{8,16},{9,... | collective-permute-start | bytes 393224 | tf_op jit(solution)/shard_map/ppermute | solution.py:26
  81.4 1.0 collective-permute-start.15
  82.4 0.1 reshape.74
  82.5 0.1 reshape.75
  82.6 0.1 reshape.76
  82.7 0.1 stack_reshape.15
  82.7 0.1 stack.109.place
  82.8 9.5 %all-to-all-start.2 = ((f32[128,1,128]{2,1,0:T(1,128)}), f32[128,1,128]{2,1,0:T(1,128)S(1)}, u32[]{:S(2)}, u32[]{:S(2)}) async-start(f32[128,1,128]{2,1,0:T(1,128)} %bitcast.91), calls=%async_computation.2 | async-start | bytes 131072 | tf_op jit(solution)/shard_map/all_to_all | solution.py:345
  92.3 1.0 pad_maximum_fusion.1
  93.4 3.4 %collective-permute-start.17 = (bf16[4,4,32,128]{3,2,1,0:T(8,128)(2,1)S(1)}, bf16[4,4,32,128]{3,2,1,0:T(8,128)(2,1)S(1)}, u32[]{:S(2)}, u32[]{:S(2)}) collective-permute-start(bf16[4,4,32,128]{3,2,1,0:T(8,128)(2,1)S(1)} %get-tuple-element.52), channel_id=1, source_target_pairs={{0,1},{1,2},{2,3},{3,4},{4,5},{5,6},{6,7},{8,9},{9,10},{10,11},{11... | collective-permute-start | bytes 393224 | tf_op jit(solution)/shard_map/ppermute | solution.py:26
  96.7 4.6 %collective-permute-start.18 = (bf16[4,4,32,128]{3,2,1,0:T(8,128)(2,1)S(1)}, bf16[4,4,32,128]{3,2,1,0:T(8,128)(2,1)S(1)}, u32[]{:S(2)}, u32[]{:S(2)}) collective-permute-start(bf16[4,4,32,128]{3,2,1,0:T(8,128)(2,1)S(1)} %get-tuple-element.51), channel_id=1, source_target_pairs={{1,0},{2,1},{3,2},{4,3},{5,4},{6,5},{7,6},{9,8},{10,9},{11,10},{12... | collective-permute-start | bytes 393224 | tf_op jit(solution)/shard_map/ppermute | solution.py:26
  101.4 0.1 reshape.72
  101.5 0.1 broadcast_in_dim.15
  101.5 0.1 stack_reshape.14
  101.6 0.1 broadcast_in_dim.16
  101.7 0.1 reshape.73
  101.8 1.1 collective-permute-done.17.up
  102.9 1.2 %collective-permute-done.18.down = bf16[4,4,32,128]{3,2,1,0:T(8,128)(2,1)S(1)} collective-permute-done((bf16[4,4,32,128]{3,2,1,0:T(8,128)(2,1)S(1)}, bf16[4,4,32,128]{3,2,1,0:T(8,128)(2,1)S(1)}, u32[]{:S(2)}, u32[]{:S(2)}) %collective-permute-start.18) | collective-permute-done | bytes 131104 | tf_op jit(solution)/shard_map/ppermute | solution.py:26
  104.1 9.6 %conv_out.1 = bf16[2,2,4,4,32,256]{5,4,3,2,1,0:T(8,128)(2,1)S(1)} custom-call(s32[5]{0:T(128)S(1)} %stack.109.place, bf16[4,4,4,32,128]{4,3,2,1,0:T(8,128)(2,1)S(1)} %copy.28.main, bf16[4,4,32,128]{3,2,1,0:T(8,128)(2,1)S(1)} %collective-permute-done.17.up, bf16[4,4,32,128]{3,2,1,0:T(8,128)(2,1)S(1)} %collective-permute-done.18.down, ...), custom_call_target="tpu_custom_call" | custom-call | flops 4899999744 | bytes 18000000 | tf_op jit(solution)/shard_map/conv_out/pallas_call | solution.py:266
  113.7 0.8 copy.29
  114.5 1.1 copy.30
  (56 shorter events, 0.5 us)
Async XLA Ops:
  0.0 7.9 %copy-start.2 = (bf16[60,2,8,512]{3,2,1,0:T(8,128)(2,1)S(1)}, bf16[60,2,8,512]{3,2,1,0:T(8,128)(2,1)}, u32[]{:S(2)}) copy-start(bf16[60,2,8,512]{3,2,1,0:T(8,128)(2,1)} %param.13) | copy-start | bytes 2949124
  2.6 18.7 %all-to-all-start = ((bf16[4,4,6,32,128]{4,3,2,1,0:T(8,128)(2,1)}), bf16[4,4,6,32,128]{4,3,2,1,0:T(8,128)(2,1)}, u32[]{:S(2)}, u32[]{:S(2)}) async-start(bf16[4,4,6,32,128]{4,3,2,1,0:T(8,128)(2,1)} %pad_maximum_fusion), calls=%async_computation | async-start | bytes 1572864 | tf_op jit(solution)/shard_map/all_to_all | solution.py:309
  8.6 14.9 %collective-permute-start.1 = (bf16[320,512]{1,0:T(8,128)(2,1)S(1)}, bf16[320,512]{1,0:T(8,128)(2,1)S(1)}, u32[]{:S(2)}, u32[]{:S(2)}) collective-permute-start(bf16[320,512]{1,0:T(8,128)(2,1)S(1)} %pad_maximum_fusion.3), channel_id=1, source_target_pairs={{0,1},{1,2},{2,3},{3,4},{4,5},{5,6},{6,7},{8,9},{9,10},{10,11},{11... | collective-permute-start | bytes 983048 | tf_op jit(solution)/shard_map/ppermute | solution.py:26
  12.2 11.6 %collective-permute-start.2 = (bf16[320,512]{1,0:T(8,128)(2,1)S(1)}, bf16[320,512]{1,0:T(8,128)(2,1)S(1)}, u32[]{:S(2)}, u32[]{:S(2)}) collective-permute-start(bf16[320,512]{1,0:T(8,128)(2,1)S(1)} %pad_maximum_fusion.4), channel_id=1, source_target_pairs={{1,0},{2,1},{3,2},{4,3},{5,4},{6,5},{7,6},{9,8},{10,9},{11,10},{12... | collective-permute-start | bytes 983048 | tf_op jit(solution)/shard_map/ppermute | solution.py:26
  17.7 20.3 %collective-permute-start.8 = (bf16[9,3,32,256]{3,2,1,0:T(8,128)(2,1)S(1)}, bf16[9,3,32,256]{3,2,1,0:T(8,128)(2,1)}, u32[]{:S(2)}, u32[]{:S(2)}) collective-permute-start(bf16[9,3,32,256]{3,2,1,0:T(8,128)(2,1)S(1)} %constant_dynamic-slice_fusion), channel_id=1, source_target_pairs={{0,64},{1,65},{2,66},{3,67},{4,68},{5,69},{6,70},{7,71},{8,72},{9,... | collective-permute-start | bytes 1327112 | tf_op jit(solution)/shard_map/ppermute | solution.py:26
  21.3 26.0 %collective-permute-start = (bf16[4,4,6,32,128]{4,3,2,1,0:T(8,128)(2,1)}, bf16[4,4,6,32,128]{4,3,2,1,0:T(8,128)(2,1)}, u32[]{:S(2)}, u32[]{:S(2)}) collective-permute-start(bf16[4,4,6,32,128]{4,3,2,1,0:T(8,128)(2,1)} %all-to-all-done.own), channel_id=1, source_target_pairs={{0,16},{1,17},{2,18},{3,19},{4,20},{5,21},{6,22},{7,23},{8,24},{9,... | collective-permute-start | bytes 2359304 | tf_op jit(solution)/shard_map/ppermute | solution.py:26
  24.8 22.6 %all-to-all-start.1 = ((bf16[4,2,6,32,128]{4,3,2,1,0:T(8,128)(2,1)}), bf16[4,2,6,32,128]{4,3,2,1,0:T(8,128)(2,1)S(1)}, u32[]{:S(2)}, u32[]{:S(2)}) async-start(bf16[4,2,6,32,128]{4,3,2,1,0:T(8,128)(2,1)} %pad_maximum_fusion.2), calls=%async_computation.1 | async-start | bytes 786432 | tf_op jit(solution)/shard_map/all_to_all | solution.py:309
  30.6 29.4 %collective-permute-start.6 = (bf16[9,3,32,512]{3,2,1,0:T(8,128)(2,1)}, bf16[9,3,32,512]{3,2,1,0:T(8,128)(2,1)}, u32[]{:S(2)}, u32[]{:S(2)}) collective-permute-start(bf16[9,3,32,512]{3,2,1,0:T(8,128)(2,1)} %bitcast.84), channel_id=1, source_target_pairs={{0,32},{1,33},{2,34},{3,35},{4,36},{5,37},{6,38},{7,39},{8,40},{9,... | collective-permute-start | bytes 2654216 | tf_op jit(solution)/shard_map/ppermute | solution.py:26
  32.7 27.3 %collective-permute-start.7 = (bf16[9,3,32,512]{3,2,1,0:T(8,128)(2,1)}, bf16[9,3,32,512]{3,2,1,0:T(8,128)(2,1)}, u32[]{:S(2)}, u32[]{:S(2)}) collective-permute-start(bf16[9,3,32,512]{3,2,1,0:T(8,128)(2,1)} %bitcast.85), channel_id=1, source_target_pairs={{0,96},{1,97},{2,98},{3,99},{4,100},{5,101},{6,102},{7,103},{8,104... | collective-permute-start | bytes 2654216 | tf_op jit(solution)/shard_map/ppermute | solution.py:26
  34.0 2.1 %collective-permute-start.3 = (bf16[2,10,512]{2,1,0:T(8,128)(2,1)S(1)}, bf16[2,10,512]{2,1,0:T(8,128)(2,1)S(1)}, u32[]{:S(2)}, u32[]{:S(2)}) collective-permute-start(bf16[2,10,512]{2,1,0:T(8,128)(2,1)S(1)} %pad_maximum_fusion.6), channel_id=1, source_target_pairs={{0,8},{1,9},{2,10},{3,11},{4,12},{5,13},{6,14},{7,15},{8,16},{9,17... | collective-permute-start | bytes 61448 | tf_op jit(solution)/shard_map/ppermute | solution.py:26
  36.2 5.9 %collective-permute-start.4 = (bf16[2,10,512]{2,1,0:T(8,128)(2,1)S(1)}, bf16[2,10,512]{2,1,0:T(8,128)(2,1)S(1)}, u32[]{:S(2)}, u32[]{:S(2)}) collective-permute-start(bf16[2,10,512]{2,1,0:T(8,128)(2,1)S(1)} %pad_maximum_fusion.7), channel_id=1, source_target_pairs={{8,0},{9,1},{10,2},{11,3},{12,4},{13,5},{14,6},{15,7},{16,8},{17,9... | collective-permute-start | bytes 61448 | tf_op jit(solution)/shard_map/ppermute | solution.py:26
  38.1 19.1 %collective-permute-start.9 = (bf16[9,3,32,256]{3,2,1,0:T(8,128)(2,1)}, bf16[9,3,32,256]{3,2,1,0:T(8,128)(2,1)S(1)}, u32[]{:S(2)}, u32[]{:S(2)}) collective-permute-start(bf16[9,3,32,256]{3,2,1,0:T(8,128)(2,1)} %collective-permute-done.8.near), channel_id=1, source_target_pairs={{0,1},{1,0},{2,3},{3,2},{4,5},{5,4},{6,7},{7,6},{8,9},{9,8},{10,11... | collective-permute-start | bytes 1327112 | tf_op jit(solution)/shard_map/ppermute | solution.py:26
  42.0 21.3 %collective-permute-start.10 = (bf16[4,4,6,32,128]{4,3,2,1,0:T(8,128)(2,1)}, bf16[4,4,6,32,128]{4,3,2,1,0:T(8,128)(2,1)S(1)}, u32[]{:S(2)}, u32[]{:S(2)}) collective-permute-start(bf16[4,4,6,32,128]{4,3,2,1,0:T(8,128)(2,1)} %all-to-all-done.own), channel_id=1, source_target_pairs={{0,8},{1,9},{2,10},{3,11},{4,12},{5,13},{6,14},{7,15},{8,0},{9,1},... | collective-permute-start | bytes 2359304 | tf_op jit(solution)/shard_map/ppermute | solution.py:26
  47.3 12.7 %copy-start.3 = (bf16[4,2,6,32,128]{4,3,2,1,0:T(8,128)(2,1)}, bf16[4,2,6,32,128]{4,3,2,1,0:T(8,128)(2,1)S(1)}, u32[]{:S(2)}) copy-start(bf16[4,2,6,32,128]{4,3,2,1,0:T(8,128)(2,1)S(1)} %all-to-all-done.1.own_edge) | copy-start | bytes 1179652
  47.3 12.7 %collective-permute-start.5 = (bf16[4,2,6,32,128]{4,3,2,1,0:T(8,128)(2,1)S(1)}, bf16[4,2,6,32,128]{4,3,2,1,0:T(8,128)(2,1)}, u32[]{:S(2)}, u32[]{:S(2)}) collective-permute-start(bf16[4,2,6,32,128]{4,3,2,1,0:T(8,128)(2,1)S(1)} %all-to-all-done.1.own_edge), channel_id=1, source_target_pairs={{0,16},{1,17},{2,18},{3,19},{4,20},{5,21},{6,22},{7,23},{8,24},{9,... | collective-permute-start | bytes 1179656 | tf_op jit(solution)/shard_map/ppermute | solution.py:26
  49.9 10.7 %copy-start.4 = (f32[512]{0:T(512)S(1)}, f32[512]{0:T(512)}, u32[]{:S(2)}) copy-start(f32[512]{0:T(512)} %param.10) | copy-start | bytes 6148
  56.2 1.0 copy-start.1
  57.2 8.2 %copy-start.9 = (bf16[9,3,32,256]{3,2,1,0:T(8,128)(2,1)}, bf16[9,3,32,256]{3,2,1,0:T(8,128)(2,1)S(1)}, u32[]{:S(2)}) copy-start(bf16[9,3,32,256]{3,2,1,0:T(8,128)(2,1)S(1)} %collective-permute-done.9.far) | copy-start | bytes 1327108
  60.0 3.8 %collective-permute-start.11 = (bf16[4,4,6,32,128]{4,3,2,1,0:T(8,128)(2,1)}, bf16[4,4,6,32,128]{4,3,2,1,0:T(8,128)(2,1)S(1)}, u32[]{:S(2)}, u32[]{:S(2)}) collective-permute-start(bf16[4,4,6,32,128]{4,3,2,1,0:T(8,128)(2,1)} %collective-permute-done.other), channel_id=1, source_target_pairs={{0,8},{1,9},{2,10},{3,11},{4,12},{5,13},{6,14},{7,15},{8,0},{9,1},... | collective-permute-start | bytes 2359304 | tf_op jit(solution)/shard_map/ppermute | solution.py:26
  60.1 3.2 %collective-permute-start.12 = (bf16[4,2,6,32,128]{4,3,2,1,0:T(8,128)(2,1)S(1)}, bf16[4,2,6,32,128]{4,3,2,1,0:T(8,128)(2,1)S(1)}, u32[]{:S(2)}, u32[]{:S(2)}) collective-permute-start(bf16[4,2,6,32,128]{4,3,2,1,0:T(8,128)(2,1)S(1)} %all-to-all-done.1.own_edge), channel_id=1, source_target_pairs={{0,8},{1,9},{2,10},{3,11},{4,12},{5,13},{6,14},{7,15},{8,0},{9,1},... | collective-permute-start | bytes 1179656 | tf_op jit(solution)/shard_map/ppermute | solution.py:26
  60.6 3.2 %collective-permute-start.13 = (bf16[4,2,6,32,128]{4,3,2,1,0:T(8,128)(2,1)}, bf16[4,2,6,32,128]{4,3,2,1,0:T(8,128)(2,1)}, u32[]{:S(2)}, u32[]{:S(2)}) collective-permute-start(bf16[4,2,6,32,128]{4,3,2,1,0:T(8,128)(2,1)} %collective-permute-done.5.other_edge), channel_id=1, source_target_pairs={{0,8},{1,9},{2,10},{3,11},{4,12},{5,13},{6,14},{7,15},{8,0},{9,1},... | collective-permute-start | bytes 1179656 | tf_op jit(solution)/shard_map/ppermute | solution.py:26
  63.3 2.1 %copy-start.10 = (bf16[4,2,6,32,128]{4,3,2,1,0:T(8,128)(2,1)}, bf16[4,2,6,32,128]{4,3,2,1,0:T(8,128)(2,1)S(1)}, u32[]{:S(2)}) copy-start(bf16[4,2,6,32,128]{4,3,2,1,0:T(8,128)(2,1)S(1)} %collective-permute-done.12.own_edge_swap) | copy-start | bytes 1179652
  63.3 2.1 %copy-start.7 = (bf16[4,4,6,32,128]{4,3,2,1,0:T(8,128)(2,1)}, bf16[4,4,6,32,128]{4,3,2,1,0:T(8,128)(2,1)S(1)}, u32[]{:S(2)}) copy-start(bf16[4,4,6,32,128]{4,3,2,1,0:T(8,128)(2,1)S(1)} %collective-permute-done.10.own_swap) | copy-start | bytes 2359300
  63.8 0.9 copy-start.8
  65.4 17.0 %copy-start.5 = (f32[512]{0:T(512)S(1)}, f32[512]{0:T(512)}, u32[]{:S(2)}) copy-start(f32[512]{0:T(512)} %param.11) | copy-start | bytes 6148
  65.4 17.1 %copy-start.6 = (f32[512]{0:T(512)S(1)}, f32[512]{0:T(512)}, u32[]{:S(2)}) copy-start(f32[512]{0:T(512)} %param.12) | copy-start | bytes 6148
  65.4 38.7 %copy-start = (f32[256]{0:T(256)S(1)}, f32[256]{0:T(256)}, u32[]{:S(2)}) copy-start(f32[256]{0:T(256)} %param.15) | copy-start | bytes 3076
  78.7 4.2 %collective-permute-start.14 = (bf16[4,4,32,128]{3,2,1,0:T(8,128)(2,1)}, bf16[4,4,32,128]{3,2,1,0:T(8,128)(2,1)S(1)}, u32[]{:S(2)}, u32[]{:S(2)}) collective-permute-start(bf16[4,4,32,128]{3,2,1,0:T(8,128)(2,1)} %get-tuple-element.35), channel_id=1, source_target_pairs={{0,8},{1,9},{2,10},{3,11},{4,12},{5,13},{6,14},{7,15},{8,0},{9,1},... | collective-permute-start | bytes 393224 | tf_op jit(solution)/shard_map/ppermute | solution.py:26
  78.9 13.4 %collective-permute-start.16 = (bf16[4,4,32,128]{3,2,1,0:T(8,128)(2,1)}, bf16[4,4,32,128]{3,2,1,0:T(8,128)(2,1)S(1)}, u32[]{:S(2)}, u32[]{:S(2)}) collective-permute-start(bf16[4,4,32,128]{3,2,1,0:T(8,128)(2,1)} %get-tuple-element.38), channel_id=1, source_target_pairs={{0,24},{1,25},{2,26},{3,27},{4,28},{5,29},{6,30},{7,31},{8,16},{9,... | collective-permute-start | bytes 393224 | tf_op jit(solution)/shard_map/ppermute | solution.py:26
  81.4 10.9 %collective-permute-start.15 = (bf16[4,4,32,128]{3,2,1,0:T(8,128)(2,1)}, bf16[4,4,32,128]{3,2,1,0:T(8,128)(2,1)S(1)}, u32[]{:S(2)}, u32[]{:S(2)}) collective-permute-start(bf16[4,4,32,128]{3,2,1,0:T(8,128)(2,1)} %get-tuple-element.37), channel_id=1, source_target_pairs={{0,16},{1,17},{2,18},{3,19},{4,20},{5,21},{6,22},{7,23},{8,24},{9,... | collective-permute-start | bytes 393224 | tf_op jit(solution)/shard_map/ppermute | solution.py:26
  82.8 18.5 %all-to-all-start.2 = ((f32[128,1,128]{2,1,0:T(1,128)}), f32[128,1,128]{2,1,0:T(1,128)S(1)}, u32[]{:S(2)}, u32[]{:S(2)}) async-start(f32[128,1,128]{2,1,0:T(1,128)} %bitcast.91), calls=%async_computation.2 | async-start | bytes 131072 | tf_op jit(solution)/shard_map/all_to_all | solution.py:345
  93.4 9.6 %collective-permute-start.17 = (bf16[4,4,32,128]{3,2,1,0:T(8,128)(2,1)S(1)}, bf16[4,4,32,128]{3,2,1,0:T(8,128)(2,1)S(1)}, u32[]{:S(2)}, u32[]{:S(2)}) collective-permute-start(bf16[4,4,32,128]{3,2,1,0:T(8,128)(2,1)S(1)} %get-tuple-element.52), channel_id=1, source_target_pairs={{0,1},{1,2},{2,3},{3,4},{4,5},{5,6},{6,7},{8,9},{9,10},{10,11},{11... | collective-permute-start | bytes 393224 | tf_op jit(solution)/shard_map/ppermute | solution.py:26
  96.7 7.4 %collective-permute-start.18 = (bf16[4,4,32,128]{3,2,1,0:T(8,128)(2,1)S(1)}, bf16[4,4,32,128]{3,2,1,0:T(8,128)(2,1)S(1)}, u32[]{:S(2)}, u32[]{:S(2)}) collective-permute-start(bf16[4,4,32,128]{3,2,1,0:T(8,128)(2,1)S(1)} %get-tuple-element.51), channel_id=1, source_target_pairs={{1,0},{2,1},{3,2},{4,3},{5,4},{6,5},{7,6},{9,8},{10,9},{11,10},{12... | collective-permute-start | bytes 393224 | tf_op jit(solution)/shard_map/ppermute | solution.py:26

commit v4 on v3

--- a/solution.py
+++ b/solution.py
@@ -54,16 +54,15 @@
             (own_swap, own_edge_swap, 0, 1 - core), (other_swap, other_edge_swap, 1, 1 - core),
         ):
             block = (half + dh) % 2 * 2 + owner
-            group.append((source.at[:, :, frames], x.at[:, 1:5, frames, block]))
-            for side in range(2):
-                group.append((ends.at[:, side, frames], x.at[:, 5 * side, frames, block]))
+            group.append((source.at[:, :, frames], x.at[:, 0:4, frames, block]))
+            group.append((ends.at[:, :, frames], x.at[:, 4:6, frames, block]))
         if tap is not None:
             taps = pl.ds(3 * tap, 3)
             for dz, source in ((0, w0), (1, w1), (3, w3)):
-                group.append((source.at[taps], w.at[taps, :, (z + 4 - dz) % 4]))
+                group.append((source.at[taps], w.at[:, tap, :, (z + 4 - dz) % 4]))
             for which, source in ((odd, near), (1 - odd, far)):
                 columns = pl.ds(pl.multiple_of(which * 256, 256), 256)
-                group.append((source.at[taps], w.at[taps, :, (z + 2) % 4, :, columns]))
+                group.append((source.at[taps], w.at[:, tap, :, (z + 2) % 4, :, columns]))
         start = sum(len(g) for g in groups)
         groups.append([fetch(start + i, *pair) for i, pair in enumerate(group)])
     for group in groups:
@@ -72,15 +71,6 @@
     moments[...] = jnp.zeros_like(moments)
     lane = lax.broadcasted_iota(jnp.int32, (128, 128), 1)
     inside = (lane >= 4) & (lane < 124)
-
-    def frame_tap(t, g, a):
-        summed = None
-        for b in range(3):
-            rhs = jnp.concatenate([x[:, b + g * 2 + h, t + a].reshape(512, 128) for h in range(2)], axis=1)
-            lhs = w[a * 3 + b].reshape(384, 512)
-            term = jnp.dot(lhs, rhs, preferred_element_type=F32)
-            summed = term if summed is None else summed + term
-        return summed
 
     def finish(t, g, summed):
         for h in range(2):
@@ -94,25 +84,28 @@
             for r, strip in enumerate((strip0, strip1, strip2, strip3)):
                 strip[g * 2 + h, t] = turned[pl.ds(3 + 30 * ((half * 2 + core) ^ r), 32), :].astype(BF16)
 
-    def frame(t, _):
+    for source in range(6):
+        if source < 4:
+            for copy in groups[source]:
+                copy.wait()
+        taps = range(max(0, source - 3), min(2, source) + 1)
         for g in range(2):
-            finish(t, g, frame_tap(t, g, 0) + frame_tap(t, g, 1) + frame_tap(t, g, 2))
-        return 0
-
-    for a in range(3):
-        for copy in groups[a]:
-            copy.wait()
-        for g in range(2):
-            term = frame_tap(0, g, a)
-            if a == 0:
-                acc[g] = term
-            elif a == 1:
-                acc[g] += term
-            else:
-                finish(0, g, acc[g] + term)
-    for copy in groups[3]:
-        copy.wait()
-    lax.fori_loop(1, 4, frame, 0)
+            summed = None
+            for b in range(3):
+                rows = [(4, 0, 1, 2, 3, 5)[b + g * 2 + h] for h in range(2)]
+                rhs = jnp.concatenate([x[:, r, source].reshape(512, 128) for r in rows], axis=1)
+                lhs = w[b, taps[0] : taps[-1] + 1].reshape(len(taps) * 384, 512)
+                term = jnp.dot(lhs, rhs, preferred_element_type=F32)
+                summed = term if summed is None else summed + term
+            for i, a in enumerate(taps):
+                t = source - a
+                part = summed[i * 384 : i * 384 + 384]
+                if a == 0:
+                    acc[t, g] = part
+                elif a == 1:
+                    acc[t, g] += part
+                else:
+                    finish(t, g, acc[t, g] + part)
     lane, group = (lax.broadcasted_iota(jnp.int32, (8, 128), i) for i in (1, 0))
     row = jnp.zeros((1, 128), F32)
     for i in range(2):
@@ -131,11 +124,11 @@
         out_specs=[pl.BlockSpec(memory_space=pltpu.VMEM)] * 5,
         scratch_shapes=[
             pltpu.VMEM((4, 6, 6, 4, 32, 128), BF16),
-            pltpu.VMEM((9, 3, 4, 32, 512), BF16),
-            pltpu.VMEM((2, 384, 256), F32),
+            pltpu.VMEM((3, 3, 3, 4, 32, 512), BF16),
+            pltpu.VMEM((4, 2, 384, 256), F32),
             pltpu.VMEM((128, 128), F32),
             pltpu.VMEM((2, 128, 128), F32),
-            pltpu.SemaphoreType.DMA((63,)),
+            pltpu.SemaphoreType.DMA((47,)),
         ],
         compiler_params=pltpu.CompilerParams(vmem_limit_bytes=56 * 1024 * 1024),
         cost_estimate=pl.CostEstimate(flops=7_200_000_000, bytes_accessed=9_000_000, transcendentals=0),
@@ -258,14 +251,17 @@
     multiply(1, w1)
     collapse(raw.at[0], w0)
     multiply(0, w0)
-    out[...] = acc[...].astype(BF16)
+    for pw in range(2):
+        for t in range(4):
+            rows = jnp.concatenate([acc[pw, r % 2, t, r // 2][None] for r in range(8)])
+            out[:, pw, t] = jnp.swapaxes(rows, 0, 1)[:30].astype(BF16)
 
 
 def conv_out(place, main, up, down, vectors, rim, bias, weight):
     whole = pl.BlockSpec(memory_space=pltpu.VMEM)
     return pl.pallas_call(
         conv_out_kernel,
-        out_shape=jax.ShapeDtypeStruct((2, 2, 4, 4, 32, 256), BF16),
+        out_shape=jax.ShapeDtypeStruct((30, 2, 4, 8, 256), BF16),
         in_specs=[pl.BlockSpec(memory_space=pltpu.SMEM)] + [whole] * 6 + [pl.BlockSpec(memory_space=pltpu.HBM)],
         out_specs=whole,
         scratch_shapes=[
@@ -355,7 +351,7 @@
     edges = jnp.stack([strip, chan == 0, chan == 15, row == 0, row == 7]).astype(jnp.int32)
     decoded = conv_out(edges, first, above, below, vectors, rim, conv_out_bias.reshape(1, 256),
                        conv_out_weight)
-    return decoded.transpose(4, 0, 2, 3, 1, 5)[:30].reshape(60, 4, 8, 256)
+    return decoded.reshape(60, 4, 8, 256)
 
 
 def solution(mesh):

time: 118 us -> 115 us (0.975)
  local copies, waits for them, and re-layouts: 9.59 us -> 6.68 us
    unnamed x23 -> x19, local copies, waits for them, and re-layouts: 3.19 us -> 2.18 us
  transfers between devices with their start and end apart: 22 -> 22, of which waited for: 8 -> 8; matrix products, arithmetic and copies ran while one was open for 5% -> 5% of each run, Pallas kernels for 5% -> 6%
where the time goes in v4:
time: 115 us; the launch traced here: 113 us
  starting transfers between devices  60.7 us (53%)
  Pallas kernels  28.6 us (25%)
  waiting for transfers between devices  12.9 us (11%)
  local copies, waits for them, and re-layouts  6.68 us (6%)
  other arithmetic  3.66 us (3%)
    ppermute x19, starting transfers between devices, send(): return lax.ppermute(array, BOTH, device_perm(move))  40.2 us
    ppermute x19, waiting for transfers between devices, send(): return lax.ppermute(array, BOTH, device_perm(move))  12.9 us
    pallas_call x1, Pallas kernels, conv_in(): pl.pallas_call(conv_in_kernel, out_shape=[jax.ShapeDtypeStruct((4, 4, 32,...  12.2 us
    all_to_all x2, starting transfers between devices, to_zones(): lax.all_to_all(pieces, 'chan', split_axis=0, concat_axis=0, axis_index_gr...  11.1 us
    pallas_call x1, Pallas kernels, conv_out(): pl.pallas_call(conv_out_kernel, out_shape=jax.ShapeDtypeStruct((30, 2, 4,...  10.1 us
    all_to_all x1, starting transfers between devices, body(): lax.all_to_all(stats, BOTH, split_axis=0, concat_axis=0, tiled=True)  9.44 us
    pallas_call x1, Pallas kernels, conv_rim(): pl.pallas_call(rim_kernel, out_shape=jax.ShapeDtypeStruct((2, 2, 2, 4, 32...  6.28 us
  transfers between devices with their start and end apart: 22, of which 8 were waited for; matrix products, arithmetic and copies ran while one was open for 5% of the time, Pallas kernels for 6%

profile of v4, /device:TPU:2, one launch (start us, length us, event | category | flops | bytes accessed | tf_op | source)
XLA Modules:
  0.0 113.1 jit_solution(5873510889179928587)
XLA Ops:
  0.0 1.3 %copy.28 = bf16[480,6,4,32]{0,3,1,2:T(8,128)(2,1)S(1)} copy(bf16[480,6,4,32]{0,3,2,1:T(8,128)(2,1)} %param.8) | data formatting | bytes 1474560 | tf_op args[0]
  1.3 0.3 fusion
  1.6 1.0 pad_maximum_fusion
  2.6 5.3 %all-to-all-start = ((bf16[4,4,6,32,128]{4,3,2,1,0:T(8,128)(2,1)}), bf16[4,4,6,32,128]{4,3,2,1,0:T(8,128)(2,1)}, u32[]{:S(2)}, u32[]{:S(2)}) async-start(bf16[4,4,6,32,128]{4,3,2,1,0:T(8,128)(2,1)} %pad_maximum_fusion), calls=%async_computation | async-start | bytes 1572864 | tf_op jit(solution)/shard_map/all_to_all | solution.py:305
  7.9 0.1 pad_bitcast_fusion
  8.0 0.3 fusion.9
  8.4 0.2 pad_slice_fusion.1
  8.6 3.5 %collective-permute-start.1 = (bf16[320,512]{1,0:T(8,128)(2,1)S(1)}, bf16[320,512]{1,0:T(8,128)(2,1)S(1)}, u32[]{:S(2)}, u32[]{:S(2)}) collective-permute-start(bf16[320,512]{1,0:T(8,128)(2,1)S(1)} %pad_maximum_fusion.3), channel_id=1, source_target_pairs={{0,1},{1,2},{2,3},{3,4},{4,5},{5,6},{6,7},{8,9},{9,10},{10,11},{11... | collective-permute-start | bytes 983048 | tf_op jit(solution)/shard_map/ppermute | solution.py:26
  12.2 4.5 %collective-permute-start.2 = (bf16[320,512]{1,0:T(8,128)(2,1)S(1)}, bf16[320,512]{1,0:T(8,128)(2,1)S(1)}, u32[]{:S(2)}, u32[]{:S(2)}) collective-permute-start(bf16[320,512]{1,0:T(8,128)(2,1)S(1)} %pad_maximum_fusion.4), channel_id=1, source_target_pairs={{1,0},{2,1},{3,2},{4,3},{5,4},{6,5},{7,6},{9,8},{10,9},{11,10},{12... | collective-permute-start | bytes 983048 | tf_op jit(solution)/shard_map/ppermute | solution.py:26
  16.7 1.0 constant_dynamic-slice_fusion
  17.7 3.6 %collective-permute-start.8 = (bf16[9,3,32,256]{3,2,1,0:T(8,128)(2,1)S(1)}, bf16[9,3,32,256]{3,2,1,0:T(8,128)(2,1)}, u32[]{:S(2)}, u32[]{:S(2)}) collective-permute-start(bf16[9,3,32,256]{3,2,1,0:T(8,128)(2,1)S(1)} %constant_dynamic-slice_fusion), channel_id=1, source_target_pairs={{0,64},{1,65},{2,66},{3,67},{4,68},{5,69},{6,70},{7,71},{8,72},{9,... | collective-permute-start | bytes 1327112 | tf_op jit(solution)/shard_map/ppermute | solution.py:26
  21.3 2.1 %collective-permute-start = (bf16[4,4,6,32,128]{4,3,2,1,0:T(8,128)(2,1)}, bf16[4,4,6,32,128]{4,3,2,1,0:T(8,128)(2,1)}, u32[]{:S(2)}, u32[]{:S(2)}) collective-permute-start(bf16[4,4,6,32,128]{4,3,2,1,0:T(8,128)(2,1)} %all-to-all-done.own), channel_id=1, source_target_pairs={{0,16},{1,17},{2,18},{3,19},{4,20},{5,21},{6,22},{7,23},{8,24},{9,... | collective-permute-start | bytes 2359304 | tf_op jit(solution)/shard_map/ppermute | solution.py:26
  23.4 0.0 collective-permute-done.1
  23.5 0.3 collective-permute-done.2
  23.8 0.2 fusion.5
  24.0 0.8 pad_maximum_fusion.2
  24.8 5.8 %all-to-all-start.1 = ((bf16[4,2,6,32,128]{4,3,2,1,0:T(8,128)(2,1)}), bf16[4,2,6,32,128]{4,3,2,1,0:T(8,128)(2,1)S(1)}, u32[]{:S(2)}, u32[]{:S(2)}) async-start(bf16[4,2,6,32,128]{4,3,2,1,0:T(8,128)(2,1)} %pad_maximum_fusion.2), calls=%async_computation.1 | async-start | bytes 786432 | tf_op jit(solution)/shard_map/all_to_all | solution.py:305
  30.6 2.1 %collective-permute-start.6 = (bf16[9,3,32,512]{3,2,1,0:T(8,128)(2,1)}, bf16[9,3,32,512]{3,2,1,0:T(8,128)(2,1)}, u32[]{:S(2)}, u32[]{:S(2)}) collective-permute-start(bf16[9,3,32,512]{3,2,1,0:T(8,128)(2,1)} %bitcast.80), channel_id=1, source_target_pairs={{0,32},{1,33},{2,34},{3,35},{4,36},{5,37},{6,38},{7,39},{8,40},{9,... | collective-permute-start | bytes 2654216 | tf_op jit(solution)/shard_map/ppermute | solution.py:26
  32.7 1.3 %collective-permute-start.7 = (bf16[9,3,32,512]{3,2,1,0:T(8,128)(2,1)}, bf16[9,3,32,512]{3,2,1,0:T(8,128)(2,1)}, u32[]{:S(2)}, u32[]{:S(2)}) collective-permute-start(bf16[9,3,32,512]{3,2,1,0:T(8,128)(2,1)} %bitcast.81), channel_id=1, source_target_pairs={{0,96},{1,97},{2,98},{3,99},{4,100},{5,101},{6,102},{7,103},{8,104... | collective-permute-start | bytes 2654216 | tf_op jit(solution)/shard_map/ppermute | solution.py:26
  34.0 1.3 %collective-permute-start.3 = (bf16[2,10,512]{2,1,0:T(8,128)(2,1)S(1)}, bf16[2,10,512]{2,1,0:T(8,128)(2,1)S(1)}, u32[]{:S(2)}, u32[]{:S(2)}) collective-permute-start(bf16[2,10,512]{2,1,0:T(8,128)(2,1)S(1)} %pad_maximum_fusion.6), channel_id=1, source_target_pairs={{0,8},{1,9},{2,10},{3,11},{4,12},{5,13},{6,14},{7,15},{8,16},{9,17... | collective-permute-start | bytes 61448 | tf_op jit(solution)/shard_map/ppermute | solution.py:26
  35.4 0.8 collective-permute-done.3.before
  36.2 1.3 %collective-permute-start.4 = (bf16[2,10,512]{2,1,0:T(8,128)(2,1)S(1)}, bf16[2,10,512]{2,1,0:T(8,128)(2,1)S(1)}, u32[]{:S(2)}, u32[]{:S(2)}) collective-permute-start(bf16[2,10,512]{2,1,0:T(8,128)(2,1)S(1)} %pad_maximum_fusion.7), channel_id=1, source_target_pairs={{8,0},{9,1},{10,2},{11,3},{12,4},{13,5},{14,6},{15,7},{16,8},{17,9... | collective-permute-start | bytes 61448 | tf_op jit(solution)/shard_map/ppermute | solution.py:26
  37.5 0.6 copy.22.rim
  38.0 0.0 collective-permute-done.8.near
  38.1 0.1 collective-permute-start.9
  38.1 3.9 %collective-permute-done.4.after = bf16[2,10,512]{2,1,0:T(8,128)(2,1)S(1)} collective-permute-done((bf16[2,10,512]{2,1,0:T(8,128)(2,1)S(1)}, bf16[2,10,512]{2,1,0:T(8,128)(2,1)S(1)}, u32[]{:S(2)}, u32[]{:S(2)}) %collective-permute-start.4) | collective-permute-done | bytes 20512 | tf_op jit(solution)/shard_map/ppermute | solution.py:26
  42.0 5.3 %collective-permute-start.10 = (bf16[4,4,6,32,128]{4,3,2,1,0:T(8,128)(2,1)}, bf16[4,4,6,32,128]{4,3,2,1,0:T(8,128)(2,1)}, u32[]{:S(2)}, u32[]{:S(2)}) collective-permute-start(bf16[4,4,6,32,128]{4,3,2,1,0:T(8,128)(2,1)} %all-to-all-done.own), channel_id=1, source_target_pairs={{0,8},{1,9},{2,10},{3,11},{4,12},{5,13},{6,14},{7,15},{8,0},{9,1},... | collective-permute-start | bytes 2359304 | tf_op jit(solution)/shard_map/ppermute | solution.py:26
  47.3 0.0 collective-permute-done.other
  47.3 2.6 %collective-permute-start.5 = (bf16[4,2,6,32,128]{4,3,2,1,0:T(8,128)(2,1)S(1)}, bf16[4,2,6,32,128]{4,3,2,1,0:T(8,128)(2,1)S(1)}, u32[]{:S(2)}, u32[]{:S(2)}) collective-permute-start(bf16[4,2,6,32,128]{4,3,2,1,0:T(8,128)(2,1)S(1)} %all-to-all-done.1.own_edge), channel_id=1, source_target_pairs={{0,16},{1,17},{2,18},{3,19},{4,20},{5,21},{6,22},{7,23},{8,24},{9,... | collective-permute-start | bytes 1179656 | tf_op jit(solution)/shard_map/ppermute | solution.py:26
  49.9 6.3 %conv_rim.1.rim = f32[2,2,2,4,32,256]{5,4,3,2,1,0:T(8,128)S(1)} custom-call(bf16[2,8,64,512]{3,2,1,0:T(8,128)(2,1)S(1)} %copy.22.rim, bf16[2,64,512]{2,1,0:T(8,128)(2,1)S(1)} %bitcast.66, bf16[2,64,512]{2,1,0:T(8,128)(2,1)S(1)} %bitcast.68, bf16[2,10,512]{2,1,0:T(8,128)(2,1)S(1)} %collective-permute-done.3.before, ...), custom_call_target="tpu_custom_call" | custom-call | flops 7200000000 | bytes 8000000 | tf_op jit(solution)/shard_map/conv_rim/pallas_call | solution.py:186
  56.2 0.0 collective-permute-done.9.far
  56.2 3.7 %collective-permute-done.5.other_edge = bf16[4,2,6,32,128]{4,3,2,1,0:T(8,128)(2,1)S(1)} collective-permute-done((bf16[4,2,6,32,128]{4,3,2,1,0:T(8,128)(2,1)S(1)}, bf16[4,2,6,32,128]{4,3,2,1,0:T(8,128)(2,1)S(1)}, u32[]{:S(2)}, u32[]{:S(2)}) %collective-permute-start.5) | collective-permute-done | bytes 393248 | tf_op jit(solution)/shard_map/ppermute | solution.py:26
  59.9 0.1 collective-permute-start.11
  60.0 0.5 collective-permute-start.12
  60.5 0.1 collective-permute-start.13
  60.6 0.1 reshape.70
  60.8 0.1 broadcast_in_dim.13
  60.8 0.6 pad_add_fusion.place
  61.5 1.9 %collective-permute-done.12.own_edge_swap = bf16[4,2,6,32,128]{4,3,2,1,0:T(8,128)(2,1)S(1)} collective-permute-done((bf16[4,2,6,32,128]{4,3,2,1,0:T(8,128)(2,1)S(1)}, bf16[4,2,6,32,128]{4,3,2,1,0:T(8,128)(2,1)S(1)}, u32[]{:S(2)}, u32[]{:S(2)}) %collective-permute-start.12) | collective-permute-done | bytes 393248 | tf_op jit(solution)/shard_map/ppermute | solution.py:26
  63.3 0.2 collective-permute-done.13.other_edge_swap
  63.6 0.9 copy-done.6
  64.5 0.7 broadcast_in_dim.14.bias
  65.2 0.0 copy-start
  65.2 12.2 %conv_in.1 = (bf16[4,4,32,128]{3,2,1,0:T(8,128)(2,1)}, bf16[4,4,32,128]{3,2,1,0:T(8,128)(2,1)}, bf16[4,4,32,128]{3,2,1,0:T(8,128)(2,1)}, bf16[4,4,32,128]{3,2,1,0:T(8,128)(2,1)}, f32[128,128]{1,0:T(8,128)}) custom-call(s32[4]{0:T(128)} %pad_add_fusion.place, bf16[4,4,6,32,128]{4,3,2,1,0:T(8,128)(2,1)} %all-to-all-done.own, ...), custom_call_target="tpu_custom_call" | custom-call | flops 7200000000 | bytes 9000000 | tf_op jit(solution)/shard_map/conv_in/pallas_call | solution.py:119
  77.4 0.2 collective-permute-start.14
  77.6 2.5 %collective-permute-start.16 = (bf16[4,4,32,128]{3,2,1,0:T(8,128)(2,1)}, bf16[4,4,32,128]{3,2,1,0:T(8,128)(2,1)S(1)}, u32[]{:S(2)}, u32[]{:S(2)}) collective-permute-start(bf16[4,4,32,128]{3,2,1,0:T(8,128)(2,1)} %get-tuple-element.38), channel_id=1, source_target_pairs={{0,24},{1,25},{2,26},{3,27},{4,28},{5,29},{6,30},{7,31},{8,16},{9,... | collective-permute-start | bytes 393224 | tf_op jit(solution)/shard_map/ppermute | solution.py:26
  80.1 1.0 collective-permute-start.15
  81.1 0.1 reshape.74
  81.2 0.1 reshape.75
  81.3 0.1 reshape.76
  81.4 0.1 stack_reshape.15
  81.5 0.1 stack.109.place
  81.5 9.4 %all-to-all-start.2 = ((f32[128,1,128]{2,1,0:T(1,128)}), f32[128,1,128]{2,1,0:T(1,128)S(1)}, u32[]{:S(2)}, u32[]{:S(2)}) async-start(f32[128,1,128]{2,1,0:T(1,128)} %bitcast.87), calls=%async_computation.2 | async-start | bytes 131072 | tf_op jit(solution)/shard_map/all_to_all | solution.py:341
  91.0 1.0 pad_maximum_fusion.1
  92.1 3.4 %collective-permute-start.17 = (bf16[4,4,32,128]{3,2,1,0:T(8,128)(2,1)S(1)}, bf16[4,4,32,128]{3,2,1,0:T(8,128)(2,1)S(1)}, u32[]{:S(2)}, u32[]{:S(2)}) collective-permute-start(bf16[4,4,32,128]{3,2,1,0:T(8,128)(2,1)S(1)} %get-tuple-element.52), channel_id=1, source_target_pairs={{0,1},{1,2},{2,3},{3,4},{4,5},{5,6},{6,7},{8,9},{9,10},{10,11},{11... | collective-permute-start | bytes 393224 | tf_op jit(solution)/shard_map/ppermute | solution.py:26
  95.4 4.8 %collective-permute-start.18 = (bf16[4,4,32,128]{3,2,1,0:T(8,128)(2,1)S(1)}, bf16[4,4,32,128]{3,2,1,0:T(8,128)(2,1)S(1)}, u32[]{:S(2)}, u32[]{:S(2)}) collective-permute-start(bf16[4,4,32,128]{3,2,1,0:T(8,128)(2,1)S(1)} %get-tuple-element.51), channel_id=1, source_target_pairs={{1,0},{2,1},{3,2},{4,3},{5,4},{6,5},{7,6},{9,8},{10,9},{11,10},{12... | collective-permute-start | bytes 393224 | tf_op jit(solution)/shard_map/ppermute | solution.py:26
  100.3 0.1 reshape.72
  100.4 0.1 broadcast_in_dim.15
  100.5 0.1 stack_reshape.14
  100.5 0.1 broadcast_in_dim.16
  100.6 0.1 reshape.73
  100.8 0.8 collective-permute-done.17.up
  101.6 1.2 %collective-permute-done.18.down = bf16[4,4,32,128]{3,2,1,0:T(8,128)(2,1)S(1)} collective-permute-done((bf16[4,4,32,128]{3,2,1,0:T(8,128)(2,1)S(1)}, bf16[4,4,32,128]{3,2,1,0:T(8,128)(2,1)S(1)}, u32[]{:S(2)}, u32[]{:S(2)}) %collective-permute-start.18) | collective-permute-done | bytes 131104 | tf_op jit(solution)/shard_map/ppermute | solution.py:26
  102.8 10.1 %conv_out.1 = bf16[30,2,4,8,256]{4,3,2,1,0:T(8,128)(2,1)} custom-call(s32[5]{0:T(128)S(1)} %stack.109.place, bf16[4,4,4,32,128]{4,3,2,1,0:T(8,128)(2,1)S(1)} %copy.26.main, bf16[4,4,32,128]{3,2,1,0:T(8,128)(2,1)S(1)} %collective-permute-done.17.up, bf16[4,4,32,128]{3,2,1,0:T(8,128)(2,1)S(1)} %collective-permute-done.18.down, ...), custom_call_target="tpu_custom_call" | custom-call | flops 4899999744 | bytes 18000000 | tf_op jit(solution)/shard_map/conv_out/pallas_call | solution.py:262
  (50 shorter events, 0.5 us)
Async XLA Ops:
  0.0 7.9 %copy-start.1 = (bf16[60,2,8,512]{3,2,1,0:T(8,128)(2,1)S(1)}, bf16[60,2,8,512]{3,2,1,0:T(8,128)(2,1)}, u32[]{:S(2)}) copy-start(bf16[60,2,8,512]{3,2,1,0:T(8,128)(2,1)} %param.13) | copy-start | bytes 2949124
  2.6 18.7 %all-to-all-start = ((bf16[4,4,6,32,128]{4,3,2,1,0:T(8,128)(2,1)}), bf16[4,4,6,32,128]{4,3,2,1,0:T(8,128)(2,1)}, u32[]{:S(2)}, u32[]{:S(2)}) async-start(bf16[4,4,6,32,128]{4,3,2,1,0:T(8,128)(2,1)} %pad_maximum_fusion), calls=%async_computation | async-start | bytes 1572864 | tf_op jit(solution)/shard_map/all_to_all | solution.py:305
  8.6 14.9 %collective-permute-start.1 = (bf16[320,512]{1,0:T(8,128)(2,1)S(1)}, bf16[320,512]{1,0:T(8,128)(2,1)S(1)}, u32[]{:S(2)}, u32[]{:S(2)}) collective-permute-start(bf16[320,512]{1,0:T(8,128)(2,1)S(1)} %pad_maximum_fusion.3), channel_id=1, source_target_pairs={{0,1},{1,2},{2,3},{3,4},{4,5},{5,6},{6,7},{8,9},{9,10},{10,11},{11... | collective-permute-start | bytes 983048 | tf_op jit(solution)/shard_map/ppermute | solution.py:26
  12.2 11.6 %collective-permute-start.2 = (bf16[320,512]{1,0:T(8,128)(2,1)S(1)}, bf16[320,512]{1,0:T(8,128)(2,1)S(1)}, u32[]{:S(2)}, u32[]{:S(2)}) collective-permute-start(bf16[320,512]{1,0:T(8,128)(2,1)S(1)} %pad_maximum_fusion.4), channel_id=1, source_target_pairs={{1,0},{2,1},{3,2},{4,3},{5,4},{6,5},{7,6},{9,8},{10,9},{11,10},{12... | collective-permute-start | bytes 983048 | tf_op jit(solution)/shard_map/ppermute | solution.py:26
  17.7 20.3 %collective-permute-start.8 = (bf16[9,3,32,256]{3,2,1,0:T(8,128)(2,1)S(1)}, bf16[9,3,32,256]{3,2,1,0:T(8,128)(2,1)}, u32[]{:S(2)}, u32[]{:S(2)}) collective-permute-start(bf16[9,3,32,256]{3,2,1,0:T(8,128)(2,1)S(1)} %constant_dynamic-slice_fusion), channel_id=1, source_target_pairs={{0,64},{1,65},{2,66},{3,67},{4,68},{5,69},{6,70},{7,71},{8,72},{9,... | collective-permute-start | bytes 1327112 | tf_op jit(solution)/shard_map/ppermute | solution.py:26
  21.3 26.0 %collective-permute-start = (bf16[4,4,6,32,128]{4,3,2,1,0:T(8,128)(2,1)}, bf16[4,4,6,32,128]{4,3,2,1,0:T(8,128)(2,1)}, u32[]{:S(2)}, u32[]{:S(2)}) collective-permute-start(bf16[4,4,6,32,128]{4,3,2,1,0:T(8,128)(2,1)} %all-to-all-done.own), channel_id=1, source_target_pairs={{0,16},{1,17},{2,18},{3,19},{4,20},{5,21},{6,22},{7,23},{8,24},{9,... | collective-permute-start | bytes 2359304 | tf_op jit(solution)/shard_map/ppermute | solution.py:26
  24.8 22.6 %all-to-all-start.1 = ((bf16[4,2,6,32,128]{4,3,2,1,0:T(8,128)(2,1)}), bf16[4,2,6,32,128]{4,3,2,1,0:T(8,128)(2,1)S(1)}, u32[]{:S(2)}, u32[]{:S(2)}) async-start(bf16[4,2,6,32,128]{4,3,2,1,0:T(8,128)(2,1)} %pad_maximum_fusion.2), calls=%async_computation.1 | async-start | bytes 786432 | tf_op jit(solution)/shard_map/all_to_all | solution.py:305
  30.6 29.3 %collective-permute-start.6 = (bf16[9,3,32,512]{3,2,1,0:T(8,128)(2,1)}, bf16[9,3,32,512]{3,2,1,0:T(8,128)(2,1)}, u32[]{:S(2)}, u32[]{:S(2)}) collective-permute-start(bf16[9,3,32,512]{3,2,1,0:T(8,128)(2,1)} %bitcast.80), channel_id=1, source_target_pairs={{0,32},{1,33},{2,34},{3,35},{4,36},{5,37},{6,38},{7,39},{8,40},{9,... | collective-permute-start | bytes 2654216 | tf_op jit(solution)/shard_map/ppermute | solution.py:26
  32.7 27.2 %collective-permute-start.7 = (bf16[9,3,32,512]{3,2,1,0:T(8,128)(2,1)}, bf16[9,3,32,512]{3,2,1,0:T(8,128)(2,1)}, u32[]{:S(2)}, u32[]{:S(2)}) collective-permute-start(bf16[9,3,32,512]{3,2,1,0:T(8,128)(2,1)} %bitcast.81), channel_id=1, source_target_pairs={{0,96},{1,97},{2,98},{3,99},{4,100},{5,101},{6,102},{7,103},{8,104... | collective-permute-start | bytes 2654216 | tf_op jit(solution)/shard_map/ppermute | solution.py:26
  34.0 2.1 %collective-permute-start.3 = (bf16[2,10,512]{2,1,0:T(8,128)(2,1)S(1)}, bf16[2,10,512]{2,1,0:T(8,128)(2,1)S(1)}, u32[]{:S(2)}, u32[]{:S(2)}) collective-permute-start(bf16[2,10,512]{2,1,0:T(8,128)(2,1)S(1)} %pad_maximum_fusion.6), channel_id=1, source_target_pairs={{0,8},{1,9},{2,10},{3,11},{4,12},{5,13},{6,14},{7,15},{8,16},{9,17... | collective-permute-start | bytes 61448 | tf_op jit(solution)/shard_map/ppermute | solution.py:26
  36.2 5.9 %collective-permute-start.4 = (bf16[2,10,512]{2,1,0:T(8,128)(2,1)S(1)}, bf16[2,10,512]{2,1,0:T(8,128)(2,1)S(1)}, u32[]{:S(2)}, u32[]{:S(2)}) collective-permute-start(bf16[2,10,512]{2,1,0:T(8,128)(2,1)S(1)} %pad_maximum_fusion.7), channel_id=1, source_target_pairs={{8,0},{9,1},{10,2},{11,3},{12,4},{13,5},{14,6},{15,7},{16,8},{17,9... | collective-permute-start | bytes 61448 | tf_op jit(solution)/shard_map/ppermute | solution.py:26
  38.1 18.2 %collective-permute-start.9 = (bf16[9,3,32,256]{3,2,1,0:T(8,128)(2,1)}, bf16[9,3,32,256]{3,2,1,0:T(8,128)(2,1)}, u32[]{:S(2)}, u32[]{:S(2)}) collective-permute-start(bf16[9,3,32,256]{3,2,1,0:T(8,128)(2,1)} %collective-permute-done.8.near), channel_id=1, source_target_pairs={{0,1},{1,0},{2,3},{3,2},{4,5},{5,4},{6,7},{7,6},{8,9},{9,8},{10,11... | collective-permute-start | bytes 1327112 | tf_op jit(solution)/shard_map/ppermute | solution.py:26
  42.0 21.3 %collective-permute-start.10 = (bf16[4,4,6,32,128]{4,3,2,1,0:T(8,128)(2,1)}, bf16[4,4,6,32,128]{4,3,2,1,0:T(8,128)(2,1)}, u32[]{:S(2)}, u32[]{:S(2)}) collective-permute-start(bf16[4,4,6,32,128]{4,3,2,1,0:T(8,128)(2,1)} %all-to-all-done.own), channel_id=1, source_target_pairs={{0,8},{1,9},{2,10},{3,11},{4,12},{5,13},{6,14},{7,15},{8,0},{9,1},... | collective-permute-start | bytes 2359304 | tf_op jit(solution)/shard_map/ppermute | solution.py:26
  47.3 12.7 %copy-start.2 = (bf16[4,2,6,32,128]{4,3,2,1,0:T(8,128)(2,1)}, bf16[4,2,6,32,128]{4,3,2,1,0:T(8,128)(2,1)S(1)}, u32[]{:S(2)}) copy-start(bf16[4,2,6,32,128]{4,3,2,1,0:T(8,128)(2,1)S(1)} %all-to-all-done.1.own_edge) | copy-start | bytes 1179652
  47.3 12.6 %collective-permute-start.5 = (bf16[4,2,6,32,128]{4,3,2,1,0:T(8,128)(2,1)S(1)}, bf16[4,2,6,32,128]{4,3,2,1,0:T(8,128)(2,1)S(1)}, u32[]{:S(2)}, u32[]{:S(2)}) collective-permute-start(bf16[4,2,6,32,128]{4,3,2,1,0:T(8,128)(2,1)S(1)} %all-to-all-done.1.own_edge), channel_id=1, source_target_pairs={{0,16},{1,17},{2,18},{3,19},{4,20},{5,21},{6,22},{7,23},{8,24},{9,... | collective-permute-start | bytes 1179656 | tf_op jit(solution)/shard_map/ppermute | solution.py:26
  49.9 10.7 %copy-start.3 = (f32[512]{0:T(512)S(1)}, f32[512]{0:T(512)}, u32[]{:S(2)}) copy-start(f32[512]{0:T(512)} %param.10) | copy-start | bytes 6148
  59.9 5.2 %copy-start.7 = (bf16[4,2,6,32,128]{4,3,2,1,0:T(8,128)(2,1)}, bf16[4,2,6,32,128]{4,3,2,1,0:T(8,128)(2,1)S(1)}, u32[]{:S(2)}) copy-start(bf16[4,2,6,32,128]{4,3,2,1,0:T(8,128)(2,1)S(1)} %collective-permute-done.5.other_edge) | copy-start | bytes 1179652
  59.9 3.6 %collective-permute-start.11 = (bf16[4,4,6,32,128]{4,3,2,1,0:T(8,128)(2,1)}, bf16[4,4,6,32,128]{4,3,2,1,0:T(8,128)(2,1)S(1)}, u32[]{:S(2)}, u32[]{:S(2)}) collective-permute-start(bf16[4,4,6,32,128]{4,3,2,1,0:T(8,128)(2,1)} %collective-permute-done.other), channel_id=1, source_target_pairs={{0,8},{1,9},{2,10},{3,11},{4,12},{5,13},{6,14},{7,15},{8,0},{9,1},... | collective-permute-start | bytes 2359304 | tf_op jit(solution)/shard_map/ppermute | solution.py:26
  60.0 3.3 %collective-permute-start.12 = (bf16[4,2,6,32,128]{4,3,2,1,0:T(8,128)(2,1)S(1)}, bf16[4,2,6,32,128]{4,3,2,1,0:T(8,128)(2,1)S(1)}, u32[]{:S(2)}, u32[]{:S(2)}) collective-permute-start(bf16[4,2,6,32,128]{4,3,2,1,0:T(8,128)(2,1)S(1)} %all-to-all-done.1.own_edge), channel_id=1, source_target_pairs={{0,8},{1,9},{2,10},{3,11},{4,12},{5,13},{6,14},{7,15},{8,0},{9,1},... | collective-permute-start | bytes 1179656 | tf_op jit(solution)/shard_map/ppermute | solution.py:26
  60.5 3.0 %collective-permute-start.13 = (bf16[4,2,6,32,128]{4,3,2,1,0:T(8,128)(2,1)S(1)}, bf16[4,2,6,32,128]{4,3,2,1,0:T(8,128)(2,1)}, u32[]{:S(2)}, u32[]{:S(2)}) collective-permute-start(bf16[4,2,6,32,128]{4,3,2,1,0:T(8,128)(2,1)S(1)} %collective-permute-done.5.other_edge), channel_id=1, source_target_pairs={{0,8},{1,9},{2,10},{3,11},{4,12},{5,13},{6,14},{7,15},{8,0},{9,1},... | collective-permute-start | bytes 1179656 | tf_op jit(solution)/shard_map/ppermute | solution.py:26
  63.3 1.8 %copy-start.8 = (bf16[4,2,6,32,128]{4,3,2,1,0:T(8,128)(2,1)}, bf16[4,2,6,32,128]{4,3,2,1,0:T(8,128)(2,1)S(1)}, u32[]{:S(2)}) copy-start(bf16[4,2,6,32,128]{4,3,2,1,0:T(8,128)(2,1)S(1)} %collective-permute-done.12.own_edge_swap) | copy-start | bytes 1179652
  63.6 0.9 copy-start.6
  65.2 15.9 %copy-start.4 = (f32[512]{0:T(512)S(1)}, f32[512]{0:T(512)}, u32[]{:S(2)}) copy-start(f32[512]{0:T(512)} %param.11) | copy-start | bytes 6148
  65.2 16.1 %copy-start.5 = (f32[512]{0:T(512)S(1)}, f32[512]{0:T(512)}, u32[]{:S(2)}) copy-start(f32[512]{0:T(512)} %param.12) | copy-start | bytes 6148
  65.2 37.6 %copy-start = (f32[256]{0:T(256)S(1)}, f32[256]{0:T(256)}, u32[]{:S(2)}) copy-start(f32[256]{0:T(256)} %param.15) | copy-start | bytes 3076
  77.4 4.2 %collective-permute-start.14 = (bf16[4,4,32,128]{3,2,1,0:T(8,128)(2,1)}, bf16[4,4,32,128]{3,2,1,0:T(8,128)(2,1)S(1)}, u32[]{:S(2)}, u32[]{:S(2)}) collective-permute-start(bf16[4,4,32,128]{3,2,1,0:T(8,128)(2,1)} %get-tuple-element.35), channel_id=1, source_target_pairs={{0,8},{1,9},{2,10},{3,11},{4,12},{5,13},{6,14},{7,15},{8,0},{9,1},... | collective-permute-start | bytes 393224 | tf_op jit(solution)/shard_map/ppermute | solution.py:26
  77.6 13.4 %collective-permute-start.16 = (bf16[4,4,32,128]{3,2,1,0:T(8,128)(2,1)}, bf16[4,4,32,128]{3,2,1,0:T(8,128)(2,1)S(1)}, u32[]{:S(2)}, u32[]{:S(2)}) collective-permute-start(bf16[4,4,32,128]{3,2,1,0:T(8,128)(2,1)} %get-tuple-element.38), channel_id=1, source_target_pairs={{0,24},{1,25},{2,26},{3,27},{4,28},{5,29},{6,30},{7,31},{8,16},{9,... | collective-permute-start | bytes 393224 | tf_op jit(solution)/shard_map/ppermute | solution.py:26
  80.1 10.9 %collective-permute-start.15 = (bf16[4,4,32,128]{3,2,1,0:T(8,128)(2,1)}, bf16[4,4,32,128]{3,2,1,0:T(8,128)(2,1)S(1)}, u32[]{:S(2)}, u32[]{:S(2)}) collective-permute-start(bf16[4,4,32,128]{3,2,1,0:T(8,128)(2,1)} %get-tuple-element.37), channel_id=1, source_target_pairs={{0,16},{1,17},{2,18},{3,19},{4,20},{5,21},{6,22},{7,23},{8,24},{9,... | collective-permute-start | bytes 393224 | tf_op jit(solution)/shard_map/ppermute | solution.py:26
  81.5 18.7 %all-to-all-start.2 = ((f32[128,1,128]{2,1,0:T(1,128)}), f32[128,1,128]{2,1,0:T(1,128)S(1)}, u32[]{:S(2)}, u32[]{:S(2)}) async-start(f32[128,1,128]{2,1,0:T(1,128)} %bitcast.87), calls=%async_computation.2 | async-start | bytes 131072 | tf_op jit(solution)/shard_map/all_to_all | solution.py:341
  92.1 9.6 %collective-permute-start.17 = (bf16[4,4,32,128]{3,2,1,0:T(8,128)(2,1)S(1)}, bf16[4,4,32,128]{3,2,1,0:T(8,128)(2,1)S(1)}, u32[]{:S(2)}, u32[]{:S(2)}) collective-permute-start(bf16[4,4,32,128]{3,2,1,0:T(8,128)(2,1)S(1)} %get-tuple-element.52), channel_id=1, source_target_pairs={{0,1},{1,2},{2,3},{3,4},{4,5},{5,6},{6,7},{8,9},{9,10},{10,11},{11... | collective-permute-start | bytes 393224 | tf_op jit(solution)/shard_map/ppermute | solution.py:26
  95.4 7.4 %collective-permute-start.18 = (bf16[4,4,32,128]{3,2,1,0:T(8,128)(2,1)S(1)}, bf16[4,4,32,128]{3,2,1,0:T(8,128)(2,1)S(1)}, u32[]{:S(2)}, u32[]{:S(2)}) collective-permute-start(bf16[4,4,32,128]{3,2,1,0:T(8,128)(2,1)S(1)} %get-tuple-element.51), channel_id=1, source_target_pairs={{1,0},{2,1},{3,2},{4,3},{5,4},{6,5},{7,6},{9,8},{10,9},{11,10},{12... | collective-permute-start | bytes 393224 | tf_op jit(solution)/shard_map/ppermute | solution.py:26

commit v5 on v4

--- a/solution.py
+++ b/solution.py
@@ -323,8 +323,10 @@
     before, after = send(column(59), to_chan(1)), send(column(0), to_chan(-1))
     other, before, after = lax.optimization_barrier((other, before, after))
     rim = conv_rim(rim, rim_above, rim_below, before, after, conv_out_weight)
+    rim, own_late = lax.optimization_barrier((rim, own))
+    own_swap = send(own_late, flip_core)
     other, other_edge, w1, w3, far, rim = lax.optimization_barrier((other, other_edge, w1, w3, far, rim))
-    parts = [own, other, send(own, flip_core), send(other, flip_core),
+    parts = [own, other, own_swap, send(other, flip_core),
              own_edge, other_edge, send(own_edge, flip_core), send(other_edge, flip_core)]
     weights = [weights, w1, w3, near, far]
 

time: 115 us -> 113 us (0.983)
  waiting for transfers between devices: 12.9 us -> 9.48 us
  starting transfers between devices: 60.7 us -> 62.5 us
    ppermute x19, waiting for transfers between devices: 12.9 us -> 9.47 us  [send(): return lax.ppermute(array, BOTH, device_perm(move))]
    all_to_all x1, starting transfers between devices: 9.44 us -> 10.9 us  [body(): lax.all_to_all(stats, BOTH, split_axis=0, concat_axis=0, tiled=True)]
  transfers between devices with their start and end apart: 22 -> 22, of which waited for: 8 -> 8; matrix products, arithmetic and copies ran while one was open for 5% -> 6% of each run, Pallas kernels for 6% -> 6%
where the time goes in v5:
time: 113 us; the launch traced here: 111 us
  starting transfers between devices  62.5 us (55%)
  Pallas kernels  28.6 us (25%)
  waiting for transfers between devices  9.48 us (8%)
  local copies, waits for them, and re-layouts  6.48 us (6%)
  other arithmetic  3.66 us (3%)
    ppermute x19, starting transfers between devices, send(): return lax.ppermute(array, BOTH, device_perm(move))  40.5 us
    pallas_call x1, Pallas kernels, conv_in(): pl.pallas_call(conv_in_kernel, out_shape=[jax.ShapeDtypeStruct((4, 4, 32,...  12.2 us
    all_to_all x2, starting transfers between devices, to_zones(): lax.all_to_all(pieces, 'chan', split_axis=0, concat_axis=0, axis_index_gr...  11.1 us
    all_to_all x1, starting transfers between devices, body(): lax.all_to_all(stats, BOTH, split_axis=0, concat_axis=0, tiled=True)  10.9 us
    pallas_call x1, Pallas kernels, conv_out(): pl.pallas_call(conv_out_kernel, out_shape=jax.ShapeDtypeStruct((30, 2, 4,...  10.1 us
    ppermute x19, waiting for transfers between devices, send(): return lax.ppermute(array, BOTH, device_perm(move))  9.47 us
    pallas_call x1, Pallas kernels, conv_rim(): pl.pallas_call(rim_kernel, out_shape=jax.ShapeDtypeStruct((2, 2, 2, 4, 32...  6.28 us
  transfers between devices with their start and end apart: 22, of which 8 were waited for; matrix products, arithmetic and copies ran while one was open for 6% of the time, Pallas kernels for 6%

profile of v5, /device:TPU:2, one launch (start us, length us, event | category | flops | bytes accessed | tf_op | source)
XLA Modules:
  0.0 111.3 jit_solution(11909381657719103785)
XLA Ops:
  0.0 1.3 %copy.28 = bf16[480,6,4,32]{0,3,1,2:T(8,128)(2,1)S(1)} copy(bf16[480,6,4,32]{0,3,2,1:T(8,128)(2,1)} %param.8) | data formatting | bytes 1474560 | tf_op args[0]
  1.3 0.3 fusion
  1.6 1.0 pad_maximum_fusion
  2.6 5.3 %all-to-all-start = ((bf16[4,4,6,32,128]{4,3,2,1,0:T(8,128)(2,1)}), bf16[4,4,6,32,128]{4,3,2,1,0:T(8,128)(2,1)}, u32[]{:S(2)}, u32[]{:S(2)}) async-start(bf16[4,4,6,32,128]{4,3,2,1,0:T(8,128)(2,1)} %pad_maximum_fusion), calls=%async_computation | async-start | bytes 1572864 | tf_op jit(solution)/shard_map/all_to_all | solution.py:305
  7.9 0.1 pad_bitcast_fusion
  8.0 0.3 fusion.9
  8.4 0.2 pad_slice_fusion.1
  8.6 3.5 %collective-permute-start.1 = (bf16[320,512]{1,0:T(8,128)(2,1)S(1)}, bf16[320,512]{1,0:T(8,128)(2,1)S(1)}, u32[]{:S(2)}, u32[]{:S(2)}) collective-permute-start(bf16[320,512]{1,0:T(8,128)(2,1)S(1)} %pad_maximum_fusion.3), channel_id=1, source_target_pairs={{0,1},{1,2},{2,3},{3,4},{4,5},{5,6},{6,7},{8,9},{9,10},{10,11},{11... | collective-permute-start | bytes 983048 | tf_op jit(solution)/shard_map/ppermute | solution.py:26
  12.2 4.5 %collective-permute-start.2 = (bf16[320,512]{1,0:T(8,128)(2,1)S(1)}, bf16[320,512]{1,0:T(8,128)(2,1)S(1)}, u32[]{:S(2)}, u32[]{:S(2)}) collective-permute-start(bf16[320,512]{1,0:T(8,128)(2,1)S(1)} %pad_maximum_fusion.4), channel_id=1, source_target_pairs={{1,0},{2,1},{3,2},{4,3},{5,4},{6,5},{7,6},{9,8},{10,9},{11,10},{12... | collective-permute-start | bytes 983048 | tf_op jit(solution)/shard_map/ppermute | solution.py:26
  16.7 1.0 constant_dynamic-slice_fusion
  17.7 3.6 %collective-permute-start.8 = (bf16[9,3,32,256]{3,2,1,0:T(8,128)(2,1)S(1)}, bf16[9,3,32,256]{3,2,1,0:T(8,128)(2,1)}, u32[]{:S(2)}, u32[]{:S(2)}) collective-permute-start(bf16[9,3,32,256]{3,2,1,0:T(8,128)(2,1)S(1)} %constant_dynamic-slice_fusion), channel_id=1, source_target_pairs={{0,64},{1,65},{2,66},{3,67},{4,68},{5,69},{6,70},{7,71},{8,72},{9,... | collective-permute-start | bytes 1327112 | tf_op jit(solution)/shard_map/ppermute | solution.py:26
  21.3 0.0 all-to-all-done.own
  21.3 2.1 %collective-permute-start = (bf16[4,4,6,32,128]{4,3,2,1,0:T(8,128)(2,1)}, bf16[4,4,6,32,128]{4,3,2,1,0:T(8,128)(2,1)}, u32[]{:S(2)}, u32[]{:S(2)}) collective-permute-start(bf16[4,4,6,32,128]{4,3,2,1,0:T(8,128)(2,1)} %all-to-all-done.own), channel_id=1, source_target_pairs={{0,16},{1,17},{2,18},{3,19},{4,20},{5,21},{6,22},{7,23},{8,24},{9,... | collective-permute-start | bytes 2359304 | tf_op jit(solution)/shard_map/ppermute | solution.py:26
  23.5 0.3 collective-permute-done.2
  23.8 0.2 fusion.5
  24.0 0.8 pad_maximum_fusion.2
  24.8 5.8 %all-to-all-start.1 = ((bf16[4,2,6,32,128]{4,3,2,1,0:T(8,128)(2,1)}), bf16[4,2,6,32,128]{4,3,2,1,0:T(8,128)(2,1)S(1)}, u32[]{:S(2)}, u32[]{:S(2)}) async-start(bf16[4,2,6,32,128]{4,3,2,1,0:T(8,128)(2,1)} %pad_maximum_fusion.2), calls=%async_computation.1 | async-start | bytes 786432 | tf_op jit(solution)/shard_map/all_to_all | solution.py:305
  30.6 2.1 %collective-permute-start.6 = (bf16[9,3,32,512]{3,2,1,0:T(8,128)(2,1)}, bf16[9,3,32,512]{3,2,1,0:T(8,128)(2,1)}, u32[]{:S(2)}, u32[]{:S(2)}) collective-permute-start(bf16[9,3,32,512]{3,2,1,0:T(8,128)(2,1)} %bitcast.80), channel_id=1, source_target_pairs={{0,32},{1,33},{2,34},{3,35},{4,36},{5,37},{6,38},{7,39},{8,40},{9,... | collective-permute-start | bytes 2654216 | tf_op jit(solution)/shard_map/ppermute | solution.py:26
  32.7 1.3 %collective-permute-start.7 = (bf16[9,3,32,512]{3,2,1,0:T(8,128)(2,1)}, bf16[9,3,32,512]{3,2,1,0:T(8,128)(2,1)}, u32[]{:S(2)}, u32[]{:S(2)}) collective-permute-start(bf16[9,3,32,512]{3,2,1,0:T(8,128)(2,1)} %bitcast.81), channel_id=1, source_target_pairs={{0,96},{1,97},{2,98},{3,99},{4,100},{5,101},{6,102},{7,103},{8,104... | collective-permute-start | bytes 2654216 | tf_op jit(solution)/shard_map/ppermute | solution.py:26
  34.0 1.3 %collective-permute-start.3 = (bf16[2,10,512]{2,1,0:T(8,128)(2,1)S(1)}, bf16[2,10,512]{2,1,0:T(8,128)(2,1)S(1)}, u32[]{:S(2)}, u32[]{:S(2)}) collective-permute-start(bf16[2,10,512]{2,1,0:T(8,128)(2,1)S(1)} %pad_maximum_fusion.6), channel_id=1, source_target_pairs={{0,8},{1,9},{2,10},{3,11},{4,12},{5,13},{6,14},{7,15},{8,16},{9,17... | collective-permute-start | bytes 61448 | tf_op jit(solution)/shard_map/ppermute | solution.py:26
  35.4 0.8 collective-permute-done.3.before
  36.2 1.3 %collective-permute-start.4 = (bf16[2,10,512]{2,1,0:T(8,128)(2,1)S(1)}, bf16[2,10,512]{2,1,0:T(8,128)(2,1)S(1)}, u32[]{:S(2)}, u32[]{:S(2)}) collective-permute-start(bf16[2,10,512]{2,1,0:T(8,128)(2,1)S(1)} %pad_maximum_fusion.7), channel_id=1, source_target_pairs={{8,0},{9,1},{10,2},{11,3},{12,4},{13,5},{14,6},{15,7},{16,8},{17,9... | collective-permute-start | bytes 61448 | tf_op jit(solution)/shard_map/ppermute | solution.py:26
  37.5 0.6 copy.22.rim
  38.1 0.1 collective-permute-start.9
  38.1 3.9 %collective-permute-done.4.after = bf16[2,10,512]{2,1,0:T(8,128)(2,1)S(1)} collective-permute-done((bf16[2,10,512]{2,1,0:T(8,128)(2,1)S(1)}, bf16[2,10,512]{2,1,0:T(8,128)(2,1)S(1)}, u32[]{:S(2)}, u32[]{:S(2)}) %collective-permute-start.4) | collective-permute-done | bytes 20512 | tf_op jit(solution)/shard_map/ppermute | solution.py:26
  42.0 0.0 all-to-all-done.1.own_edge
  42.0 4.8 %collective-permute-start.5 = (bf16[4,2,6,32,128]{4,3,2,1,0:T(8,128)(2,1)S(1)}, bf16[4,2,6,32,128]{4,3,2,1,0:T(8,128)(2,1)S(1)}, u32[]{:S(2)}, u32[]{:S(2)}) collective-permute-start(bf16[4,2,6,32,128]{4,3,2,1,0:T(8,128)(2,1)S(1)} %all-to-all-done.1.own_edge), channel_id=1, source_target_pairs={{0,16},{1,17},{2,18},{3,19},{4,20},{5,21},{6,22},{7,23},{8,24},{9,... | collective-permute-start | bytes 1179656 | tf_op jit(solution)/shard_map/ppermute | solution.py:26
  46.8 0.0 collective-permute-done.other
  46.8 6.3 %conv_rim.1.rim = f32[2,2,2,4,32,256]{5,4,3,2,1,0:T(8,128)S(1)} custom-call(bf16[2,8,64,512]{3,2,1,0:T(8,128)(2,1)S(1)} %copy.22.rim, bf16[2,64,512]{2,1,0:T(8,128)(2,1)S(1)} %bitcast.66, bf16[2,64,512]{2,1,0:T(8,128)(2,1)S(1)} %bitcast.68, bf16[2,10,512]{2,1,0:T(8,128)(2,1)S(1)} %collective-permute-done.3.before, ...), custom_call_target="tpu_custom_call" | custom-call | flops 7200000000 | bytes 8000000 | tf_op jit(solution)/shard_map/conv_rim/pallas_call | solution.py:186
  53.1 2.8 %collective-permute-start.10 = (bf16[4,4,6,32,128]{4,3,2,1,0:T(8,128)(2,1)}, bf16[4,4,6,32,128]{4,3,2,1,0:T(8,128)(2,1)S(1)}, u32[]{:S(2)}, u32[]{:S(2)}) collective-permute-start(bf16[4,4,6,32,128]{4,3,2,1,0:T(8,128)(2,1)} %all-to-all-done.own), channel_id=1, source_target_pairs={{0,8},{1,9},{2,10},{3,11},{4,12},{5,13},{6,14},{7,15},{8,0},{9,1},... | collective-permute-start | bytes 2359304 | tf_op jit(solution)/shard_map/ppermute | solution.py:26
  55.9 0.0 collective-permute-done.9.far
  56.0 0.7 collective-permute-start.11
  56.7 0.1 collective-permute-start.12
  56.8 0.4 collective-permute-start.13
  57.2 0.1 reshape.70
  57.3 0.1 broadcast_in_dim.13
  57.4 0.6 pad_add_fusion.place
  58.0 1.9 %collective-permute-done.12.own_edge_swap = bf16[4,2,6,32,128]{4,3,2,1,0:T(8,128)(2,1)S(1)} collective-permute-done((bf16[4,2,6,32,128]{4,3,2,1,0:T(8,128)(2,1)S(1)}, bf16[4,2,6,32,128]{4,3,2,1,0:T(8,128)(2,1)S(1)}, u32[]{:S(2)}, u32[]{:S(2)}) %collective-permute-start.12) | collective-permute-done | bytes 393248 | tf_op jit(solution)/shard_map/ppermute | solution.py:26
  60.0 0.3 collective-permute-done.13.other_edge_swap
  60.2 0.2 collective-permute-done.11.other_swap
  60.4 0.7 copy-done.6
  61.1 0.7 broadcast_in_dim.14.bias
  61.8 0.0 copy-start
  61.8 12.2 %conv_in.1 = (bf16[4,4,32,128]{3,2,1,0:T(8,128)(2,1)}, bf16[4,4,32,128]{3,2,1,0:T(8,128)(2,1)}, bf16[4,4,32,128]{3,2,1,0:T(8,128)(2,1)}, bf16[4,4,32,128]{3,2,1,0:T(8,128)(2,1)}, f32[128,128]{1,0:T(8,128)}) custom-call(s32[4]{0:T(128)} %pad_add_fusion.place, bf16[4,4,6,32,128]{4,3,2,1,0:T(8,128)(2,1)} %all-to-all-done.own, ...), custom_call_target="tpu_custom_call" | custom-call | flops 7200000000 | bytes 9000000 | tf_op jit(solution)/shard_map/conv_in/pallas_call | solution.py:119
  74.0 0.5 collective-permute-start.14
  74.5 2.9 %collective-permute-start.16 = (bf16[4,4,32,128]{3,2,1,0:T(8,128)(2,1)}, bf16[4,4,32,128]{3,2,1,0:T(8,128)(2,1)S(1)}, u32[]{:S(2)}, u32[]{:S(2)}) collective-permute-start(bf16[4,4,32,128]{3,2,1,0:T(8,128)(2,1)} %get-tuple-element.42), channel_id=1, source_target_pairs={{0,24},{1,25},{2,26},{3,27},{4,28},{5,29},{6,30},{7,31},{8,16},{9,... | collective-permute-start | bytes 393224 | tf_op jit(solution)/shard_map/ppermute | solution.py:26
  77.4 0.4 collective-permute-start.15
  77.8 0.1 reshape.74
  77.9 0.1 reshape.75
  77.9 0.1 reshape.76
  78.0 0.1 stack_reshape.15
  78.1 0.1 stack.109.place
  78.2 10.9 %all-to-all-start.2 = ((f32[128,1,128]{2,1,0:T(1,128)}), f32[128,1,128]{2,1,0:T(1,128)S(1)}, u32[]{:S(2)}, u32[]{:S(2)}) async-start(f32[128,1,128]{2,1,0:T(1,128)} %bitcast.87), calls=%async_computation.2 | async-start | bytes 131072 | tf_op jit(solution)/shard_map/all_to_all | solution.py:343
  89.2 1.0 pad_maximum_fusion.1
  90.2 3.4 %collective-permute-start.17 = (bf16[4,4,32,128]{3,2,1,0:T(8,128)(2,1)S(1)}, bf16[4,4,32,128]{3,2,1,0:T(8,128)(2,1)S(1)}, u32[]{:S(2)}, u32[]{:S(2)}) collective-permute-start(bf16[4,4,32,128]{3,2,1,0:T(8,128)(2,1)S(1)} %get-tuple-element.56), channel_id=1, source_target_pairs={{0,1},{1,2},{2,3},{3,4},{4,5},{5,6},{6,7},{8,9},{9,10},{10,11},{11... | collective-permute-start | bytes 393224 | tf_op jit(solution)/shard_map/ppermute | solution.py:26
  93.6 4.8 %collective-permute-start.18 = (bf16[4,4,32,128]{3,2,1,0:T(8,128)(2,1)S(1)}, bf16[4,4,32,128]{3,2,1,0:T(8,128)(2,1)S(1)}, u32[]{:S(2)}, u32[]{:S(2)}) collective-permute-start(bf16[4,4,32,128]{3,2,1,0:T(8,128)(2,1)S(1)} %get-tuple-element.55), channel_id=1, source_target_pairs={{1,0},{2,1},{3,2},{4,3},{5,4},{6,5},{7,6},{9,8},{10,9},{11,10},{12... | collective-permute-start | bytes 393224 | tf_op jit(solution)/shard_map/ppermute | solution.py:26
  98.4 0.1 reshape.72
  98.5 0.1 broadcast_in_dim.15
  98.6 0.1 stack_reshape.14
  98.7 0.1 broadcast_in_dim.16
  98.8 0.1 reshape.73
  98.9 0.8 collective-permute-done.17.up
  99.8 1.2 %collective-permute-done.18.down = bf16[4,4,32,128]{3,2,1,0:T(8,128)(2,1)S(1)} collective-permute-done((bf16[4,4,32,128]{3,2,1,0:T(8,128)(2,1)S(1)}, bf16[4,4,32,128]{3,2,1,0:T(8,128)(2,1)S(1)}, u32[]{:S(2)}, u32[]{:S(2)}) %collective-permute-start.18) | collective-permute-done | bytes 131104 | tf_op jit(solution)/shard_map/ppermute | solution.py:26
  100.9 10.1 %conv_out.1 = bf16[30,2,4,8,256]{4,3,2,1,0:T(8,128)(2,1)} custom-call(s32[5]{0:T(128)S(1)} %stack.109.place, bf16[4,4,4,32,128]{4,3,2,1,0:T(8,128)(2,1)S(1)} %copy.26.main, bf16[4,4,32,128]{3,2,1,0:T(8,128)(2,1)S(1)} %collective-permute-done.17.up, bf16[4,4,32,128]{3,2,1,0:T(8,128)(2,1)S(1)} %collective-permute-done.18.down, ...), custom_call_target="tpu_custom_call" | custom-call | flops 4899999744 | bytes 18000000 | tf_op jit(solution)/shard_map/conv_out/pallas_call | solution.py:262
  (50 shorter events, 0.5 us)
Async XLA Ops:
  0.0 7.9 %copy-start.1 = (bf16[60,2,8,512]{3,2,1,0:T(8,128)(2,1)S(1)}, bf16[60,2,8,512]{3,2,1,0:T(8,128)(2,1)}, u32[]{:S(2)}) copy-start(bf16[60,2,8,512]{3,2,1,0:T(8,128)(2,1)} %param.13) | copy-start | bytes 2949124
  2.6 18.7 %all-to-all-start = ((bf16[4,4,6,32,128]{4,3,2,1,0:T(8,128)(2,1)}), bf16[4,4,6,32,128]{4,3,2,1,0:T(8,128)(2,1)}, u32[]{:S(2)}, u32[]{:S(2)}) async-start(bf16[4,4,6,32,128]{4,3,2,1,0:T(8,128)(2,1)} %pad_maximum_fusion), calls=%async_computation | async-start | bytes 1572864 | tf_op jit(solution)/shard_map/all_to_all | solution.py:305
  8.6 14.9 %collective-permute-start.1 = (bf16[320,512]{1,0:T(8,128)(2,1)S(1)}, bf16[320,512]{1,0:T(8,128)(2,1)S(1)}, u32[]{:S(2)}, u32[]{:S(2)}) collective-permute-start(bf16[320,512]{1,0:T(8,128)(2,1)S(1)} %pad_maximum_fusion.3), channel_id=1, source_target_pairs={{0,1},{1,2},{2,3},{3,4},{4,5},{5,6},{6,7},{8,9},{9,10},{10,11},{11... | collective-permute-start | bytes 983048 | tf_op jit(solution)/shard_map/ppermute | solution.py:26
  12.2 11.6 %collective-permute-start.2 = (bf16[320,512]{1,0:T(8,128)(2,1)S(1)}, bf16[320,512]{1,0:T(8,128)(2,1)S(1)}, u32[]{:S(2)}, u32[]{:S(2)}) collective-permute-start(bf16[320,512]{1,0:T(8,128)(2,1)S(1)} %pad_maximum_fusion.4), channel_id=1, source_target_pairs={{1,0},{2,1},{3,2},{4,3},{5,4},{6,5},{7,6},{9,8},{10,9},{11,10},{12... | collective-permute-start | bytes 983048 | tf_op jit(solution)/shard_map/ppermute | solution.py:26
  17.7 20.3 %collective-permute-start.8 = (bf16[9,3,32,256]{3,2,1,0:T(8,128)(2,1)S(1)}, bf16[9,3,32,256]{3,2,1,0:T(8,128)(2,1)}, u32[]{:S(2)}, u32[]{:S(2)}) collective-permute-start(bf16[9,3,32,256]{3,2,1,0:T(8,128)(2,1)S(1)} %constant_dynamic-slice_fusion), channel_id=1, source_target_pairs={{0,64},{1,65},{2,66},{3,67},{4,68},{5,69},{6,70},{7,71},{8,72},{9,... | collective-permute-start | bytes 1327112 | tf_op jit(solution)/shard_map/ppermute | solution.py:26
  21.3 25.5 %collective-permute-start = (bf16[4,4,6,32,128]{4,3,2,1,0:T(8,128)(2,1)}, bf16[4,4,6,32,128]{4,3,2,1,0:T(8,128)(2,1)}, u32[]{:S(2)}, u32[]{:S(2)}) collective-permute-start(bf16[4,4,6,32,128]{4,3,2,1,0:T(8,128)(2,1)} %all-to-all-done.own), channel_id=1, source_target_pairs={{0,16},{1,17},{2,18},{3,19},{4,20},{5,21},{6,22},{7,23},{8,24},{9,... | collective-permute-start | bytes 2359304 | tf_op jit(solution)/shard_map/ppermute | solution.py:26
  24.8 17.3 %all-to-all-start.1 = ((bf16[4,2,6,32,128]{4,3,2,1,0:T(8,128)(2,1)}), bf16[4,2,6,32,128]{4,3,2,1,0:T(8,128)(2,1)S(1)}, u32[]{:S(2)}, u32[]{:S(2)}) async-start(bf16[4,2,6,32,128]{4,3,2,1,0:T(8,128)(2,1)} %pad_maximum_fusion.2), calls=%async_computation.1 | async-start | bytes 786432 | tf_op jit(solution)/shard_map/all_to_all | solution.py:305
  30.6 25.3 %collective-permute-start.6 = (bf16[9,3,32,512]{3,2,1,0:T(8,128)(2,1)}, bf16[9,3,32,512]{3,2,1,0:T(8,128)(2,1)}, u32[]{:S(2)}, u32[]{:S(2)}) collective-permute-start(bf16[9,3,32,512]{3,2,1,0:T(8,128)(2,1)} %bitcast.80), channel_id=1, source_target_pairs={{0,32},{1,33},{2,34},{3,35},{4,36},{5,37},{6,38},{7,39},{8,40},{9,... | collective-permute-start | bytes 2654216 | tf_op jit(solution)/shard_map/ppermute | solution.py:26
  32.7 23.2 %collective-permute-start.7 = (bf16[9,3,32,512]{3,2,1,0:T(8,128)(2,1)}, bf16[9,3,32,512]{3,2,1,0:T(8,128)(2,1)}, u32[]{:S(2)}, u32[]{:S(2)}) collective-permute-start(bf16[9,3,32,512]{3,2,1,0:T(8,128)(2,1)} %bitcast.81), channel_id=1, source_target_pairs={{0,96},{1,97},{2,98},{3,99},{4,100},{5,101},{6,102},{7,103},{8,104... | collective-permute-start | bytes 2654216 | tf_op jit(solution)/shard_map/ppermute | solution.py:26
  34.0 2.1 %collective-permute-start.3 = (bf16[2,10,512]{2,1,0:T(8,128)(2,1)S(1)}, bf16[2,10,512]{2,1,0:T(8,128)(2,1)S(1)}, u32[]{:S(2)}, u32[]{:S(2)}) collective-permute-start(bf16[2,10,512]{2,1,0:T(8,128)(2,1)S(1)} %pad_maximum_fusion.6), channel_id=1, source_target_pairs={{0,8},{1,9},{2,10},{3,11},{4,12},{5,13},{6,14},{7,15},{8,16},{9,17... | collective-permute-start | bytes 61448 | tf_op jit(solution)/shard_map/ppermute | solution.py:26
  36.2 5.9 %collective-permute-start.4 = (bf16[2,10,512]{2,1,0:T(8,128)(2,1)S(1)}, bf16[2,10,512]{2,1,0:T(8,128)(2,1)S(1)}, u32[]{:S(2)}, u32[]{:S(2)}) collective-permute-start(bf16[2,10,512]{2,1,0:T(8,128)(2,1)S(1)} %pad_maximum_fusion.7), channel_id=1, source_target_pairs={{8,0},{9,1},{10,2},{11,3},{12,4},{13,5},{14,6},{15,7},{16,8},{17,9... | collective-permute-start | bytes 61448 | tf_op jit(solution)/shard_map/ppermute | solution.py:26
  38.1 17.9 %collective-permute-start.9 = (bf16[9,3,32,256]{3,2,1,0:T(8,128)(2,1)}, bf16[9,3,32,256]{3,2,1,0:T(8,128)(2,1)}, u32[]{:S(2)}, u32[]{:S(2)}) collective-permute-start(bf16[9,3,32,256]{3,2,1,0:T(8,128)(2,1)} %collective-permute-done.8.near), channel_id=1, source_target_pairs={{0,1},{1,0},{2,3},{3,2},{4,5},{5,4},{6,7},{7,6},{8,9},{9,8},{10,11... | collective-permute-start | bytes 1327112 | tf_op jit(solution)/shard_map/ppermute | solution.py:26
  42.0 14.7 %copy-start.2 = (bf16[4,2,6,32,128]{4,3,2,1,0:T(8,128)(2,1)}, bf16[4,2,6,32,128]{4,3,2,1,0:T(8,128)(2,1)S(1)}, u32[]{:S(2)}) copy-start(bf16[4,2,6,32,128]{4,3,2,1,0:T(8,128)(2,1)S(1)} %all-to-all-done.1.own_edge) | copy-start | bytes 1179652
  42.0 13.9 %collective-permute-start.5 = (bf16[4,2,6,32,128]{4,3,2,1,0:T(8,128)(2,1)S(1)}, bf16[4,2,6,32,128]{4,3,2,1,0:T(8,128)(2,1)S(1)}, u32[]{:S(2)}, u32[]{:S(2)}) collective-permute-start(bf16[4,2,6,32,128]{4,3,2,1,0:T(8,128)(2,1)S(1)} %all-to-all-done.1.own_edge), channel_id=1, source_target_pairs={{0,16},{1,17},{2,18},{3,19},{4,20},{5,21},{6,22},{7,23},{8,24},{9,... | collective-permute-start | bytes 1179656 | tf_op jit(solution)/shard_map/ppermute | solution.py:26
  46.8 10.4 %copy-start.3 = (f32[512]{0:T(512)S(1)}, f32[512]{0:T(512)}, u32[]{:S(2)}) copy-start(f32[512]{0:T(512)} %param.10) | copy-start | bytes 6148
  53.1 7.1 %collective-permute-start.10 = (bf16[4,4,6,32,128]{4,3,2,1,0:T(8,128)(2,1)}, bf16[4,4,6,32,128]{4,3,2,1,0:T(8,128)(2,1)S(1)}, u32[]{:S(2)}, u32[]{:S(2)}) collective-permute-start(bf16[4,4,6,32,128]{4,3,2,1,0:T(8,128)(2,1)} %all-to-all-done.own), channel_id=1, source_target_pairs={{0,8},{1,9},{2,10},{3,11},{4,12},{5,13},{6,14},{7,15},{8,0},{9,1},... | collective-permute-start | bytes 2359304 | tf_op jit(solution)/shard_map/ppermute | solution.py:26
  55.9 5.9 %copy-start.7 = (bf16[4,2,6,32,128]{4,3,2,1,0:T(8,128)(2,1)}, bf16[4,2,6,32,128]{4,3,2,1,0:T(8,128)(2,1)S(1)}, u32[]{:S(2)}) copy-start(bf16[4,2,6,32,128]{4,3,2,1,0:T(8,128)(2,1)S(1)} %collective-permute-done.5.other_edge) | copy-start | bytes 1179652
  56.0 4.5 %collective-permute-start.11 = (bf16[4,4,6,32,128]{4,3,2,1,0:T(8,128)(2,1)}, bf16[4,4,6,32,128]{4,3,2,1,0:T(8,128)(2,1)}, u32[]{:S(2)}, u32[]{:S(2)}) collective-permute-start(bf16[4,4,6,32,128]{4,3,2,1,0:T(8,128)(2,1)} %collective-permute-done.other), channel_id=1, source_target_pairs={{0,8},{1,9},{2,10},{3,11},{4,12},{5,13},{6,14},{7,15},{8,0},{9,1},... | collective-permute-start | bytes 2359304 | tf_op jit(solution)/shard_map/ppermute | solution.py:26
  56.7 3.3 %collective-permute-start.12 = (bf16[4,2,6,32,128]{4,3,2,1,0:T(8,128)(2,1)S(1)}, bf16[4,2,6,32,128]{4,3,2,1,0:T(8,128)(2,1)S(1)}, u32[]{:S(2)}, u32[]{:S(2)}) collective-permute-start(bf16[4,2,6,32,128]{4,3,2,1,0:T(8,128)(2,1)S(1)} %all-to-all-done.1.own_edge), channel_id=1, source_target_pairs={{0,8},{1,9},{2,10},{3,11},{4,12},{5,13},{6,14},{7,15},{8,0},{9,1},... | collective-permute-start | bytes 1179656 | tf_op jit(solution)/shard_map/ppermute | solution.py:26
  56.8 3.4 %collective-permute-start.13 = (bf16[4,2,6,32,128]{4,3,2,1,0:T(8,128)(2,1)S(1)}, bf16[4,2,6,32,128]{4,3,2,1,0:T(8,128)(2,1)}, u32[]{:S(2)}, u32[]{:S(2)}) collective-permute-start(bf16[4,2,6,32,128]{4,3,2,1,0:T(8,128)(2,1)S(1)} %collective-permute-done.5.other_edge), channel_id=1, source_target_pairs={{0,8},{1,9},{2,10},{3,11},{4,12},{5,13},{6,14},{7,15},{8,0},{9,1},... | collective-permute-start | bytes 1179656 | tf_op jit(solution)/shard_map/ppermute | solution.py:26
  60.0 1.8 %copy-start.8 = (bf16[4,2,6,32,128]{4,3,2,1,0:T(8,128)(2,1)}, bf16[4,2,6,32,128]{4,3,2,1,0:T(8,128)(2,1)S(1)}, u32[]{:S(2)}) copy-start(bf16[4,2,6,32,128]{4,3,2,1,0:T(8,128)(2,1)S(1)} %collective-permute-done.12.own_edge_swap) | copy-start | bytes 1179652
  60.2 0.9 copy-start.6
  61.8 16.0 %copy-start.4 = (f32[512]{0:T(512)S(1)}, f32[512]{0:T(512)}, u32[]{:S(2)}) copy-start(f32[512]{0:T(512)} %param.11) | copy-start | bytes 6148
  61.8 16.1 %copy-start.5 = (f32[512]{0:T(512)S(1)}, f32[512]{0:T(512)}, u32[]{:S(2)}) copy-start(f32[512]{0:T(512)} %param.12) | copy-start | bytes 6148
  61.8 39.1 %copy-start = (f32[256]{0:T(256)S(1)}, f32[256]{0:T(256)}, u32[]{:S(2)}) copy-start(f32[256]{0:T(256)} %param.15) | copy-start | bytes 3076
  74.0 4.2 %collective-permute-start.14 = (bf16[4,4,32,128]{3,2,1,0:T(8,128)(2,1)}, bf16[4,4,32,128]{3,2,1,0:T(8,128)(2,1)S(1)}, u32[]{:S(2)}, u32[]{:S(2)}) collective-permute-start(bf16[4,4,32,128]{3,2,1,0:T(8,128)(2,1)} %get-tuple-element.39), channel_id=1, source_target_pairs={{0,8},{1,9},{2,10},{3,11},{4,12},{5,13},{6,14},{7,15},{8,0},{9,1},... | collective-permute-start | bytes 393224 | tf_op jit(solution)/shard_map/ppermute | solution.py:26
  74.5 14.7 %collective-permute-start.16 = (bf16[4,4,32,128]{3,2,1,0:T(8,128)(2,1)}, bf16[4,4,32,128]{3,2,1,0:T(8,128)(2,1)S(1)}, u32[]{:S(2)}, u32[]{:S(2)}) collective-permute-start(bf16[4,4,32,128]{3,2,1,0:T(8,128)(2,1)} %get-tuple-element.42), channel_id=1, source_target_pairs={{0,24},{1,25},{2,26},{3,27},{4,28},{5,29},{6,30},{7,31},{8,16},{9,... | collective-permute-start | bytes 393224 | tf_op jit(solution)/shard_map/ppermute | solution.py:26
  77.4 11.8 %collective-permute-start.15 = (bf16[4,4,32,128]{3,2,1,0:T(8,128)(2,1)}, bf16[4,4,32,128]{3,2,1,0:T(8,128)(2,1)S(1)}, u32[]{:S(2)}, u32[]{:S(2)}) collective-permute-start(bf16[4,4,32,128]{3,2,1,0:T(8,128)(2,1)} %get-tuple-element.41), channel_id=1, source_target_pairs={{0,16},{1,17},{2,18},{3,19},{4,20},{5,21},{6,22},{7,23},{8,24},{9,... | collective-permute-start | bytes 393224 | tf_op jit(solution)/shard_map/ppermute | solution.py:26
  78.2 20.2 %all-to-all-start.2 = ((f32[128,1,128]{2,1,0:T(1,128)}), f32[128,1,128]{2,1,0:T(1,128)S(1)}, u32[]{:S(2)}, u32[]{:S(2)}) async-start(f32[128,1,128]{2,1,0:T(1,128)} %bitcast.87), calls=%async_computation.2 | async-start | bytes 131072 | tf_op jit(solution)/shard_map/all_to_all | solution.py:343
  90.2 9.6 %collective-permute-start.17 = (bf16[4,4,32,128]{3,2,1,0:T(8,128)(2,1)S(1)}, bf16[4,4,32,128]{3,2,1,0:T(8,128)(2,1)S(1)}, u32[]{:S(2)}, u32[]{:S(2)}) collective-permute-start(bf16[4,4,32,128]{3,2,1,0:T(8,128)(2,1)S(1)} %get-tuple-element.56), channel_id=1, source_target_pairs={{0,1},{1,2},{2,3},{3,4},{4,5},{5,6},{6,7},{8,9},{9,10},{10,11},{11... | collective-permute-start | bytes 393224 | tf_op jit(solution)/shard_map/ppermute | solution.py:26
  93.6 7.4 %collective-permute-start.18 = (bf16[4,4,32,128]{3,2,1,0:T(8,128)(2,1)S(1)}, bf16[4,4,32,128]{3,2,1,0:T(8,128)(2,1)S(1)}, u32[]{:S(2)}, u32[]{:S(2)}) collective-permute-start(bf16[4,4,32,128]{3,2,1,0:T(8,128)(2,1)S(1)} %get-tuple-element.55), channel_id=1, source_target_pairs={{1,0},{2,1},{3,2},{4,3},{5,4},{6,5},{7,6},{9,8},{10,9},{11,10},{12... | collective-permute-start | bytes 393224 | tf_op jit(solution)/shard_map/ppermute | solution.py:26

commit v6 on v5

--- a/solution.py
+++ b/solution.py
@@ -65,7 +65,7 @@
                 group.append((source.at[taps], w.at[:, tap, :, (z + 2) % 4, :, columns]))
         start = sum(len(g) for g in groups)
         groups.append([fetch(start + i, *pair) for i, pair in enumerate(group)])
-    for group in groups:
+    for group in groups[:2]:
         for copy in group:
             copy.start()
     moments[...] = jnp.zeros_like(moments)
@@ -88,6 +88,8 @@
         if source < 4:
             for copy in groups[source]:
                 copy.wait()
+            for copy in groups[source + 2] if source < 2 else ():
+                copy.start()
         taps = range(max(0, source - 3), min(2, source) + 1)
         for g in range(2):
             summed = None
@@ -202,7 +204,8 @@
 
 def conv_out_kernel(place, main, up, down, vectors, rim, bias, weight, out, n, acc, raw, w0, w1, w2, sems):
     fetches = [pltpu.make_async_copy(weight.at[tap], raw.at[tap], sems.at[tap]) for tap in range(3)]
-    for fetch in fetches:
+    rim_fetch = pltpu.make_async_copy(rim, acc.at[:, :, 0:2], sems.at[3])
+    for fetch in (*fetches, rim_fetch):
         fetch.start()
     own, left, right, top, bottom = (place[i] for i in range(5))
     row = lax.broadcasted_iota(jnp.int32, (32, 128), 0)
@@ -227,13 +230,6 @@
         return 0
 
     lax.fori_loop(0, 4, frame, 0)
-    whole = jnp.broadcast_to(bias[...], (32, 256))
-    for pw in range(2):
-        for ph in range(2):
-            for t in range(4):
-                for h in range(4):
-                    acc[pw, ph, t, h] = rim[pw, ph, t, h] + whole if t < 2 else whole
-
     def multiply(tap, w):
         frames = 2 + tap
         for ph in range(2):
@@ -241,9 +237,14 @@
                 for pw in range(2):
                     lhs = n[0:frames, ph + j : ph + j + 4, :, pw * 512 : pw * 512 + 1024]
                     term = jnp.dot(lhs.reshape(frames * 128, 1024), w[ph, j, pw], preferred_element_type=F32)
-                    acc[pw, ph, 4 - frames : 4] += term.reshape(frames, 4, 32, 256)
-
-    for fetch in fetches:
+                    term = term.reshape(frames, 4, 32, 256)
+                    if tap == 2 and j == 0:
+                        acc[pw, ph, 0:2] += term[0:2]
+                        acc[pw, ph, 2:4] = term[2:4]
+                    else:
+                        acc[pw, ph, 4 - frames : 4] += term
+
+    for fetch in (*fetches, rim_fetch):
         fetch.wait()
     collapse(raw.at[2], w2)
     multiply(2, w2)
@@ -254,7 +255,7 @@
     for pw in range(2):
         for t in range(4):
             rows = jnp.concatenate([acc[pw, r % 2, t, r // 2][None] for r in range(8)])
-            out[:, pw, t] = jnp.swapaxes(rows, 0, 1)[:30].astype(BF16)
+            out[:, pw, t] = (jnp.swapaxes(rows, 0, 1)[:30] + bias[...]).astype(BF16)
 
 
 def conv_out(place, main, up, down, vectors, rim, bias, weight):
@@ -262,7 +263,7 @@
     return pl.pallas_call(
         conv_out_kernel,
         out_shape=jax.ShapeDtypeStruct((30, 2, 4, 8, 256), BF16),
-        in_specs=[pl.BlockSpec(memory_space=pltpu.SMEM)] + [whole] * 6 + [pl.BlockSpec(memory_space=pltpu.HBM)],
+        in_specs=[pl.BlockSpec(memory_space=pltpu.SMEM)] + [whole] * 4 + [pl.BlockSpec(memory_space=pl.ANY), whole, pl.BlockSpec(memory_space=pltpu.HBM)],
         out_specs=whole,
         scratch_shapes=[
             pltpu.VMEM((4, 6, 32, 1536), BF16),
@@ -271,7 +272,7 @@
             pltpu.VMEM((2, 2, 2, 1024, 256), BF16),
             pltpu.VMEM((2, 2, 2, 1024, 256), BF16),
             pltpu.VMEM((2, 2, 2, 1024, 256), BF16),
-            pltpu.SemaphoreType.DMA((3,)),
+            pltpu.SemaphoreType.DMA((4,)),
         ],
         compiler_params=pltpu.CompilerParams(vmem_limit_bytes=52 * 1024 * 1024),
         cost_estimate=pl.CostEstimate(flops=4_900_000_000, bytes_accessed=18_000_000, transcendentals=400_000),

time: 113 us -> 114 us (level)
  no operation moved by 1% of the time
where the time goes in v6:
time: 114 us; the launch traced here: 111 us
  starting transfers between devices  62.5 us (55%)
  Pallas kernels  28.7 us (25%)
  waiting for transfers between devices  9.48 us (8%)
  local copies, waits for them, and re-layouts  6.48 us (6%)
  other arithmetic  3.66 us (3%)
    ppermute x19, starting transfers between devices, send(): return lax.ppermute(array, BOTH, device_perm(move))  40.5 us
    pallas_call x1, Pallas kernels, conv_in(): pl.pallas_call(conv_in_kernel, out_shape=[jax.ShapeDtypeStruct((4, 4, 32,...  12.2 us
    all_to_all x2, starting transfers between devices, to_zones(): lax.all_to_all(pieces, 'chan', split_axis=0, concat_axis=0, axis_index_gr...  11.1 us
    all_to_all x1, starting transfers between devices, body(): lax.all_to_all(stats, BOTH, split_axis=0, concat_axis=0, tiled=True)  10.9 us
    pallas_call x1, Pallas kernels, conv_out(): pl.pallas_call(conv_out_kernel, out_shape=jax.ShapeDtypeStruct((30, 2, 4,...  10.2 us
    ppermute x19, waiting for transfers between devices, send(): return lax.ppermute(array, BOTH, device_perm(move))  9.47 us
    pallas_call x1, Pallas kernels, conv_rim(): pl.pallas_call(rim_kernel, out_shape=jax.ShapeDtypeStruct((2, 2, 2, 4, 32...  6.28 us
  transfers between devices with their start and end apart: 22, of which 8 were waited for; matrix products, arithmetic and copies ran while one was open for 6% of the time, Pallas kernels for 6%

profile of v6, /device:TPU:2, one launch (start us, length us, event | category | flops | bytes accessed | tf_op | source)
XLA Modules:
  0.0 111.4 jit_solution(13238688367811754490)
XLA Ops:
  0.0 1.3 %copy.28 = bf16[480,6,4,32]{0,3,1,2:T(8,128)(2,1)S(1)} copy(bf16[480,6,4,32]{0,3,2,1:T(8,128)(2,1)} %param.8) | data formatting | bytes 1474560 | tf_op args[0]
  1.3 0.3 fusion
  1.6 1.0 pad_maximum_fusion
  2.6 5.3 %all-to-all-start = ((bf16[4,4,6,32,128]{4,3,2,1,0:T(8,128)(2,1)}), bf16[4,4,6,32,128]{4,3,2,1,0:T(8,128)(2,1)}, u32[]{:S(2)}, u32[]{:S(2)}) async-start(bf16[4,4,6,32,128]{4,3,2,1,0:T(8,128)(2,1)} %pad_maximum_fusion), calls=%async_computation | async-start | bytes 1572864 | tf_op jit(solution)/shard_map/all_to_all | solution.py:306
  7.9 0.1 pad_bitcast_fusion
  8.0 0.3 fusion.9
  8.4 0.2 pad_slice_fusion.1
  8.6 3.5 %collective-permute-start.1 = (bf16[320,512]{1,0:T(8,128)(2,1)S(1)}, bf16[320,512]{1,0:T(8,128)(2,1)S(1)}, u32[]{:S(2)}, u32[]{:S(2)}) collective-permute-start(bf16[320,512]{1,0:T(8,128)(2,1)S(1)} %pad_maximum_fusion.3), channel_id=1, source_target_pairs={{0,1},{1,2},{2,3},{3,4},{4,5},{5,6},{6,7},{8,9},{9,10},{10,11},{11... | collective-permute-start | bytes 983048 | tf_op jit(solution)/shard_map/ppermute | solution.py:26
  12.2 4.5 %collective-permute-start.2 = (bf16[320,512]{1,0:T(8,128)(2,1)S(1)}, bf16[320,512]{1,0:T(8,128)(2,1)S(1)}, u32[]{:S(2)}, u32[]{:S(2)}) collective-permute-start(bf16[320,512]{1,0:T(8,128)(2,1)S(1)} %pad_maximum_fusion.4), channel_id=1, source_target_pairs={{1,0},{2,1},{3,2},{4,3},{5,4},{6,5},{7,6},{9,8},{10,9},{11,10},{12... | collective-permute-start | bytes 983048 | tf_op jit(solution)/shard_map/ppermute | solution.py:26
  16.7 1.0 constant_dynamic-slice_fusion
  17.7 3.6 %collective-permute-start.8 = (bf16[9,3,32,256]{3,2,1,0:T(8,128)(2,1)S(1)}, bf16[9,3,32,256]{3,2,1,0:T(8,128)(2,1)}, u32[]{:S(2)}, u32[]{:S(2)}) collective-permute-start(bf16[9,3,32,256]{3,2,1,0:T(8,128)(2,1)S(1)} %constant_dynamic-slice_fusion), channel_id=1, source_target_pairs={{0,64},{1,65},{2,66},{3,67},{4,68},{5,69},{6,70},{7,71},{8,72},{9,... | collective-permute-start | bytes 1327112 | tf_op jit(solution)/shard_map/ppermute | solution.py:26
  21.3 2.1 %collective-permute-start = (bf16[4,4,6,32,128]{4,3,2,1,0:T(8,128)(2,1)}, bf16[4,4,6,32,128]{4,3,2,1,0:T(8,128)(2,1)}, u32[]{:S(2)}, u32[]{:S(2)}) collective-permute-start(bf16[4,4,6,32,128]{4,3,2,1,0:T(8,128)(2,1)} %all-to-all-done.own), channel_id=1, source_target_pairs={{0,16},{1,17},{2,18},{3,19},{4,20},{5,21},{6,22},{7,23},{8,24},{9,... | collective-permute-start | bytes 2359304 | tf_op jit(solution)/shard_map/ppermute | solution.py:26
  23.4 0.0 collective-permute-done.1
  23.5 0.3 collective-permute-done.2
  23.8 0.2 fusion.5
  24.0 0.8 pad_maximum_fusion.2
  24.8 5.8 %all-to-all-start.1 = ((bf16[4,2,6,32,128]{4,3,2,1,0:T(8,128)(2,1)}), bf16[4,2,6,32,128]{4,3,2,1,0:T(8,128)(2,1)S(1)}, u32[]{:S(2)}, u32[]{:S(2)}) async-start(bf16[4,2,6,32,128]{4,3,2,1,0:T(8,128)(2,1)} %pad_maximum_fusion.2), calls=%async_computation.1 | async-start | bytes 786432 | tf_op jit(solution)/shard_map/all_to_all | solution.py:306
  30.6 2.1 %collective-permute-start.6 = (bf16[9,3,32,512]{3,2,1,0:T(8,128)(2,1)}, bf16[9,3,32,512]{3,2,1,0:T(8,128)(2,1)}, u32[]{:S(2)}, u32[]{:S(2)}) collective-permute-start(bf16[9,3,32,512]{3,2,1,0:T(8,128)(2,1)} %bitcast.80), channel_id=1, source_target_pairs={{0,32},{1,33},{2,34},{3,35},{4,36},{5,37},{6,38},{7,39},{8,40},{9,... | collective-permute-start | bytes 2654216 | tf_op jit(solution)/shard_map/ppermute | solution.py:26
  32.7 1.3 %collective-permute-start.7 = (bf16[9,3,32,512]{3,2,1,0:T(8,128)(2,1)}, bf16[9,3,32,512]{3,2,1,0:T(8,128)(2,1)}, u32[]{:S(2)}, u32[]{:S(2)}) collective-permute-start(bf16[9,3,32,512]{3,2,1,0:T(8,128)(2,1)} %bitcast.81), channel_id=1, source_target_pairs={{0,96},{1,97},{2,98},{3,99},{4,100},{5,101},{6,102},{7,103},{8,104... | collective-permute-start | bytes 2654216 | tf_op jit(solution)/shard_map/ppermute | solution.py:26
  34.0 1.3 %collective-permute-start.3 = (bf16[2,10,512]{2,1,0:T(8,128)(2,1)S(1)}, bf16[2,10,512]{2,1,0:T(8,128)(2,1)S(1)}, u32[]{:S(2)}, u32[]{:S(2)}) collective-permute-start(bf16[2,10,512]{2,1,0:T(8,128)(2,1)S(1)} %pad_maximum_fusion.6), channel_id=1, source_target_pairs={{0,8},{1,9},{2,10},{3,11},{4,12},{5,13},{6,14},{7,15},{8,16},{9,17... | collective-permute-start | bytes 61448 | tf_op jit(solution)/shard_map/ppermute | solution.py:26
  35.4 0.8 collective-permute-done.3.before
  36.2 1.3 %collective-permute-start.4 = (bf16[2,10,512]{2,1,0:T(8,128)(2,1)S(1)}, bf16[2,10,512]{2,1,0:T(8,128)(2,1)S(1)}, u32[]{:S(2)}, u32[]{:S(2)}) collective-permute-start(bf16[2,10,512]{2,1,0:T(8,128)(2,1)S(1)} %pad_maximum_fusion.7), channel_id=1, source_target_pairs={{8,0},{9,1},{10,2},{11,3},{12,4},{13,5},{14,6},{15,7},{16,8},{17,9... | collective-permute-start | bytes 61448 | tf_op jit(solution)/shard_map/ppermute | solution.py:26
  37.5 0.6 copy.22.rim
  38.0 0.0 collective-permute-done.8.near
  38.1 0.1 collective-permute-start.9
  38.1 3.9 %collective-permute-done.4.after = bf16[2,10,512]{2,1,0:T(8,128)(2,1)S(1)} collective-permute-done((bf16[2,10,512]{2,1,0:T(8,128)(2,1)S(1)}, bf16[2,10,512]{2,1,0:T(8,128)(2,1)S(1)}, u32[]{:S(2)}, u32[]{:S(2)}) %collective-permute-start.4) | collective-permute-done | bytes 20512 | tf_op jit(solution)/shard_map/ppermute | solution.py:26
  42.0 0.0 all-to-all-done.1.own_edge
  42.0 4.8 %collective-permute-start.5 = (bf16[4,2,6,32,128]{4,3,2,1,0:T(8,128)(2,1)S(1)}, bf16[4,2,6,32,128]{4,3,2,1,0:T(8,128)(2,1)S(1)}, u32[]{:S(2)}, u32[]{:S(2)}) collective-permute-start(bf16[4,2,6,32,128]{4,3,2,1,0:T(8,128)(2,1)S(1)} %all-to-all-done.1.own_edge), channel_id=1, source_target_pairs={{0,16},{1,17},{2,18},{3,19},{4,20},{5,21},{6,22},{7,23},{8,24},{9,... | collective-permute-start | bytes 1179656 | tf_op jit(solution)/shard_map/ppermute | solution.py:26
  46.8 6.3 %conv_rim.1.rim = f32[2,2,2,4,32,256]{5,4,3,2,1,0:T(8,128)S(1)} custom-call(bf16[2,8,64,512]{3,2,1,0:T(8,128)(2,1)S(1)} %copy.22.rim, bf16[2,64,512]{2,1,0:T(8,128)(2,1)S(1)} %bitcast.66, bf16[2,64,512]{2,1,0:T(8,128)(2,1)S(1)} %bitcast.68, bf16[2,10,512]{2,1,0:T(8,128)(2,1)S(1)} %collective-permute-done.3.before, ...), custom_call_target="tpu_custom_call" | custom-call | flops 7200000000 | bytes 8000000 | tf_op jit(solution)/shard_map/conv_rim/pallas_call | solution.py:188
  53.1 2.8 %collective-permute-start.10 = (bf16[4,4,6,32,128]{4,3,2,1,0:T(8,128)(2,1)}, bf16[4,4,6,32,128]{4,3,2,1,0:T(8,128)(2,1)S(1)}, u32[]{:S(2)}, u32[]{:S(2)}) collective-permute-start(bf16[4,4,6,32,128]{4,3,2,1,0:T(8,128)(2,1)} %all-to-all-done.own), channel_id=1, source_target_pairs={{0,8},{1,9},{2,10},{3,11},{4,12},{5,13},{6,14},{7,15},{8,0},{9,1},... | collective-permute-start | bytes 2359304 | tf_op jit(solution)/shard_map/ppermute | solution.py:26
  55.9 0.0 collective-permute-done.5.other_edge
  56.0 0.7 collective-permute-start.11
  56.7 0.1 collective-permute-start.12
  56.8 0.4 collective-permute-start.13
  57.2 0.1 reshape.70
  57.3 0.1 broadcast_in_dim.13
  57.4 0.6 pad_add_fusion.place
  58.0 1.9 %collective-permute-done.12.own_edge_swap = bf16[4,2,6,32,128]{4,3,2,1,0:T(8,128)(2,1)S(1)} collective-permute-done((bf16[4,2,6,32,128]{4,3,2,1,0:T(8,128)(2,1)S(1)}, bf16[4,2,6,32,128]{4,3,2,1,0:T(8,128)(2,1)S(1)}, u32[]{:S(2)}, u32[]{:S(2)}) %collective-permute-start.12) | collective-permute-done | bytes 393248 | tf_op jit(solution)/shard_map/ppermute | solution.py:26
  60.0 0.3 collective-permute-done.13.other_edge_swap
  60.2 0.2 collective-permute-done.11.other_swap
  60.4 0.7 copy-done.6
  61.1 0.7 broadcast_in_dim.14.bias
  61.8 0.0 copy-start
  61.8 12.2 %conv_in.1 = (bf16[4,4,32,128]{3,2,1,0:T(8,128)(2,1)}, bf16[4,4,32,128]{3,2,1,0:T(8,128)(2,1)}, bf16[4,4,32,128]{3,2,1,0:T(8,128)(2,1)}, bf16[4,4,32,128]{3,2,1,0:T(8,128)(2,1)}, f32[128,128]{1,0:T(8,128)}) custom-call(s32[4]{0:T(128)} %pad_add_fusion.place, bf16[4,4,6,32,128]{4,3,2,1,0:T(8,128)(2,1)} %all-to-all-done.own, ...), custom_call_target="tpu_custom_call" | custom-call | flops 7200000000 | bytes 9000000 | tf_op jit(solution)/shard_map/conv_in/pallas_call | solution.py:121
  74.1 0.4 collective-permute-start.14
  74.5 2.9 %collective-permute-start.16 = (bf16[4,4,32,128]{3,2,1,0:T(8,128)(2,1)}, bf16[4,4,32,128]{3,2,1,0:T(8,128)(2,1)S(1)}, u32[]{:S(2)}, u32[]{:S(2)}) collective-permute-start(bf16[4,4,32,128]{3,2,1,0:T(8,128)(2,1)} %get-tuple-element.42), channel_id=1, source_target_pairs={{0,24},{1,25},{2,26},{3,27},{4,28},{5,29},{6,30},{7,31},{8,16},{9,... | collective-permute-start | bytes 393224 | tf_op jit(solution)/shard_map/ppermute | solution.py:26
  77.4 0.4 collective-permute-start.15
  77.8 0.1 reshape.74
  77.9 0.1 reshape.75
  78.0 0.1 reshape.76
  78.1 0.1 stack_reshape.15
  78.2 0.1 stack.109.place
  78.3 10.9 %all-to-all-start.2 = ((f32[128,1,128]{2,1,0:T(1,128)}), f32[128,1,128]{2,1,0:T(1,128)S(1)}, u32[]{:S(2)}, u32[]{:S(2)}) async-start(f32[128,1,128]{2,1,0:T(1,128)} %bitcast.87), calls=%async_computation.2 | async-start | bytes 131072 | tf_op jit(solution)/shard_map/all_to_all | solution.py:344
  89.2 1.0 pad_maximum_fusion.1
  90.3 3.4 %collective-permute-start.17 = (bf16[4,4,32,128]{3,2,1,0:T(8,128)(2,1)S(1)}, bf16[4,4,32,128]{3,2,1,0:T(8,128)(2,1)S(1)}, u32[]{:S(2)}, u32[]{:S(2)}) collective-permute-start(bf16[4,4,32,128]{3,2,1,0:T(8,128)(2,1)S(1)} %get-tuple-element.56), channel_id=1, source_target_pairs={{0,1},{1,2},{2,3},{3,4},{4,5},{5,6},{6,7},{8,9},{9,10},{10,11},{11... | collective-permute-start | bytes 393224 | tf_op jit(solution)/shard_map/ppermute | solution.py:26
  93.6 4.8 %collective-permute-start.18 = (bf16[4,4,32,128]{3,2,1,0:T(8,128)(2,1)S(1)}, bf16[4,4,32,128]{3,2,1,0:T(8,128)(2,1)S(1)}, u32[]{:S(2)}, u32[]{:S(2)}) collective-permute-start(bf16[4,4,32,128]{3,2,1,0:T(8,128)(2,1)S(1)} %get-tuple-element.55), channel_id=1, source_target_pairs={{1,0},{2,1},{3,2},{4,3},{5,4},{6,5},{7,6},{9,8},{10,9},{11,10},{12... | collective-permute-start | bytes 393224 | tf_op jit(solution)/shard_map/ppermute | solution.py:26
  98.5 0.1 reshape.72
  98.6 0.1 broadcast_in_dim.15
  98.6 0.1 stack_reshape.14
  98.7 0.1 broadcast_in_dim.16
  98.8 0.1 reshape.73
  99.0 0.8 collective-permute-done.17.up
  99.8 1.2 %collective-permute-done.18.down = bf16[4,4,32,128]{3,2,1,0:T(8,128)(2,1)S(1)} collective-permute-done((bf16[4,4,32,128]{3,2,1,0:T(8,128)(2,1)S(1)}, bf16[4,4,32,128]{3,2,1,0:T(8,128)(2,1)S(1)}, u32[]{:S(2)}, u32[]{:S(2)}) %collective-permute-start.18) | collective-permute-done | bytes 131104 | tf_op jit(solution)/shard_map/ppermute | solution.py:26
  101.0 10.2 %conv_out.1 = bf16[30,2,4,8,256]{4,3,2,1,0:T(8,128)(2,1)} custom-call(s32[5]{0:T(128)S(1)} %stack.109.place, bf16[4,4,4,32,128]{4,3,2,1,0:T(8,128)(2,1)S(1)} %copy.26.main, bf16[4,4,32,128]{3,2,1,0:T(8,128)(2,1)S(1)} %collective-permute-done.17.up, bf16[4,4,32,128]{3,2,1,0:T(8,128)(2,1)S(1)} %collective-permute-done.18.down, ...), custom_call_target="tpu_custom_call" | custom-call | flops 4899999744 | bytes 18000000 | tf_op jit(solution)/shard_map/conv_out/pallas_call | solution.py:263
  (50 shorter events, 0.5 us)
Async XLA Ops:
  0.0 7.9 %copy-start.1 = (bf16[60,2,8,512]{3,2,1,0:T(8,128)(2,1)S(1)}, bf16[60,2,8,512]{3,2,1,0:T(8,128)(2,1)}, u32[]{:S(2)}) copy-start(bf16[60,2,8,512]{3,2,1,0:T(8,128)(2,1)} %param.13) | copy-start | bytes 2949124
  2.6 18.7 %all-to-all-start = ((bf16[4,4,6,32,128]{4,3,2,1,0:T(8,128)(2,1)}), bf16[4,4,6,32,128]{4,3,2,1,0:T(8,128)(2,1)}, u32[]{:S(2)}, u32[]{:S(2)}) async-start(bf16[4,4,6,32,128]{4,3,2,1,0:T(8,128)(2,1)} %pad_maximum_fusion), calls=%async_computation | async-start | bytes 1572864 | tf_op jit(solution)/shard_map/all_to_all | solution.py:306
  8.6 14.9 %collective-permute-start.1 = (bf16[320,512]{1,0:T(8,128)(2,1)S(1)}, bf16[320,512]{1,0:T(8,128)(2,1)S(1)}, u32[]{:S(2)}, u32[]{:S(2)}) collective-permute-start(bf16[320,512]{1,0:T(8,128)(2,1)S(1)} %pad_maximum_fusion.3), channel_id=1, source_target_pairs={{0,1},{1,2},{2,3},{3,4},{4,5},{5,6},{6,7},{8,9},{9,10},{10,11},{11... | collective-permute-start | bytes 983048 | tf_op jit(solution)/shard_map/ppermute | solution.py:26
  12.2 11.6 %collective-permute-start.2 = (bf16[320,512]{1,0:T(8,128)(2,1)S(1)}, bf16[320,512]{1,0:T(8,128)(2,1)S(1)}, u32[]{:S(2)}, u32[]{:S(2)}) collective-permute-start(bf16[320,512]{1,0:T(8,128)(2,1)S(1)} %pad_maximum_fusion.4), channel_id=1, source_target_pairs={{1,0},{2,1},{3,2},{4,3},{5,4},{6,5},{7,6},{9,8},{10,9},{11,10},{12... | collective-permute-start | bytes 983048 | tf_op jit(solution)/shard_map/ppermute | solution.py:26
  17.7 20.3 %collective-permute-start.8 = (bf16[9,3,32,256]{3,2,1,0:T(8,128)(2,1)S(1)}, bf16[9,3,32,256]{3,2,1,0:T(8,128)(2,1)}, u32[]{:S(2)}, u32[]{:S(2)}) collective-permute-start(bf16[9,3,32,256]{3,2,1,0:T(8,128)(2,1)S(1)} %constant_dynamic-slice_fusion), channel_id=1, source_target_pairs={{0,64},{1,65},{2,66},{3,67},{4,68},{5,69},{6,70},{7,71},{8,72},{9,... | collective-permute-start | bytes 1327112 | tf_op jit(solution)/shard_map/ppermute | solution.py:26
  21.3 25.5 %collective-permute-start = (bf16[4,4,6,32,128]{4,3,2,1,0:T(8,128)(2,1)}, bf16[4,4,6,32,128]{4,3,2,1,0:T(8,128)(2,1)}, u32[]{:S(2)}, u32[]{:S(2)}) collective-permute-start(bf16[4,4,6,32,128]{4,3,2,1,0:T(8,128)(2,1)} %all-to-all-done.own), channel_id=1, source_target_pairs={{0,16},{1,17},{2,18},{3,19},{4,20},{5,21},{6,22},{7,23},{8,24},{9,... | collective-permute-start | bytes 2359304 | tf_op jit(solution)/shard_map/ppermute | solution.py:26
  24.8 17.3 %all-to-all-start.1 = ((bf16[4,2,6,32,128]{4,3,2,1,0:T(8,128)(2,1)}), bf16[4,2,6,32,128]{4,3,2,1,0:T(8,128)(2,1)S(1)}, u32[]{:S(2)}, u32[]{:S(2)}) async-start(bf16[4,2,6,32,128]{4,3,2,1,0:T(8,128)(2,1)} %pad_maximum_fusion.2), calls=%async_computation.1 | async-start | bytes 786432 | tf_op jit(solution)/shard_map/all_to_all | solution.py:306
  30.6 25.3 %collective-permute-start.6 = (bf16[9,3,32,512]{3,2,1,0:T(8,128)(2,1)}, bf16[9,3,32,512]{3,2,1,0:T(8,128)(2,1)}, u32[]{:S(2)}, u32[]{:S(2)}) collective-permute-start(bf16[9,3,32,512]{3,2,1,0:T(8,128)(2,1)} %bitcast.80), channel_id=1, source_target_pairs={{0,32},{1,33},{2,34},{3,35},{4,36},{5,37},{6,38},{7,39},{8,40},{9,... | collective-permute-start | bytes 2654216 | tf_op jit(solution)/shard_map/ppermute | solution.py:26
  32.7 23.2 %collective-permute-start.7 = (bf16[9,3,32,512]{3,2,1,0:T(8,128)(2,1)}, bf16[9,3,32,512]{3,2,1,0:T(8,128)(2,1)}, u32[]{:S(2)}, u32[]{:S(2)}) collective-permute-start(bf16[9,3,32,512]{3,2,1,0:T(8,128)(2,1)} %bitcast.81), channel_id=1, source_target_pairs={{0,96},{1,97},{2,98},{3,99},{4,100},{5,101},{6,102},{7,103},{8,104... | collective-permute-start | bytes 2654216 | tf_op jit(solution)/shard_map/ppermute | solution.py:26
  34.0 2.1 %collective-permute-start.3 = (bf16[2,10,512]{2,1,0:T(8,128)(2,1)S(1)}, bf16[2,10,512]{2,1,0:T(8,128)(2,1)S(1)}, u32[]{:S(2)}, u32[]{:S(2)}) collective-permute-start(bf16[2,10,512]{2,1,0:T(8,128)(2,1)S(1)} %pad_maximum_fusion.6), channel_id=1, source_target_pairs={{0,8},{1,9},{2,10},{3,11},{4,12},{5,13},{6,14},{7,15},{8,16},{9,17... | collective-permute-start | bytes 61448 | tf_op jit(solution)/shard_map/ppermute | solution.py:26
  36.2 5.9 %collective-permute-start.4 = (bf16[2,10,512]{2,1,0:T(8,128)(2,1)S(1)}, bf16[2,10,512]{2,1,0:T(8,128)(2,1)S(1)}, u32[]{:S(2)}, u32[]{:S(2)}) collective-permute-start(bf16[2,10,512]{2,1,0:T(8,128)(2,1)S(1)} %pad_maximum_fusion.7), channel_id=1, source_target_pairs={{8,0},{9,1},{10,2},{11,3},{12,4},{13,5},{14,6},{15,7},{16,8},{17,9... | collective-permute-start | bytes 61448 | tf_op jit(solution)/shard_map/ppermute | solution.py:26
  38.1 17.9 %collective-permute-start.9 = (bf16[9,3,32,256]{3,2,1,0:T(8,128)(2,1)}, bf16[9,3,32,256]{3,2,1,0:T(8,128)(2,1)}, u32[]{:S(2)}, u32[]{:S(2)}) collective-permute-start(bf16[9,3,32,256]{3,2,1,0:T(8,128)(2,1)} %collective-permute-done.8.near), channel_id=1, source_target_pairs={{0,1},{1,0},{2,3},{3,2},{4,5},{5,4},{6,7},{7,6},{8,9},{9,8},{10,11... | collective-permute-start | bytes 1327112 | tf_op jit(solution)/shard_map/ppermute | solution.py:26
  42.0 14.7 %copy-start.2 = (bf16[4,2,6,32,128]{4,3,2,1,0:T(8,128)(2,1)}, bf16[4,2,6,32,128]{4,3,2,1,0:T(8,128)(2,1)S(1)}, u32[]{:S(2)}) copy-start(bf16[4,2,6,32,128]{4,3,2,1,0:T(8,128)(2,1)S(1)} %all-to-all-done.1.own_edge) | copy-start | bytes 1179652
  42.0 13.9 %collective-permute-start.5 = (bf16[4,2,6,32,128]{4,3,2,1,0:T(8,128)(2,1)S(1)}, bf16[4,2,6,32,128]{4,3,2,1,0:T(8,128)(2,1)S(1)}, u32[]{:S(2)}, u32[]{:S(2)}) collective-permute-start(bf16[4,2,6,32,128]{4,3,2,1,0:T(8,128)(2,1)S(1)} %all-to-all-done.1.own_edge), channel_id=1, source_target_pairs={{0,16},{1,17},{2,18},{3,19},{4,20},{5,21},{6,22},{7,23},{8,24},{9,... | collective-permute-start | bytes 1179656 | tf_op jit(solution)/shard_map/ppermute | solution.py:26
  46.8 10.4 %copy-start.3 = (f32[512]{0:T(512)S(1)}, f32[512]{0:T(512)}, u32[]{:S(2)}) copy-start(f32[512]{0:T(512)} %param.10) | copy-start | bytes 6148
  53.1 7.1 %collective-permute-start.10 = (bf16[4,4,6,32,128]{4,3,2,1,0:T(8,128)(2,1)}, bf16[4,4,6,32,128]{4,3,2,1,0:T(8,128)(2,1)S(1)}, u32[]{:S(2)}, u32[]{:S(2)}) collective-permute-start(bf16[4,4,6,32,128]{4,3,2,1,0:T(8,128)(2,1)} %all-to-all-done.own), channel_id=1, source_target_pairs={{0,8},{1,9},{2,10},{3,11},{4,12},{5,13},{6,14},{7,15},{8,0},{9,1},... | collective-permute-start | bytes 2359304 | tf_op jit(solution)/shard_map/ppermute | solution.py:26
  55.9 5.9 %copy-start.7 = (bf16[4,2,6,32,128]{4,3,2,1,0:T(8,128)(2,1)}, bf16[4,2,6,32,128]{4,3,2,1,0:T(8,128)(2,1)S(1)}, u32[]{:S(2)}) copy-start(bf16[4,2,6,32,128]{4,3,2,1,0:T(8,128)(2,1)S(1)} %collective-permute-done.5.other_edge) | copy-start | bytes 1179652
  56.0 4.5 %collective-permute-start.11 = (bf16[4,4,6,32,128]{4,3,2,1,0:T(8,128)(2,1)}, bf16[4,4,6,32,128]{4,3,2,1,0:T(8,128)(2,1)}, u32[]{:S(2)}, u32[]{:S(2)}) collective-permute-start(bf16[4,4,6,32,128]{4,3,2,1,0:T(8,128)(2,1)} %collective-permute-done.other), channel_id=1, source_target_pairs={{0,8},{1,9},{2,10},{3,11},{4,12},{5,13},{6,14},{7,15},{8,0},{9,1},... | collective-permute-start | bytes 2359304 | tf_op jit(solution)/shard_map/ppermute | solution.py:26
  56.7 3.3 %collective-permute-start.12 = (bf16[4,2,6,32,128]{4,3,2,1,0:T(8,128)(2,1)S(1)}, bf16[4,2,6,32,128]{4,3,2,1,0:T(8,128)(2,1)S(1)}, u32[]{:S(2)}, u32[]{:S(2)}) collective-permute-start(bf16[4,2,6,32,128]{4,3,2,1,0:T(8,128)(2,1)S(1)} %all-to-all-done.1.own_edge), channel_id=1, source_target_pairs={{0,8},{1,9},{2,10},{3,11},{4,12},{5,13},{6,14},{7,15},{8,0},{9,1},... | collective-permute-start | bytes 1179656 | tf_op jit(solution)/shard_map/ppermute | solution.py:26
  56.8 3.4 %collective-permute-start.13 = (bf16[4,2,6,32,128]{4,3,2,1,0:T(8,128)(2,1)S(1)}, bf16[4,2,6,32,128]{4,3,2,1,0:T(8,128)(2,1)}, u32[]{:S(2)}, u32[]{:S(2)}) collective-permute-start(bf16[4,2,6,32,128]{4,3,2,1,0:T(8,128)(2,1)S(1)} %collective-permute-done.5.other_edge), channel_id=1, source_target_pairs={{0,8},{1,9},{2,10},{3,11},{4,12},{5,13},{6,14},{7,15},{8,0},{9,1},... | collective-permute-start | bytes 1179656 | tf_op jit(solution)/shard_map/ppermute | solution.py:26
  60.0 1.8 %copy-start.8 = (bf16[4,2,6,32,128]{4,3,2,1,0:T(8,128)(2,1)}, bf16[4,2,6,32,128]{4,3,2,1,0:T(8,128)(2,1)S(1)}, u32[]{:S(2)}) copy-start(bf16[4,2,6,32,128]{4,3,2,1,0:T(8,128)(2,1)S(1)} %collective-permute-done.12.own_edge_swap) | copy-start | bytes 1179652
  60.2 0.9 copy-start.6
  61.8 16.0 %copy-start.4 = (f32[512]{0:T(512)S(1)}, f32[512]{0:T(512)}, u32[]{:S(2)}) copy-start(f32[512]{0:T(512)} %param.11) | copy-start | bytes 6148
  61.8 16.2 %copy-start.5 = (f32[512]{0:T(512)S(1)}, f32[512]{0:T(512)}, u32[]{:S(2)}) copy-start(f32[512]{0:T(512)} %param.12) | copy-start | bytes 6148
  61.8 39.2 %copy-start = (f32[256]{0:T(256)S(1)}, f32[256]{0:T(256)}, u32[]{:S(2)}) copy-start(f32[256]{0:T(256)} %param.15) | copy-start | bytes 3076
  74.1 4.2 %collective-permute-start.14 = (bf16[4,4,32,128]{3,2,1,0:T(8,128)(2,1)}, bf16[4,4,32,128]{3,2,1,0:T(8,128)(2,1)S(1)}, u32[]{:S(2)}, u32[]{:S(2)}) collective-permute-start(bf16[4,4,32,128]{3,2,1,0:T(8,128)(2,1)} %get-tuple-element.39), channel_id=1, source_target_pairs={{0,8},{1,9},{2,10},{3,11},{4,12},{5,13},{6,14},{7,15},{8,0},{9,1},... | collective-permute-start | bytes 393224 | tf_op jit(solution)/shard_map/ppermute | solution.py:26
  74.5 14.7 %collective-permute-start.16 = (bf16[4,4,32,128]{3,2,1,0:T(8,128)(2,1)}, bf16[4,4,32,128]{3,2,1,0:T(8,128)(2,1)S(1)}, u32[]{:S(2)}, u32[]{:S(2)}) collective-permute-start(bf16[4,4,32,128]{3,2,1,0:T(8,128)(2,1)} %get-tuple-element.42), channel_id=1, source_target_pairs={{0,24},{1,25},{2,26},{3,27},{4,28},{5,29},{6,30},{7,31},{8,16},{9,... | collective-permute-start | bytes 393224 | tf_op jit(solution)/shard_map/ppermute | solution.py:26
  77.4 11.8 %collective-permute-start.15 = (bf16[4,4,32,128]{3,2,1,0:T(8,128)(2,1)}, bf16[4,4,32,128]{3,2,1,0:T(8,128)(2,1)S(1)}, u32[]{:S(2)}, u32[]{:S(2)}) collective-permute-start(bf16[4,4,32,128]{3,2,1,0:T(8,128)(2,1)} %get-tuple-element.41), channel_id=1, source_target_pairs={{0,16},{1,17},{2,18},{3,19},{4,20},{5,21},{6,22},{7,23},{8,24},{9,... | collective-permute-start | bytes 393224 | tf_op jit(solution)/shard_map/ppermute | solution.py:26
  78.3 20.2 %all-to-all-start.2 = ((f32[128,1,128]{2,1,0:T(1,128)}), f32[128,1,128]{2,1,0:T(1,128)S(1)}, u32[]{:S(2)}, u32[]{:S(2)}) async-start(f32[128,1,128]{2,1,0:T(1,128)} %bitcast.87), calls=%async_computation.2 | async-start | bytes 131072 | tf_op jit(solution)/shard_map/all_to_all | solution.py:344
  90.3 9.6 %collective-permute-start.17 = (bf16[4,4,32,128]{3,2,1,0:T(8,128)(2,1)S(1)}, bf16[4,4,32,128]{3,2,1,0:T(8,128)(2,1)S(1)}, u32[]{:S(2)}, u32[]{:S(2)}) collective-permute-start(bf16[4,4,32,128]{3,2,1,0:T(8,128)(2,1)S(1)} %get-tuple-element.56), channel_id=1, source_target_pairs={{0,1},{1,2},{2,3},{3,4},{4,5},{5,6},{6,7},{8,9},{9,10},{10,11},{11... | collective-permute-start | bytes 393224 | tf_op jit(solution)/shard_map/ppermute | solution.py:26
  93.6 7.4 %collective-permute-start.18 = (bf16[4,4,32,128]{3,2,1,0:T(8,128)(2,1)S(1)}, bf16[4,4,32,128]{3,2,1,0:T(8,128)(2,1)S(1)}, u32[]{:S(2)}, u32[]{:S(2)}) collective-permute-start(bf16[4,4,32,128]{3,2,1,0:T(8,128)(2,1)S(1)} %get-tuple-element.55), channel_id=1, source_target_pairs={{1,0},{2,1},{3,2},{4,3},{5,4},{6,5},{7,6},{9,8},{10,9},{11,10},{12... | collective-permute-start | bytes 393224 | tf_op jit(solution)/shard_map/ppermute | solution.py:26
